TPU v7x, 32 devices: a whole 2x2x4 slice. The times are simulated.
32 devices in a mesh: fsdp: 8 (over z, y), tp: 4 (over x, core).
Axes of the slice: x: 2, y: 2, z: 4, core: 2. Of those that a mesh axis runs over, the one named last changes fastest.
Arguments:
- tokens: bfloat16 [16384, 768], P(('fsdp', 'tp')), may hold values from -6 to 6
- cotangent: bfloat16 [16384, 768], P(('fsdp', 'tp')), may hold values from -6 to 6
- lengths: int32 [8, 7], P('fsdp'), may hold values from 1 to 512, 2048 in all within a row
- w_query: bfloat16 [2, 768, 768], P(None, 'fsdp', 'tp'), may hold values from -0.21875 to 0.21875
- w_key: bfloat16 [2, 768, 768], P(None, 'fsdp', 'tp'), may hold values from -0.21875 to 0.21875
- w_value: bfloat16 [2, 768, 768], P(None, 'fsdp', 'tp'), may hold values from -0.21875 to 0.21875
- w_out: bfloat16 [2, 768, 768], P(None, 'tp', 'fsdp'), may hold values from -0.625 to 0.625
- w_up: bfloat16 [2, 768, 3072], P(None, 'fsdp', 'tp'), may hold values from -0.21875 to 0.21875
- w_down: bfloat16 [2, 3072, 768], P(None, 'tp', 'fsdp'), may hold values from -0.109375 to 0.109375
- norm_gain: float32 [2, 2, 768], P(None, None, ('fsdp', 'tp')), may hold values from 0.5 to 1.5
- norm_shift: float32 [2, 2, 768], P(None, None, ('fsdp', 'tp')), may hold values from -1.2 to 1.2
- attn_bias: float32 [2, 3, 768], P(None, None, ('fsdp', 'tp')), may hold values from -1.2 to 1.2
- up_bias: float32 [2, 3072], P(None, ('fsdp', 'tp')), may hold values from -1.2 to 1.2
- down_bias: float32 [2, 768], P(None, ('fsdp', 'tp')), may hold values from -1.2 to 1.2
Outputs:
- stream_out: bfloat16 [16384, 768], P(('fsdp', 'tp'))
- grad_tokens: float32 [16384, 768], P(('fsdp', 'tp'))
- grad_query: float32 [2, 768, 768], P(None, 'fsdp', 'tp')
- grad_key: float32 [2, 768, 768], P(None, 'fsdp', 'tp')
- grad_value: float32 [2, 768, 768], P(None, 'fsdp', 'tp')
- grad_out: float32 [2, 768, 768], P(None, 'tp', 'fsdp')
- grad_up: float32 [2, 768, 3072], P(None, 'fsdp', 'tp')
- grad_down: float32 [2, 3072, 768], P(None, 'tp', 'fsdp')
- grad_gain: float32 [2, 2, 768], P(None, None, ('fsdp', 'tp'))
- grad_shift: float32 [2, 2, 768], P(None, None, ('fsdp', 'tp'))
- grad_attn_bias: float32 [2, 3, 768], P(None, None, ('fsdp', 'tp'))
- grad_up_bias: float32 [2, 3072], P(None, ('fsdp', 'tp'))
- grad_down_bias: float32 [2, 768], P(None, ('fsdp', 'tp'))
Inputs may be any that keep to these rules, and one draw needn't show every extreme that they name: Each row lists the lengths of the 7 sequences packed in order into one group of 2048 rows; a row sums to 2048 and its largest length is exactly 512.
All inputs are finite; a program needn't handle non-finite values.
Results may differ from a plain program's by a relative error of at most 0.025.
Values may be sent and summed in bfloat16 or wider, within the bound.
No kernel may reach another device: no remote copies, remote signals or barrier semaphores. Data moves between devices by JAX's collectives and lax.ppermute only.
A program may use at most 256 MiB of HBM per device.

v0:
```python
import jax
import jax.numpy as jnp
from jax import lax
from jax.sharding import PartitionSpec as P

HEAD = 64
MAXLEN = 512


eps = 1e-05
masked_fill = -1e30


def layer_norm(values, gain_row, shift_row):
    row_mean = jnp.mean(values, axis=-1, keepdims=True)
    centred = values - row_mean
    row_var = jnp.mean(centred * centred, axis=-1, keepdims=True)
    return centred * lax.rsqrt(row_var + eps) * gain_row + shift_row


def contract_rows(left, right):
    return lax.dot_general(
        left, right, (((0,), (0,)), ((), ())), preferred_element_type=jnp.float32
    )


def contract_cols(left, right):
    return lax.dot_general(
        left, right, (((1,), (1,)), ((), ())), preferred_element_type=jnp.float32
    )


def spread_rows(rows):
    return lax.all_gather(rows, "tp", axis=0, tiled=True)


def collect_rows(partial_value):
    return lax.psum_scatter(
        partial_value.astype(jnp.bfloat16), "tp", scatter_dimension=0, tiled=True
    ).astype(jnp.float32)


def spread_grads(rows):
    return lax.all_gather(rows, "tp", axis=0, tiled=True)


def collect_grads(partial_value):
    return lax.psum_scatter(
        partial_value.astype(jnp.bfloat16), "tp", scatter_dimension=0, tiled=True
    ).astype(jnp.float32)


def fetch_layer(layer_index, w_query, w_key, w_value, w_out, w_up, w_down):
    return (
        lax.all_gather(w_query[layer_index], "fsdp", axis=0, tiled=True),
        lax.all_gather(w_key[layer_index], "fsdp", axis=0, tiled=True),
        lax.all_gather(w_value[layer_index], "fsdp", axis=0, tiled=True),
        lax.all_gather(w_out[layer_index], "fsdp", axis=1, tiled=True),
        lax.all_gather(w_up[layer_index], "fsdp", axis=0, tiled=True),
        lax.all_gather(w_down[layer_index], "fsdp", axis=1, tiled=True),
    )


def masked_scores(query_low, key_pad, segments, segment_pad, first_row, block_rows, reach):
    heads_here = query_low.shape[1] // HEAD
    window = reach + block_rows
    query_block = query_low[first_row : first_row + block_rows].reshape(
        block_rows, heads_here, HEAD
    )
    key_window = key_pad[first_row : first_row + window].reshape(window, heads_here, HEAD)
    raw_scores = jnp.einsum(
        "qhd,khd->hqk", query_block, key_window, preferred_element_type=jnp.float32
    )
    query_pos = first_row + jnp.arange(block_rows, dtype=jnp.int32)
    key_pos = first_row - reach + jnp.arange(window, dtype=jnp.int32)
    same_seq = (
        segments[first_row : first_row + block_rows][:, None]
        == segment_pad[first_row : first_row + window][None, :]
    )
    allowed = same_seq & (key_pos[None, :] <= query_pos[:, None])
    return jnp.where(allowed[None], raw_scores * HEAD ** (-0.5), masked_fill)


def attend_forward(query_low, key_low, value_low, segments, reach, block_rows):
    group_rows, head_cols = query_low.shape
    heads_here = head_cols // HEAD
    window = reach + block_rows
    zero_rows = jnp.zeros((reach, head_cols), jnp.bfloat16)
    key_pad = jnp.concatenate([zero_rows, key_low], 0)
    value_pad = jnp.concatenate([zero_rows, value_low], 0)
    segment_pad = jnp.concatenate([jnp.full((reach,), -1, jnp.int32), segments], 0)
    outputs = []
    log_totals = []
    for first_row in range(0, group_rows, block_rows):
        scores = masked_scores(
            query_low, key_pad, segments, segment_pad, first_row, block_rows, reach
        )
        row_max = jnp.max(scores, axis=-1, keepdims=True)
        exp_terms = jnp.exp(scores - row_max)
        row_total = jnp.sum(exp_terms, axis=-1, keepdims=True)
        probs_low = (exp_terms / row_total).astype(jnp.bfloat16)
        value_window = value_pad[first_row : first_row + window].reshape(window, heads_here, HEAD)
        attended = jnp.einsum(
            "hqk,khd->qhd", probs_low, value_window, preferred_element_type=jnp.float32
        )
        outputs.append(attended.reshape(block_rows, head_cols))
        log_totals.append(row_max + jnp.log(row_total))
    return (jnp.concatenate(outputs, 0), log_totals, (key_pad, value_pad, segment_pad))


def attend_backward(query_low, padded, segments, log_totals, grad_attended, reach, block_rows):
    key_pad, value_pad, segment_pad = padded
    group_rows, head_cols = query_low.shape
    heads_here = head_cols // HEAD
    window = reach + block_rows
    grad_keys = jnp.zeros((reach + group_rows, heads_here, HEAD), jnp.float32)
    grad_values = jnp.zeros((reach + group_rows, heads_here, HEAD), jnp.float32)
    grad_queries = []
    for block_index, first_row in enumerate(range(0, group_rows, block_rows)):
        scores = masked_scores(
            query_low, key_pad, segments, segment_pad, first_row, block_rows, reach
        )
        probs = jnp.exp(scores - log_totals[block_index])
        probs_low = probs.astype(jnp.bfloat16)
        key_window = key_pad[first_row : first_row + window].reshape(window, heads_here, HEAD)
        value_window = value_pad[first_row : first_row + window].reshape(window, heads_here, HEAD)
        query_block = query_low[first_row : first_row + block_rows].reshape(
            block_rows, heads_here, HEAD
        )
        grad_block = grad_attended[first_row : first_row + block_rows].reshape(
            block_rows, heads_here, HEAD
        )
        grad_values = grad_values.at[first_row : first_row + window].add(
            jnp.einsum("hqk,qhd->khd", probs_low, grad_block, preferred_element_type=jnp.float32)
        )
        grad_probs = jnp.einsum(
            "qhd,khd->hqk", grad_block, value_window, preferred_element_type=jnp.float32
        )
        inner = jnp.sum(probs * grad_probs, axis=-1, keepdims=True)
        grad_raw = (probs * (grad_probs - inner) * HEAD ** (-0.5)).astype(jnp.bfloat16)
        grad_queries.append(
            jnp.einsum(
                "hqk,khd->qhd", grad_raw, key_window, preferred_element_type=jnp.float32
            ).reshape(block_rows, head_cols)
        )
        grad_keys = grad_keys.at[first_row : first_row + window].add(
            jnp.einsum("hqk,qhd->khd", grad_raw, query_block, preferred_element_type=jnp.float32)
        )
    return (
        jnp.concatenate(grad_queries, 0),
        grad_keys[reach:].reshape(group_rows, head_cols),
        grad_values[reach:].reshape(group_rows, head_cols),
    )


def place_part(part, start_col, full_cols):
    return lax.dynamic_update_slice_in_dim(jnp.zeros((full_cols,), jnp.float32), part, start_col, 0)


def on_device(
    tokens,
    cotangent,
    lengths,
    w_query,
    w_key,
    w_value,
    w_out,
    w_up,
    w_down,
    norm_gain,
    norm_shift,
    attn_bias,
    up_bias,
    down_bias,
):
    tp_count = lax.axis_size("tp")
    tp_index = lax.axis_index("tp")
    tok_rows = tokens.shape[0]
    width = tokens.shape[1]
    group_rows = tok_rows * tp_count
    head_cols = w_query.shape[2]
    hidden_cols = w_up.shape[2]
    layer_count = w_query.shape[0]
    reach = min(MAXLEN, group_rows)
    block_rows = min(512, group_rows)
    gain_all, shift_all, bias_attn, bias_up, bias_down = (
        lax.all_gather(norm_gain, ("fsdp", "tp"), axis=2, tiled=True),
        lax.all_gather(norm_shift, ("fsdp", "tp"), axis=2, tiled=True),
        lax.all_gather(attn_bias, ("fsdp", "tp"), axis=2, tiled=True),
        lax.all_gather(up_bias, ("fsdp", "tp"), axis=1, tiled=True),
        lax.all_gather(down_bias, ("fsdp", "tp"), axis=1, tiled=True),
    )
    hidden_full = bias_up.shape[1]
    head_start = tp_index * head_cols
    hidden_start = tp_index * hidden_cols
    seq_ends = jnp.cumsum(lengths[0])
    row_ids = jnp.arange(group_rows, dtype=jnp.int32)
    segments = jnp.sum((row_ids[:, None] >= seq_ends[None, :]).astype(jnp.int32), axis=1)
    stream = tokens.astype(jnp.float32)
    saved = []
    for layer_index in range(layer_count):
        weights = fetch_layer(layer_index, w_query, w_key, w_value, w_out, w_up, w_down)
        weight_query, weight_key, weight_value, weight_out, weight_up, weight_down = weights
        bias_query = lax.dynamic_slice_in_dim(bias_attn[layer_index, 0], head_start, head_cols)
        bias_value = lax.dynamic_slice_in_dim(bias_attn[layer_index, 1], head_start, head_cols)
        bias_hidden = lax.dynamic_slice_in_dim(bias_up[layer_index], hidden_start, hidden_cols)
        normed_first = spread_rows(
            layer_norm(stream, gain_all[layer_index, 0], shift_all[layer_index, 0]).astype(
                jnp.bfloat16
            )
        )
        query_low = (
            jnp.dot(normed_first, weight_query, preferred_element_type=jnp.float32) + bias_query
        ).astype(jnp.bfloat16)
        key_low = jnp.dot(normed_first, weight_key, preferred_element_type=jnp.float32).astype(
            jnp.bfloat16
        )
        value_low = (
            jnp.dot(normed_first, weight_value, preferred_element_type=jnp.float32) + bias_value
        ).astype(jnp.bfloat16)
        attended, log_totals, padded = attend_forward(
            query_low, key_low, value_low, segments, reach, block_rows
        )
        attended_low = attended.astype(jnp.bfloat16)
        attn_part = collect_rows(
            jnp.dot(attended_low, weight_out, preferred_element_type=jnp.float32)
        )
        stream_mid = stream + attn_part + bias_attn[layer_index, 2]
        normed_second = spread_rows(
            layer_norm(stream_mid, gain_all[layer_index, 1], shift_all[layer_index, 1]).astype(
                jnp.bfloat16
            )
        )
        hidden_pre = (
            jnp.dot(normed_second, weight_up, preferred_element_type=jnp.float32) + bias_hidden
        )
        hidden_low = jax.nn.gelu(hidden_pre).astype(jnp.bfloat16)
        stream_next = (
            stream_mid
            + collect_rows(jnp.dot(hidden_low, weight_down, preferred_element_type=jnp.float32))
            + bias_down[layer_index]
        )
        saved.append(
            (
                stream,
                normed_first,
                query_low,
                padded,
                log_totals,
                attended_low,
                stream_mid,
                normed_second,
                hidden_pre,
                hidden_low,
                weights,
            )
        )
        stream = stream_next
    grad_stream = cotangent.astype(jnp.float32)
    matrix_grads = [None] * layer_count
    gain_grads = [None] * layer_count
    shift_grads = [None] * layer_count
    attn_grads = [None] * layer_count
    up_grads = [None] * layer_count
    down_grads = [None] * layer_count
    for layer_index in reversed(range(layer_count)):
        (
            stream_in,
            normed_first,
            query_low,
            padded,
            log_totals,
            attended_low,
            stream_mid,
            normed_second,
            hidden_pre,
            hidden_low,
            kept_weights,
        ) = saved[layer_index]
        weights = fetch_layer(layer_index, w_query, w_key, w_value, w_out, w_up, w_down)
        weight_query, weight_key, weight_value, weight_out, weight_up, weight_down = weights
        down_grads[layer_index] = jnp.sum(grad_stream, axis=0)
        grad_rows_low = spread_grads(grad_stream.astype(jnp.bfloat16))
        grad_w_down = contract_rows(hidden_low, grad_rows_low)
        grad_hidden = contract_cols(grad_rows_low, weight_down)
        grad_pre_low = jax.vjp(jax.nn.gelu, hidden_pre)[1](grad_hidden)[0].astype(jnp.bfloat16)
        grad_bias_hidden = jnp.sum(grad_pre_low.astype(jnp.float32), axis=0)
        grad_w_up = contract_rows(normed_second, grad_pre_low)
        grad_normed = collect_grads(contract_cols(grad_pre_low, weight_up))
        norm_pull = jax.vjp(
            layer_norm, stream_mid, gain_all[layer_index, 1], shift_all[layer_index, 1]
        )[1]
        grad_from_norm, grad_gain_second, grad_shift_second = norm_pull(grad_normed)
        grad_stream = grad_stream + grad_from_norm
        grad_bias_out = jnp.sum(grad_stream, axis=0)
        grad_rows_low = spread_grads(grad_stream.astype(jnp.bfloat16))
        grad_w_out = contract_rows(attended_low, grad_rows_low)
        grad_attended = contract_cols(grad_rows_low, weight_out).astype(jnp.bfloat16)
        grad_queries, grad_keys, grad_values = attend_backward(
            query_low, padded, segments, log_totals, grad_attended, reach, block_rows
        )
        query_grad_low = grad_queries.astype(jnp.bfloat16)
        key_grad_low = grad_keys.astype(jnp.bfloat16)
        value_grad_low = grad_values.astype(jnp.bfloat16)
        grad_bias_query = jnp.sum(query_grad_low.astype(jnp.float32), axis=0)
        grad_bias_value = jnp.sum(value_grad_low.astype(jnp.float32), axis=0)
        grad_w_query = contract_rows(normed_first, query_grad_low)
        grad_w_key = contract_rows(normed_first, key_grad_low)
        grad_w_value = contract_rows(normed_first, value_grad_low)
        grad_normed = collect_grads(
            contract_cols(query_grad_low, weight_query)
            + contract_cols(key_grad_low, weight_key)
            + contract_cols(value_grad_low, weight_value)
        )
        norm_pull = jax.vjp(
            layer_norm, stream_in, gain_all[layer_index, 0], shift_all[layer_index, 0]
        )[1]
        grad_from_norm, grad_gain_first, grad_shift_first = norm_pull(grad_normed)
        grad_stream = grad_stream + grad_from_norm
        matrix_grads[layer_index] = (
            lax.psum_scatter(
                grad_w_query.astype(jnp.bfloat16), "fsdp", scatter_dimension=0, tiled=True
            ).astype(jnp.float32),
            lax.psum_scatter(
                grad_w_key.astype(jnp.bfloat16), "fsdp", scatter_dimension=0, tiled=True
            ).astype(jnp.float32),
            lax.psum_scatter(
                grad_w_value.astype(jnp.bfloat16), "fsdp", scatter_dimension=0, tiled=True
            ).astype(jnp.float32),
            lax.psum_scatter(
                grad_w_out.astype(jnp.bfloat16), "fsdp", scatter_dimension=1, tiled=True
            ).astype(jnp.float32),
            lax.psum_scatter(
                grad_w_up.astype(jnp.bfloat16), "fsdp", scatter_dimension=0, tiled=True
            ).astype(jnp.float32),
            lax.psum_scatter(
                grad_w_down.astype(jnp.bfloat16), "fsdp", scatter_dimension=1, tiled=True
            ).astype(jnp.float32),
        )
        gain_grads[layer_index] = jnp.stack([grad_gain_first, grad_gain_second])
        shift_grads[layer_index] = jnp.stack([grad_shift_first, grad_shift_second])
        attn_grads[layer_index] = jnp.stack(
            [
                place_part(grad_bias_query, head_start, width),
                place_part(grad_bias_value, head_start, width),
                grad_bias_out,
            ]
        )
        up_grads[layer_index] = place_part(grad_bias_hidden, hidden_start, hidden_full)
    gain_shard, shift_shard, attn_shard, up_shard, down_shard = (
        lax.psum_scatter(jnp.stack(gain_grads), ("fsdp", "tp"), scatter_dimension=2, tiled=True),
        lax.psum_scatter(jnp.stack(shift_grads), ("fsdp", "tp"), scatter_dimension=2, tiled=True),
        lax.psum_scatter(jnp.stack(attn_grads), ("fsdp", "tp"), scatter_dimension=2, tiled=True),
        lax.psum_scatter(jnp.stack(up_grads), ("fsdp", "tp"), scatter_dimension=1, tiled=True),
        lax.psum_scatter(jnp.stack(down_grads), ("fsdp", "tp"), scatter_dimension=1, tiled=True),
    )
    stacked = [
        jnp.stack([matrix_grads[layer_index][member] for layer_index in range(layer_count)])
        for member in range(6)
    ]
    return (
        stream.astype(jnp.bfloat16),
        grad_stream,
        stacked[0],
        stacked[1],
        stacked[2],
        stacked[3],
        stacked[4],
        stacked[5],
        gain_shard,
        shift_shard,
        attn_shard,
        up_shard,
        down_shard,
    )


def solution(mesh):
    return jax.shard_map(
        on_device,
        mesh=mesh,
        in_specs=(
            P(("fsdp", "tp"), None),
            P(("fsdp", "tp"), None),
            P("fsdp", None),
            P(None, "fsdp", "tp"),
            P(None, "fsdp", "tp"),
            P(None, "fsdp", "tp"),
            P(None, "tp", "fsdp"),
            P(None, "fsdp", "tp"),
            P(None, "tp", "fsdp"),
            P(None, None, ("fsdp", "tp")),
            P(None, None, ("fsdp", "tp")),
            P(None, None, ("fsdp", "tp")),
            P(None, ("fsdp", "tp")),
            P(None, ("fsdp", "tp")),
        ),
        out_specs=(
            P(("fsdp", "tp"), None),
            P(("fsdp", "tp"), None),
            P(None, "fsdp", "tp"),
            P(None, "fsdp", "tp"),
            P(None, "fsdp", "tp"),
            P(None, "tp", "fsdp"),
            P(None, "fsdp", "tp"),
            P(None, "tp", "fsdp"),
            P(None, None, ("fsdp", "tp")),
            P(None, None, ("fsdp", "tp")),
            P(None, None, ("fsdp", "tp")),
            P(None, ("fsdp", "tp")),
            P(None, ("fsdp", "tp")),
        ),
        check_vma=False,
    )
```

profile of v0, /device:TPU:0, one launch (start us, length us, event | category | flops | bytes accessed | tf_op | source)
XLA Modules:
  0.0 2281.9 jit_solution(1900157587030748132)
XLA Ops:
  12.6 45.3 %all_gather.88 = f32[2,2,768]{1,0,2:T(2,128)S(1)} all-gather(f32[2,2,24]{1,0,2:T(2,128)S(1)} %copy.50), channel_id=1, replica_groups=mesh['fsdp'=8,'tp'=4] {'fsdp','tp'}, dimensions={2}, use_global_device_ids=true | all-gather | bytes 12672 | tf_op jit(solution)/shard_map/all_gather | solution.py:188
  67.6 39.2 %all_gather.87 = f32[2,2,768]{1,0,2:T(2,128)S(1)} all-gather(f32[2,2,24]{1,0,2:T(2,128)S(1)} %copy.49), channel_id=1, replica_groups=mesh['fsdp'=8,'tp'=4] {'fsdp','tp'}, dimensions={2}, use_global_device_ids=true | all-gather | bytes 12672 | tf_op jit(solution)/shard_map/all_gather | solution.py:187
  118.4 32.1 %all-gather.3 = bf16[1,192,768]{1,0,2:T(2,128)(2,1)S(1)} all-gather(bf16[1,192,96]{1,0,2:T(2,128)(2,1)S(1)} %copy.73), channel_id=5, replica_groups=mesh['fsdp'=8,'tp'=4] {'fsdp'}, dimensions={2}, use_global_device_ids=true | all-gather | bytes 331776 | tf_op jit(solution)/shard_map/all_gather | solution.py:58
  152.1 40.7 %all_gather.91 = f32[2,3,768]{1,0,2:T(2,128)S(1)} all-gather(f32[2,3,24]{1,0,2:T(2,128)S(1)} %copy.51), channel_id=1, replica_groups=mesh['fsdp'=8,'tp'=4] {'fsdp','tp'}, dimensions={2}, use_global_device_ids=true | all-gather | bytes 19008 | tf_op jit(solution)/shard_map/all_gather | solution.py:189
  192.8 15.9 fusion.465
  210.9 33.2 %all-gather = bf16[1,768,192]{2,1,0:T(8,128)(2,1)} all-gather(bf16[1,96,192]{2,1,0:T(8,128)(2,1)S(1)} %get-tuple-element.354), channel_id=2, replica_groups=mesh['fsdp'=8,'tp'=4] {'fsdp'}, dimensions={1}, use_global_device_ids=true | all-gather | bytes 331776 | tf_op jit(solution)/shard_map/all_gather | solution.py:57
  244.2 31.2 %all-gather.2 = bf16[1,768,192]{2,1,0:T(8,128)(2,1)S(1)} all-gather(bf16[1,96,192]{2,1,0:T(8,128)(2,1)S(1)} %get-tuple-element.350), channel_id=4, replica_groups=mesh['fsdp'=8,'tp'=4] {'fsdp'}, dimensions={1}, use_global_device_ids=true | all-gather | bytes 331776 | tf_op jit(solution)/shard_map/all_gather | solution.py:56
  275.4 33.4 %all-gather.1 = bf16[1,768,192]{2,1,0:T(8,128)(2,1)} all-gather(bf16[1,96,192]{2,1,0:T(8,128)(2,1)S(1)} %get-tuple-element.352), channel_id=3, replica_groups=mesh['fsdp'=8,'tp'=4] {'fsdp'}, dimensions={1}, use_global_device_ids=true | all-gather | bytes 331776 | tf_op jit(solution)/shard_map/all_gather | solution.py:55
  340.9 33.6 %reduce-scatter.32.cloned.1.call-done = bf16[512,768]{1,0:T(8,128)(2,1)} async-done(((bf16[2048,768]{1,0:T(8,128)(2,1)}), bf16[512,768]{1,0:T(8,128)(2,1)}) %reduce-scatter.32.cloned.1.call-update) | async-done | bytes 786448 | tf_op jit(solution)/shard_map/reduce_scatter | solution.py:38
  381.0 41.0 %all-gather.12 = f32[32,96,2]{1,2,0:T(2,128)S(1)} all-gather(f32[1,96,2]{1,2,0:T(2,128)S(1)} %bitcast.516), channel_id=1, replica_groups=mesh['fsdp'=8,'tp'=4] {'fsdp','tp'}, dimensions={0}, use_global_device_ids=true | all-gather | bytes 25344 | tf_op jit(solution)/shard_map/all_gather | solution.py:190
  430.4 24.6 %all-gather.45.cloned.1.call-done = bf16[1,768,768]{1,2,0:T(8,128)(2,1)} async-done(((bf16[1,768,96]{1,2,0:T(8,128)(2,1)}), bf16[1,768,768]{1,2,0:T(8,128)(2,1)}) %all-gather.45.cloned.1.call-update) | async-done | bytes 1179664 | tf_op jit(solution)/shard_map/all_gather | solution.py:60
  464.0 39.0 %all-gather.13 = f32[32,24,2]{1,2,0:T(2,128)S(1)} all-gather(f32[1,24,2]{1,2,0:T(2,128)S(1)} %bitcast.517), channel_id=1, replica_groups=mesh['fsdp'=8,'tp'=4] {'fsdp','tp'}, dimensions={0}, use_global_device_ids=true | all-gather | bytes 6336 | tf_op jit(solution)/shard_map/all_gather | solution.py:191
  507.1 32.3 %all-gather.9 = bf16[1,192,768]{1,0,2:T(2,128)(2,1)S(1)} all-gather(bf16[1,192,96]{1,0,2:T(2,128)(2,1)S(1)} %copy.74), channel_id=11, replica_groups=mesh['fsdp'=8,'tp'=4] {'fsdp'}, dimensions={2}, use_global_device_ids=true | all-gather | bytes 331776 | tf_op jit(solution)/shard_map/all_gather | solution.py:58
  544.9 33.2 %all-gather.6 = bf16[1,768,192]{2,1,0:T(8,128)(2,1)} all-gather(bf16[1,96,192]{2,1,0:T(8,128)(2,1)S(1)} %get-tuple-element.353), channel_id=8, replica_groups=mesh['fsdp'=8,'tp'=4] {'fsdp'}, dimensions={1}, use_global_device_ids=true | all-gather | bytes 331776 | tf_op jit(solution)/shard_map/all_gather | solution.py:57
  578.1 31.1 %all-gather.8 = bf16[1,768,192]{2,1,0:T(8,128)(2,1)S(1)} all-gather(bf16[1,96,192]{2,1,0:T(8,128)(2,1)S(1)} %get-tuple-element.349), channel_id=10, replica_groups=mesh['fsdp'=8,'tp'=4] {'fsdp'}, dimensions={1}, use_global_device_ids=true | all-gather | bytes 331776 | tf_op jit(solution)/shard_map/all_gather | solution.py:56
  609.2 30.9 %all-gather.7 = bf16[1,768,192]{2,1,0:T(8,128)(2,1)S(1)} all-gather(bf16[1,96,192]{2,1,0:T(8,128)(2,1)S(1)} %get-tuple-element.351), channel_id=9, replica_groups=mesh['fsdp'=8,'tp'=4] {'fsdp'}, dimensions={1}, use_global_device_ids=true | all-gather | bytes 331776 | tf_op jit(solution)/shard_map/all_gather | solution.py:55
  669.4 33.3 %reduce-scatter.36.cloned.1.call-done = bf16[512,768]{1,0:T(8,128)(2,1)} async-done(((bf16[2048,768]{1,0:T(8,128)(2,1)}), bf16[512,768]{1,0:T(8,128)(2,1)}) %reduce-scatter.36.cloned.1.call-update) | async-done | bytes 786448 | tf_op jit(solution)/shard_map/reduce_scatter | solution.py:38
  710.0 37.3 %all-gather.47.cloned.1.call-done = bf16[1,768,768]{2,1,0:T(8,128)(2,1)} async-done(((bf16[1,96,768]{2,1,0:T(8,128)(2,1)}), bf16[1,768,768]{2,1,0:T(8,128)(2,1)}) %all-gather.47.cloned.1.call-update) | async-done | bytes 1179664 | tf_op jit(solution)/shard_map/all_gather | solution.py:59
  747.3 29.0 %all-gather.33.cloned.1.call-done = bf16[2048,768]{1,0:T(8,128)(2,1)} async-done(((bf16[512,768]{1,0:T(8,128)(2,1)}), bf16[2048,768]{1,0:T(8,128)(2,1)}) %all-gather.33.cloned.1.call-update) | async-done | bytes 3145744 | tf_op jit(solution)/shard_map/all_gather | solution.py:34
  783.8 36.9 %all-gather.49.cloned.1.call-done = bf16[1,768,768]{1,2,0:T(8,128)(2,1)} async-done(((bf16[1,768,96]{1,2,0:T(8,128)(2,1)}), bf16[1,768,768]{1,2,0:T(8,128)(2,1)}) %all-gather.49.cloned.1.call-update) | async-done | bytes 1179664 | tf_op jit(solution)/shard_map/all_gather | solution.py:60
  820.7 28.4 %all-gather.35.cloned.1.call-done = bf16[2048,768]{1,0:T(8,128)(2,1)} async-done(((bf16[512,768]{1,0:T(8,128)(2,1)}), bf16[2048,768]{1,0:T(8,128)(2,1)}) %all-gather.35.cloned.1.call-update) | async-done | bytes 3145744 | tf_op jit(solution)/shard_map/all_gather | solution.py:44
  873.2 29.1 %reduce-scatter.40.cloned.1.call-done = bf16[512,768]{1,0:T(8,128)(2,1)} async-done(((bf16[2048,768]{1,0:T(8,128)(2,1)}), bf16[512,768]{1,0:T(8,128)(2,1)}) %reduce-scatter.40.cloned.1.call-update) | async-done | bytes 786448 | tf_op jit(solution)/shard_map/reduce_scatter | solution.py:48
  906.0 36.7 %reduce-scatter.38.cloned.1.call-done = bf16[512,768]{1,0:T(8,128)(2,1)} async-done(((bf16[2048,768]{1,0:T(8,128)(2,1)}), bf16[512,768]{1,0:T(8,128)(2,1)}) %reduce-scatter.38.cloned.1.call-update) | async-done | bytes 786448 | tf_op jit(solution)/shard_map/reduce_scatter | solution.py:38
  953.3 24.6 %all-gather.37.cloned.1.call-done = bf16[2048,768]{1,0:T(8,128)(2,1)} async-done(((bf16[512,768]{1,0:T(8,128)(2,1)}), bf16[2048,768]{1,0:T(8,128)(2,1)}) %all-gather.37.cloned.1.call-update) | async-done | bytes 3145744 | tf_op jit(solution)/shard_map/all_gather | solution.py:44
  1073.7 17.3 fusion.307
  1091.0 17.5 fusion.313
  1108.4 17.8 fusion.319
  1132.8 38.1 %reduce-scatter.42.cloned.1.call-done = bf16[512,768]{1,0:T(8,128)(2,1)} async-done(((bf16[2048,768]{1,0:T(8,128)(2,1)}), bf16[512,768]{1,0:T(8,128)(2,1)}) %reduce-scatter.42.cloned.1.call-update) | async-done | bytes 786448 | tf_op jit(solution)/shard_map/reduce_scatter | solution.py:48
  1180.8 28.4 %all-gather.39.cloned.1.call-done = bf16[2048,768]{1,0:T(8,128)(2,1)} async-done(((bf16[512,768]{1,0:T(8,128)(2,1)}), bf16[2048,768]{1,0:T(8,128)(2,1)}) %all-gather.39.cloned.1.call-update) | async-done | bytes 3145744 | tf_op jit(solution)/shard_map/all_gather | solution.py:44
  1224.0 37.8 %reduce-scatter.44.cloned.1.call-done = bf16[512,768]{1,0:T(8,128)(2,1)} async-done(((bf16[2048,768]{1,0:T(8,128)(2,1)}), bf16[512,768]{1,0:T(8,128)(2,1)}) %reduce-scatter.44.cloned.1.call-update) | async-done | bytes 786448 | tf_op jit(solution)/shard_map/reduce_scatter | solution.py:48
  1382.4 16.6 fusion.364
  1399.0 16.7 fusion.367
  1423.4 18.0 fusion.229
  1447.8 17.8 fusion.325
  1465.6 14.6 fusion.331
  1480.1 14.3 fusion.337
  1535.4 67.1 %reduce-scatter.64.cloned.1.call-done = bf16[768,96]{0,1:T(8,128)(2,1)} async-done(((bf16[768,768]{0,1:T(8,128)(2,1)}), bf16[768,96]{0,1:T(8,128)(2,1)}) %reduce-scatter.64.cloned.1.call-update) | async-done | bytes 147472 | tf_op jit(solution)/shard_map/reduce_scatter | solution.py:336
  1604.4 65.2 %reduce-scatter.62.cloned.1.call-done = bf16[96,768]{1,0:T(8,128)(2,1)} async-done(((bf16[768,768]{1,0:T(8,128)(2,1)}), bf16[96,768]{1,0:T(8,128)(2,1)}) %reduce-scatter.62.cloned.1.call-update) | async-done | bytes 147472 | tf_op jit(solution)/shard_map/reduce_scatter | solution.py:333
  1669.5 67.1 %reduce-scatter.60.cloned.1.call-done = bf16[96,768]{1,0:T(8,128)(2,1)} async-done(((bf16[768,768]{1,0:T(8,128)(2,1)}), bf16[96,768]{1,0:T(8,128)(2,1)}) %reduce-scatter.60.cloned.1.call-update) | async-done | bytes 147472 | tf_op jit(solution)/shard_map/reduce_scatter | solution.py:333
  1742.8 57.9 %reduce-scatter.68.cloned.1.call-done = bf16[96,192]{1,0:T(8,128)(2,1)} async-done(((bf16[768,192]{1,0:T(8,128)(2,1)}), bf16[96,192]{1,0:T(8,128)(2,1)}) %reduce-scatter.68.cloned.1.call-update) | async-done | bytes 36880
  1802.4 62.4 %reduce-scatter.58.cloned.1.call-done = bf16[96,192]{1,0:T(8,128)(2,1)} async-done(((bf16[768,192]{1,0:T(8,128)(2,1)}), bf16[96,192]{1,0:T(8,128)(2,1)}) %reduce-scatter.58.cloned.1.call-update) | async-done | bytes 36880 | tf_op jit(solution)/shard_map/reduce_scatter | solution.py:327
  1864.8 64.1 %reduce-scatter.56.cloned.1.call-done = bf16[96,192]{1,0:T(8,128)(2,1)} async-done(((bf16[768,192]{1,0:T(8,128)(2,1)}), bf16[96,192]{1,0:T(8,128)(2,1)}) %reduce-scatter.56.cloned.1.call-update) | async-done | bytes 36880 | tf_op jit(solution)/shard_map/reduce_scatter | solution.py:327
  1930.4 62.5 %reduce-scatter.50.cloned.1.call-done = bf16[96,192]{1,0:T(8,128)(2,1)} async-done(((bf16[768,192]{1,0:T(8,128)(2,1)}), bf16[96,192]{1,0:T(8,128)(2,1)}) %reduce-scatter.50.cloned.1.call-update) | async-done | bytes 36880 | tf_op jit(solution)/shard_map/reduce_scatter | solution.py:321
  1992.9 64.0 %reduce-scatter.48.cloned.1.call-done = bf16[96,192]{1,0:T(8,128)(2,1)} async-done(((bf16[768,192]{1,0:T(8,128)(2,1)}), bf16[96,192]{1,0:T(8,128)(2,1)}) %reduce-scatter.48.cloned.1.call-update) | async-done | bytes 36880 | tf_op jit(solution)/shard_map/reduce_scatter | solution.py:321
  2058.5 62.5 %reduce-scatter.54.cloned.1.call-done = bf16[96,192]{1,0:T(8,128)(2,1)} async-done(((bf16[768,192]{1,0:T(8,128)(2,1)}), bf16[96,192]{1,0:T(8,128)(2,1)}) %reduce-scatter.54.cloned.1.call-update) | async-done | bytes 36880 | tf_op jit(solution)/shard_map/reduce_scatter | solution.py:324
  2120.9 64.2 %reduce-scatter.52.cloned.1.call-done = bf16[96,192]{1,0:T(8,128)(2,1)} async-done(((bf16[768,192]{1,0:T(8,128)(2,1)}), bf16[96,192]{1,0:T(8,128)(2,1)}) %reduce-scatter.52.cloned.1.call-update) | async-done | bytes 36880 | tf_op jit(solution)/shard_map/reduce_scatter | solution.py:324
  2186.6 37.9 %reduce-scatter.46.cloned.1.call-done = bf16[512,768]{1,0:T(8,128)(2,1)} async-done(((bf16[2048,768]{1,0:T(8,128)(2,1)}), bf16[512,768]{1,0:T(8,128)(2,1)}) %reduce-scatter.46.cloned.1.call-update) | async-done | bytes 786448 | tf_op jit(solution)/shard_map/reduce_scatter | solution.py:48
  2228.4 40.3 %all-reduce.13 = (f32[2,2,768]{2,1,0:T(2,128)S(1)}, f32[2,2,768]{2,1,0:T(2,128)S(1)}, f32[2,3,768]{2,1,0:T(4,128)S(1)}, f32[2,768]{1,0:T(2,128)S(1)}) all-reduce(f32[2,2,768]{2,1,0:T(2,128)S(1)} %pad_maximum_fusion.10, f32[2,2,768]{2,1,0:T(2,128)S(1)} %pad_maximum_fusion.11, ...), channel_id=34, replica_groups=mesh['fsdp'=8,'tp'=4] {'fsdp','tp'}, use_global_device_ids=true, to_apply=%region_66.67.clone | all-reduce | flops 12288 | bytes 98304
  (715 shorter events, 500.8 us)
Async XLA Ops:
  8.0 110.1 %copy-start.166 = (f32[2,3,24]{2,0,1:T(2,128)S(1)}, f32[2,3,24]{2,0,1:T(2,128)}, u32[]{:S(2)}) copy-start(f32[2,3,24]{2,0,1:T(2,128)} %param.57) | copy-start | bytes 1732
  8.0 110.2 %copy-start.110 = (bf16[2,192,96]{2,1,0:T(8,128)(2,1)S(1)}, bf16[2,192,96]{2,1,0:T(8,128)(2,1)}, u32[]{:S(2)}) copy-start(bf16[2,192,96]{2,1,0:T(8,128)(2,1)} %param.52) | copy-start | bytes 221188
  8.1 303.1 %all-gather.27.cloned.1.call-start = ((), (), s32[]{:S(2)}) async-start(), calls=%async_computation.21 | async-start | bytes 3932160 | tf_op jit(solution)/shard_map/all_gather | solution.py:34
  67.6 143.3 %copy-start.111 = (bf16[2,96,192]{2,1,0:T(8,128)(2,1)S(1)}, bf16[2,96,192]{2,1,0:T(8,128)(2,1)}, u32[]{:S(2)}) copy-start(bf16[2,96,192]{2,1,0:T(8,128)(2,1)} %param.51) | copy-start | bytes 221188
  67.6 176.5 %copy-start.112 = (bf16[2,96,192]{2,1,0:T(8,128)(2,1)S(1)}, bf16[2,96,192]{2,1,0:T(8,128)(2,1)}, u32[]{:S(2)}) copy-start(bf16[2,96,192]{2,1,0:T(8,128)(2,1)} %param.50) | copy-start | bytes 221188
  106.9 168.5 %copy-start.113 = (bf16[2,96,192]{2,1,0:T(8,128)(2,1)S(1)}, bf16[2,96,192]{2,1,0:T(8,128)(2,1)}, u32[]{:S(2)}) copy-start(bf16[2,96,192]{2,1,0:T(8,128)(2,1)} %param.49) | copy-start | bytes 221188
  116.6 261.0 %copy-start.104 = (f32[768]{0:T(1024)}, f32[768]{0:T(1024)S(1)}, u32[]{:S(2)}) copy-start(f32[768]{0:T(1024)S(1)} %get-tuple-element.276) | copy-start | bytes 9220
  116.6 389.1 %copy-start.108 = (f32[768]{0:T(1024)}, f32[768]{0:T(1024)S(1)}, u32[]{:S(2)}) copy-start(f32[768]{0:T(1024)S(1)} %get-tuple-element.275) | copy-start | bytes 9220
  117.9 256.6 %reduce-scatter.32.cloned.1.call-start = ((), (), s32[]{:S(2)}) async-start(), calls=%async_computation.22 | async-start | bytes 3932160 | tf_op jit(solution)/shard_map/reduce_scatter | solution.py:38
  208.7 295.0 %copy-start.102 = (f32[768]{0:T(1024)}, f32[768]{0:T(1024)S(1)}, u32[]{:S(2)}) copy-start(f32[768]{0:T(1024)S(1)} %get-tuple-element.329) | copy-start | bytes 9220
  340.1 82.7 %all-gather.43.cloned.1.call-start = ((), (), s32[]{:S(2)}) async-start(), calls=%async_computation.47 | async-start | bytes 1327104 | tf_op jit(solution)/shard_map/all_gather | solution.py:59
  340.9 81.9 %all-gather.29.cloned.1.call-start = ((), (), s32[]{:S(2)}) async-start(), calls=%async_computation.23 | async-start | bytes 3932160 | tf_op jit(solution)/shard_map/all_gather | solution.py:34
  380.1 74.9 %all-gather.45.cloned.1.call-start = ((), (), s32[]{:S(2)}) async-start(), calls=%async_computation.48 | async-start | bytes 1327104 | tf_op jit(solution)/shard_map/all_gather | solution.py:60
  380.9 122.8 %reduce-scatter.34.cloned.1.call-start = ((), (), s32[]{:S(2)}) async-start(), calls=%async_computation.24 | async-start | bytes 3932160 | tf_op jit(solution)/shard_map/reduce_scatter | solution.py:38
  463.9 176.2 %all-gather.31.cloned.1.call-start = ((), (), s32[]{:S(2)}) async-start(), calls=%async_computation.25 | async-start | bytes 3932160 | tf_op jit(solution)/shard_map/all_gather | solution.py:34
  505.4 138.1 %copy-start.118 = (f32[512]{0:T(512)}, f32[512]{0:T(512)S(1)}, u32[]{:S(2)}) copy-start(f32[512]{0:T(512)S(1)} %broadcast_multiply_fusion.1) | copy-start | bytes 6148
  506.9 195.8 %reduce-scatter.36.cloned.1.call-start = ((), (), s32[]{:S(2)}) async-start(), calls=%async_computation.26 | async-start | bytes 3932160 | tf_op jit(solution)/shard_map/reduce_scatter | solution.py:38
  668.2 79.1 %all-gather.47.cloned.1.call-start = ((), (), s32[]{:S(2)}) async-start(), calls=%async_computation.49 | async-start | bytes 1327104 | tf_op jit(solution)/shard_map/all_gather | solution.py:59
  669.0 107.3 %all-gather.33.cloned.1.call-start = ((), (), s32[]{:S(2)}) async-start(), calls=%async_computation.27 | async-start | bytes 3932160 | tf_op jit(solution)/shard_map/all_gather | solution.py:34
  707.5 113.2 %all-gather.49.cloned.1.call-start = ((), (), s32[]{:S(2)}) async-start(), calls=%async_computation.50 | async-start | bytes 1327104 | tf_op jit(solution)/shard_map/all_gather | solution.py:60
  708.1 141.0 %all-gather.35.cloned.1.call-start = ((), (), s32[]{:S(2)}) async-start(), calls=%async_computation.29 | async-start | bytes 3932160 | tf_op jit(solution)/shard_map/all_gather | solution.py:44
  708.7 193.6 %reduce-scatter.40.cloned.1.call-start = ((), (), s32[]{:S(2)}) async-start(), calls=%async_computation.30 | async-start | bytes 3932160 | tf_op jit(solution)/shard_map/reduce_scatter | solution.py:48
  864.2 78.5 %reduce-scatter.38.cloned.1.call-start = ((), (), s32[]{:S(2)}) async-start(), calls=%async_computation.28 | async-start | bytes 3932160 | tf_op jit(solution)/shard_map/reduce_scatter | solution.py:38
  873.2 104.7 %all-gather.37.cloned.1.call-start = ((), (), s32[]{:S(2)}) async-start(), calls=%async_computation.31 | async-start | bytes 3932160 | tf_op jit(solution)/shard_map/all_gather | solution.py:44
  949.2 221.7 %reduce-scatter.42.cloned.1.call-start = ((), (), s32[]{:S(2)}) async-start(), calls=%async_computation.32 | async-start | bytes 3932160 | tf_op jit(solution)/shard_map/reduce_scatter | solution.py:48
  1132.8 76.5 %all-gather.39.cloned.1.call-start = ((), (), s32[]{:S(2)}) async-start(), calls=%async_computation.33 | async-start | bytes 3932160 | tf_op jit(solution)/shard_map/all_gather | solution.py:44
  1180.7 81.1 %reduce-scatter.44.cloned.1.call-start = ((), (), s32[]{:S(2)}) async-start(), calls=%async_computation.34 | async-start | bytes 3932160 | tf_op jit(solution)/shard_map/reduce_scatter | solution.py:48
  1223.7 84.3 %all-gather.41.cloned.1.call-start = ((), (), s32[]{:S(2)}) async-start(), calls=%async_computation.35 | async-start | bytes 3932160 | tf_op jit(solution)/shard_map/all_gather | solution.py:44
  1271.0 247.9 %reduce-scatter.70.cloned.1.call-start = ((), (), s32[]{:S(2)}) async-start(), calls=%async_computation.52 | async-start | bytes 442368
  1275.0 250.3 %reduce-scatter.72.cloned.1.call-start = ((), (), s32[]{:S(2)}) async-start(), calls=%async_computation.53 | async-start | bytes 1622016
  1276.9 258.5 %reduce-scatter.66.cloned.1.call-start = ((), (), s32[]{:S(2)}) async-start(), calls=%async_computation.46 | async-start | bytes 1327104 | tf_op jit(solution)/shard_map/reduce_scatter | solution.py:336
  1285.9 316.6 %reduce-scatter.64.cloned.1.call-start = ((), (), s32[]{:S(2)}) async-start(), calls=%async_computation.45 | async-start | bytes 1327104 | tf_op jit(solution)/shard_map/reduce_scatter | solution.py:336
  1294.1 375.4 %reduce-scatter.62.cloned.1.call-start = ((), (), s32[]{:S(2)}) async-start(), calls=%async_computation.44 | async-start | bytes 1327104 | tf_op jit(solution)/shard_map/reduce_scatter | solution.py:333
  1301.2 435.5 %reduce-scatter.60.cloned.1.call-start = ((), (), s32[]{:S(2)}) async-start(), calls=%async_computation.43 | async-start | bytes 1327104 | tf_op jit(solution)/shard_map/reduce_scatter | solution.py:333
  1307.8 492.9 %reduce-scatter.68.cloned.1.call-start = ((), (), s32[]{:S(2)}) async-start(), calls=%async_computation.51 | async-start | bytes 442368
  1313.8 551.0 %reduce-scatter.58.cloned.1.call-start = ((), (), s32[]{:S(2)}) async-start(), calls=%async_computation.42 | async-start | bytes 442368 | tf_op jit(solution)/shard_map/reduce_scatter | solution.py:327
  1318.8 610.2 %reduce-scatter.56.cloned.1.call-start = ((), (), s32[]{:S(2)}) async-start(), calls=%async_computation.41 | async-start | bytes 442368 | tf_op jit(solution)/shard_map/reduce_scatter | solution.py:327
  1336.3 656.6 %reduce-scatter.50.cloned.1.call-start = ((), (), s32[]{:S(2)}) async-start(), calls=%async_computation.38 | async-start | bytes 442368 | tf_op jit(solution)/shard_map/reduce_scatter | solution.py:321
  1340.2 716.7 %reduce-scatter.48.cloned.1.call-start = ((), (), s32[]{:S(2)}) async-start(), calls=%async_computation.37 | async-start | bytes 442368 | tf_op jit(solution)/shard_map/reduce_scatter | solution.py:321
  1419.6 701.3 %reduce-scatter.54.cloned.1.call-start = ((), (), s32[]{:S(2)}) async-start(), calls=%async_computation.40 | async-start | bytes 442368 | tf_op jit(solution)/shard_map/reduce_scatter | solution.py:324
  1423.4 761.7 %reduce-scatter.52.cloned.1.call-start = ((), (), s32[]{:S(2)}) async-start(), calls=%async_computation.39 | async-start | bytes 442368 | tf_op jit(solution)/shard_map/reduce_scatter | solution.py:324
  1503.4 238.0 %copy-start.94 = (bf16[3,64,512]{2,1,0:T(8,128)(2,1)S(1)}, bf16[3,64,512]{2,1,0:T(8,128)(2,1)}, u32[]{:S(2)}) copy-start(bf16[3,64,512]{2,1,0:T(8,128)(2,1)} %copy-done.93) | copy-start | bytes 589828
  1503.4 238.0 %copy-start.96 = (bf16[3,64,512]{2,1,0:T(8,128)(2,1)S(1)}, bf16[3,64,512]{2,1,0:T(8,128)(2,1)}, u32[]{:S(2)}) copy-start(bf16[3,64,512]{2,1,0:T(8,128)(2,1)} %fusion.361) | copy-start | bytes 589828
  1503.4 721.0 %reduce-scatter.46.cloned.1.call-start = ((), (), s32[]{:S(2)}) async-start(), calls=%async_computation.36 | async-start | bytes 3932160 | tf_op jit(solution)/shard_map/reduce_scatter | solution.py:48
  1511.6 712.9 %copy-start.107 = (f32[768]{0:T(1024)S(1)}, f32[768]{0:T(1024)}, u32[]{:S(2)}) copy-start(f32[768]{0:T(1024)} %copy-done.106) | copy-start | bytes 9220
  1511.6 712.9 %copy-start.115 = (f32[512]{0:T(512)S(1)}, f32[512]{0:T(512)}, u32[]{:S(2)}) copy-start(f32[512]{0:T(512)} %copy-done.114) | copy-start | bytes 6148
  1511.6 714.6 %copy-start.154 = (f32[512]{0:T(512)S(1)}, f32[512]{0:T(512)}, u32[]{:S(2)}) copy-start(f32[512]{0:T(512)} %copy-done.153) | copy-start | bytes 6148
  1511.6 714.6 %copy-start.132 = (f32[512]{0:T(512)S(1)}, f32[512]{0:T(512)}, u32[]{:S(2)}) copy-start(f32[512]{0:T(512)} %copy-done.131) | copy-start | bytes 6148
  (180 other events, 2647.3 us)
Sparse Core Ops, SparseCore 0:
  118.0 25.8 all-gather.26
  340.2 34.2 reduce-scatter.31
  507.1 25.2 all-gather.30
  864.3 37.9 reduce-scatter.39
  904.7 37.9 reduce-scatter.37
  949.3 28.5 all-gather.36
  1132.9 37.9 reduce-scatter.41
  1223.8 37.9 reduce-scatter.43
Sparse Core Ops, SparseCore 1:
  343.5 37.8 all-gather.42
  383.5 27.0 all-gather.28
  413.4 41.5 all-gather.44
  464.0 36.4 reduce-scatter.33
  668.3 34.4 reduce-scatter.35
  705.8 41.5 all-gather.46
  749.4 26.8 all-gather.32
  779.2 41.5 all-gather.48
  822.2 26.8 all-gather.34
  1180.8 28.3 all-gather.38
  1271.1 28.3 all-gather.40
  1303.7 61.4 reduce-scatter.69
  1371.7 96.4 reduce-scatter.71
  1472.0 63.4 reduce-scatter.65
  1539.2 63.2 reduce-scatter.63
  1606.3 63.2 reduce-scatter.61
  1673.3 63.2 reduce-scatter.59
  1740.3 60.4 reduce-scatter.67
  1804.2 60.5 reduce-scatter.57
  1868.4 60.4 reduce-scatter.55
  1932.4 60.5 reduce-scatter.49
  1996.4 60.5 reduce-scatter.47
  2060.4 60.4 reduce-scatter.53
  2124.5 60.5 reduce-scatter.51
  2187.7 36.8 reduce-scatter.45
where the time goes:
time: 2290 us; the launch traced here: 2280 us
  waiting for transfers between devices  1100 us (48%)
  blocking collectives  503 us (22%)
  matrix products  479 us (21%)
  local copies, waits for them, and re-layouts  89.1 us (4%)
  other arithmetic  85 us (4%)
    reduce_scatter x4, waiting for transfers between devices, collect_grads(): lax.psum_scatter(partial_value.astype(jnp.bfloat16), 'tp', scatter_dimens...  143 us
    reduce_scatter x2, waiting for transfers between devices, on_device(): lax.psum_scatter(grad_w_up.astype(jnp.bfloat16), 'fsdp', scatter_dimensio...  132 us
    dot_general x8, matrix products, attend_backward(): jnp.einsum('hqk,qhd->khd', grad_raw, query_block, preferred_element_type=...  131 us
    reduce_scatter x2, waiting for transfers between devices, on_device(): lax.psum_scatter(grad_w_key.astype(jnp.bfloat16), 'fsdp', scatter_dimensi...  127 us
    reduce_scatter x2, waiting for transfers between devices, on_device(): lax.psum_scatter(grad_w_value.astype(jnp.bfloat16), 'fsdp', scatter_dimen...  127 us
    reduce_scatter x2, waiting for transfers between devices, on_device(): lax.psum_scatter(grad_w_query.astype(jnp.bfloat16), 'fsdp', scatter_dimen...  127 us
    dot_general x8, matrix products, attend_backward(): jnp.einsum('hqk,khd->qhd', grad_raw, key_window, preferred_element_type=j...  113 us
    reduce_scatter x4, waiting for transfers between devices, collect_rows(): lax.psum_scatter(partial_value.astype(jnp.bfloat16), 'tp', scatter_dimens...  104 us
  transfers between devices with their start and end apart: 33, of which 25 were waited for; matrix products, arithmetic and copies ran while one was open for 15% of the time, Pallas kernels for 0%

commit v1 on v0

v1 whole, which is shorter than its diff:
```python
import functools

import jax
import jax.numpy as jnp
from jax import lax
from jax.experimental import pallas as pl
from jax.experimental.pallas import tpu as pltpu
from jax.sharding import PartitionSpec as P

HEAD = 64
LANES = 128
QROWS = 256
eps = 1e-05
masked_fill = -1e30
VMEM_BYTES = 56 * 1024 * 1024
BOTH = ("fsdp", "tp")

f32 = jnp.float32
bf16 = jnp.bfloat16


def dot_nn(left, right):
    return lax.dot_general(left, right, (((1,), (0,)), ((), ())), preferred_element_type=f32)


def dot_nt(left, right):
    return lax.dot_general(left, right, (((1,), (1,)), ((), ())), preferred_element_type=f32)


def dot_tn(left, right):
    return lax.dot_general(left, right, (((0,), (0,)), ((), ())), preferred_element_type=f32)


def fill_bias(seg_q_ref, seg_k_ref, bias_ref, rows):
    window = rows + QROWS
    for first in range(0, rows, QROWS):
        row_pos = rows + first + lax.broadcasted_iota(jnp.int32, (QROWS, window), 0)
        col_pos = first + lax.broadcasted_iota(jnp.int32, (QROWS, window), 1)
        same = seg_q_ref[first : first + QROWS, :] == seg_k_ref[:, first : first + window]
        bias_ref[first : first + QROWS, :] = jnp.where(same & (col_pos <= row_pos), 0.0, masked_fill)


def attend_forward_body(rows, seg_q_ref, seg_k_ref, q_ref, k_ref, v_ref, o_ref, lse_ref, bias_ref):
    window = rows + QROWS

    @pl.when(pl.program_id(0) == 0)
    def _():
        fill_bias(seg_q_ref, seg_k_ref, bias_ref, rows)

    low_lane = lax.broadcasted_iota(jnp.int32, (QROWS, LANES), 1) < HEAD
    for first in range(0, rows, QROWS):
        here = slice(first, first + QROWS)
        keys = k_ref[first : first + window, :]
        values = v_ref[first : first + window, :]
        bias = bias_ref[here, :]
        queries = q_ref[here, :] * jnp.asarray(HEAD**-0.5, bf16)
        outs, lses = [], []
        for head in range(2):
            mine = low_lane if head == 0 else ~low_lane
            scores = dot_nt(jnp.where(mine, queries, 0), keys) + bias
            top = jnp.max(scores, axis=-1, keepdims=True)
            terms = jnp.exp(scores - top)
            total = jnp.sum(terms, axis=-1, keepdims=True)
            outs.append(dot_nn(terms.astype(bf16), values) * (1.0 / total))
            lses.append(top + jnp.log(total))
        o_ref[here, :] = jnp.where(low_lane, outs[0], outs[1]).astype(bf16)
        lse_ref[here, :] = jnp.where(low_lane, lses[0], lses[1])


def attend_backward_body(
    rows, seg_q_ref, seg_k_ref, q_ref, k_ref, v_ref, o_ref, lse_ref, do_ref,
    dq_ref, dk_ref, dv_ref, bias_ref, dk_acc, dv_acc,
):
    window = rows + QROWS

    @pl.when(pl.program_id(0) == 0)
    def _():
        fill_bias(seg_q_ref, seg_k_ref, bias_ref, rows)

    dk_acc[...] = jnp.zeros_like(dk_acc)
    dv_acc[...] = jnp.zeros_like(dv_acc)
    low_lane = lax.broadcasted_iota(jnp.int32, (QROWS, LANES), 1) < HEAD
    for first in range(0, rows, QROWS):
        here = slice(first, first + QROWS)
        span = slice(first, first + window)
        keys = k_ref[span, :]
        values = v_ref[span, :]
        bias = bias_ref[here, :]
        queries = q_ref[here, :] * jnp.asarray(HEAD**-0.5, bf16)
        grads = do_ref[here, :]
        product = grads.astype(f32) * o_ref[here, :].astype(f32)
        lse_both = lse_ref[here, :]
        dqs, dks, dvs = [], [], []
        for head in range(2):
            mine = low_lane if head == 0 else ~low_lane
            my_queries = jnp.where(mine, queries, 0)
            my_grads = jnp.where(mine, grads, 0)
            inner = jnp.sum(jnp.where(mine, product, 0.0), axis=-1, keepdims=True)
            lse = lse_both[:, head * HEAD : head * HEAD + 1]
            probs = jnp.exp(dot_nt(my_queries, keys) + bias - lse)
            draw = (probs * (dot_nt(my_grads, values) - inner)).astype(bf16)
            dvs.append(dot_tn(probs.astype(bf16), my_grads))
            dks.append(dot_tn(draw, my_queries))
            dqs.append(dot_nn(draw, keys))
        dv_acc[span, :] += dvs[0] + dvs[1]
        dk_acc[span, :] += dks[0] + dks[1]
        dq_ref[here, :] = (jnp.where(low_lane, dqs[0], dqs[1]) * HEAD**-0.5).astype(bf16)
    dk_ref[...] = dk_acc[...].astype(bf16)
    dv_ref[...] = dv_acc[...].astype(bf16)


def pair_spec(rows):
    return pl.BlockSpec((rows, LANES), lambda pair: (0, pair))


def whole_spec(shape):
    return pl.BlockSpec(shape, lambda *_: (0,) * len(shape))


def attend_forward(seg_q, seg_k, queries, keys, values):
    rows, width = queries.shape
    return pl.pallas_call(
        functools.partial(attend_forward_body, rows),
        grid=(width // LANES,),
        in_specs=[
            whole_spec(seg_q.shape), whole_spec(seg_k.shape),
            pair_spec(rows), pair_spec(2 * rows), pair_spec(2 * rows),
        ],
        out_specs=[pair_spec(rows), pair_spec(rows)],
        out_shape=[
            jax.ShapeDtypeStruct((rows, width), bf16),
            jax.ShapeDtypeStruct((rows, width), f32),
        ],
        scratch_shapes=[pltpu.VMEM((rows, rows + QROWS), f32)],
        compiler_params=pltpu.CompilerParams(vmem_limit_bytes=VMEM_BYTES),
        cost_estimate=pl.CostEstimate(
            flops=16 * rows * (rows + QROWS) * width, bytes_accessed=6 * rows * width * 2,
            transcendentals=rows * rows * width // HEAD,
        ),
        name="attend_forward",
    )(seg_q, seg_k, queries, keys, values)


def attend_backward(seg_q, seg_k, queries, keys, values, attended, lse, grad_attended):
    rows, width = queries.shape
    return pl.pallas_call(
        functools.partial(attend_backward_body, rows),
        grid=(width // LANES,),
        in_specs=[
            whole_spec(seg_q.shape), whole_spec(seg_k.shape),
            pair_spec(rows), pair_spec(2 * rows), pair_spec(2 * rows),
            pair_spec(rows), pair_spec(rows), pair_spec(rows),
        ],
        out_specs=[pair_spec(rows), pair_spec(2 * rows), pair_spec(2 * rows)],
        out_shape=[
            jax.ShapeDtypeStruct((rows, width), bf16),
            jax.ShapeDtypeStruct((2 * rows, width), bf16),
            jax.ShapeDtypeStruct((2 * rows, width), bf16),
        ],
        scratch_shapes=[
            pltpu.VMEM((rows, rows + QROWS), f32),
            pltpu.VMEM((2 * rows, LANES), f32),
            pltpu.VMEM((2 * rows, LANES), f32),
        ],
        compiler_params=pltpu.CompilerParams(vmem_limit_bytes=VMEM_BYTES),
        cost_estimate=pl.CostEstimate(
            flops=40 * rows * (rows + QROWS) * width, bytes_accessed=12 * rows * width * 2,
            transcendentals=rows * rows * width // HEAD,
        ),
        name="attend_backward",
    )(seg_q, seg_k, queries, keys, values, attended, lse, grad_attended)


GELU_A = 0.7978845608028654
GELU_B = 0.044715


def gelu_parts(pre):
    square = pre * pre
    bend = jnp.tanh(GELU_A * pre * (1.0 + GELU_B * square))
    half = 0.5 * (1.0 + bend)
    slope = half + 0.5 * pre * (1.0 - bend * bend) * (GELU_A * (1.0 + 3.0 * GELU_B * square))
    return pre * half, slope


def feed_forward_body(n_ref, up_ref, down_ref, bias_ref, pre_ref, out_ref):
    @pl.when(pl.program_id(0) == 0)
    def _():
        out_ref[...] = jnp.zeros_like(out_ref)

    pre = dot_nn(n_ref[...], up_ref[0]) + bias_ref[0]
    pre_ref[0] = pre
    hidden = gelu_parts(pre)[0].astype(bf16)
    out_ref[...] += dot_nt(hidden, down_ref[0])


def feed_forward(normed, up, down, bias):
    rows, width = normed.shape
    parts, _, cols = up.shape
    part = pl.BlockSpec((1, width, cols), lambda t: (t, 0, 0))
    return pl.pallas_call(
        feed_forward_body,
        grid=(parts,),
        in_specs=[
            whole_spec((rows, width)), part, part,
            pl.BlockSpec((1, 1, cols), lambda t: (t, 0, 0)),
        ],
        out_specs=[pl.BlockSpec((1, rows, cols), lambda t: (t, 0, 0)), whole_spec((rows, width))],
        out_shape=[
            jax.ShapeDtypeStruct((parts, rows, cols), f32),
            jax.ShapeDtypeStruct((rows, width), f32),
        ],
        compiler_params=pltpu.CompilerParams(vmem_limit_bytes=VMEM_BYTES),
        cost_estimate=pl.CostEstimate(
            flops=4 * rows * width * cols * parts, bytes_accessed=4 * parts * width * cols + 4 * parts * rows * cols,
            transcendentals=rows * cols * parts,
        ),
        name="feed_forward",
    )(normed, up, down, bias)


def feed_backward_body(
    g_ref, gt_ref, nt_ref, pre_ref, up_ref, down_ref, gup_ref, gdown_ref, gbias_ref, dn_ref
):
    @pl.when(pl.program_id(0) == 0)
    def _():
        dn_ref[...] = jnp.zeros_like(dn_ref)

    hidden, slope = gelu_parts(pre_ref[0])
    gdown_ref[0] = dot_nn(gt_ref[...], hidden.astype(bf16)).astype(bf16)
    dpre = (dot_nn(g_ref[...], down_ref[0]) * slope).astype(bf16)
    gbias_ref[0] = jnp.sum(dpre.astype(f32), axis=0, keepdims=True)
    gup_ref[0] = dot_nn(nt_ref[...], dpre).astype(bf16)
    dn_ref[...] += dot_nt(dpre, up_ref[0])


def feed_backward(grad_low, normed, pre, up, down):
    rows, width = normed.shape
    parts, _, cols = up.shape
    part = pl.BlockSpec((1, width, cols), lambda t: (t, 0, 0))
    return pl.pallas_call(
        feed_backward_body,
        grid=(parts,),
        in_specs=[
            whole_spec((rows, width)), whole_spec((width, rows)), whole_spec((width, rows)),
            pl.BlockSpec((1, rows, cols), lambda t: (t, 0, 0)), part, part,
        ],
        out_specs=[
            part, part, pl.BlockSpec((1, 1, cols), lambda t: (t, 0, 0)), whole_spec((rows, width)),
        ],
        out_shape=[
            jax.ShapeDtypeStruct((parts, width, cols), bf16),
            jax.ShapeDtypeStruct((parts, width, cols), bf16),
            jax.ShapeDtypeStruct((parts, 1, cols), f32),
            jax.ShapeDtypeStruct((rows, width), f32),
        ],
        compiler_params=pltpu.CompilerParams(vmem_limit_bytes=VMEM_BYTES),
        cost_estimate=pl.CostEstimate(
            flops=8 * rows * width * cols * parts, bytes_accessed=8 * parts * width * cols + 4 * parts * rows * cols,
            transcendentals=rows * cols * parts,
        ),
        name="feed_backward",
    )(grad_low, grad_low.T, normed.T, pre, up, down)


def norm_stats(values):
    mean = jnp.mean(values, axis=-1, keepdims=True)
    centred = values - mean
    var = jnp.mean(centred * centred, axis=-1, keepdims=True)
    scale = lax.rsqrt(var + eps)
    return centred * scale, scale


def norm_forward(values, gain, shift):
    return (norm_stats(values)[0] * gain + shift).astype(bf16)


def norm_backward(values, gain, grad):
    unit, scale = norm_stats(values)
    inner = grad * gain
    back = scale * (
        inner
        - jnp.mean(inner, axis=-1, keepdims=True)
        - unit * jnp.mean(inner * unit, axis=-1, keepdims=True)
    )
    return back, jnp.sum(grad * unit, axis=0), jnp.sum(grad, axis=0)


def gather_weights(shard):
    fsdp, tp = lax.axis_size("fsdp"), lax.axis_size("tp")
    rows, cols = shard.shape
    whole = lax.all_gather(shard, BOTH, axis=0, tiled=False).reshape(fsdp, tp, rows, cols)
    return whole.transpose(1, 0, 2, 3).reshape(tp, fsdp * rows, cols)


def scatter_grads(grad):
    fsdp, tp = lax.axis_size("fsdp"), lax.axis_size("tp")
    rows, cols = grad.shape[1] // fsdp, grad.shape[2]
    parts = grad.reshape(tp, fsdp, rows, cols).transpose(1, 0, 2, 3).reshape(-1, cols)
    return lax.psum_scatter(parts, BOTH, scatter_dimension=0, tiled=True).astype(f32)


def from_previous(rows):
    tp = lax.axis_size("tp")
    return lax.ppermute(rows, "tp", [(i, i + 1) for i in range(tp - 1)])


def to_previous(rows):
    tp = lax.axis_size("tp")
    return lax.ppermute(rows, "tp", [(i + 1, i) for i in range(tp - 1)])


def side_by_side(parts):
    return jnp.concatenate([parts[t] for t in range(parts.shape[0])], axis=1)


def apart(whole, parts):
    cols = whole.shape[1] // parts
    return [whole[:, t * cols : (t + 1) * cols] for t in range(parts)]


def on_device(
    tokens, cotangent, lengths, w_query, w_key, w_value, w_out, w_up, w_down,
    norm_gain, norm_shift, attn_bias, up_bias, down_bias,
):
    fsdp, tp = lax.axis_size("fsdp"), lax.axis_size("tp")
    devices = fsdp * tp
    tp_index = lax.axis_index("tp")
    rows, width = tokens.shape
    layers = w_query.shape[0]
    head_cols, hidden_cols = w_query.shape[2], w_up.shape[2]

    smalls = [norm_gain, norm_shift, attn_bias, up_bias, down_bias]
    packed = jnp.concatenate([part.reshape(1, -1) for part in smalls], axis=1)
    packed_all = lax.all_gather(packed, BOTH, axis=0, tiled=True)
    wholes, at = [], 0
    for part in smalls:
        size, lead, last = part.size, part.shape[:-1], part.shape[-1]
        piece = packed_all[:, at : at + size].reshape((devices,) + part.shape)
        wholes.append(jnp.moveaxis(piece, 0, -2).reshape(lead + (devices * last,)))
        at += size
    gain_all, shift_all, bias_attn, bias_up, bias_down = wholes

    weights = []
    for layer in range(layers):
        attn_shard = jnp.concatenate(
            [w_query[layer], w_key[layer], w_value[layer], w_out[layer].T], axis=1
        )
        weights.append(
            (gather_weights(attn_shard), gather_weights(w_up[layer]), gather_weights(w_down[layer].T))
        )

    seq_ends = jnp.cumsum(lengths[0])
    first_row = tp_index * rows
    key_ids = first_row - rows + jnp.arange(2 * rows, dtype=jnp.int32)
    segments = jnp.sum((key_ids[:, None] >= seq_ends[None, :]).astype(jnp.int32), axis=1)
    segments = jnp.where(key_ids >= 0, segments, -1)
    seg_q, seg_k = segments[rows:, None], segments[None, :]

    stream = tokens.astype(f32)
    saved = []
    for layer in range(layers):
        attn_w, up, down = weights[layer]
        wq, wk, wv, wo = (
            side_by_side(attn_w[:, :, n * head_cols : (n + 1) * head_cols]) for n in range(4)
        )
        normed = norm_forward(stream, gain_all[layer, 0], shift_all[layer, 0])
        wide = jnp.concatenate([from_previous(normed), normed], axis=0)
        queries = (dot_nn(normed, wq) + bias_attn[layer, 0]).astype(bf16)
        keys = dot_nn(wide, wk).astype(bf16)
        values = (dot_nn(wide, wv) + bias_attn[layer, 1]).astype(bf16)
        attended, lse = attend_forward(seg_q, seg_k, queries, keys, values)
        mid = stream + dot_nt(attended, wo) + bias_attn[layer, 2]
        normed_mid = norm_forward(mid, gain_all[layer, 1], shift_all[layer, 1])
        pre, fed = feed_forward(
            normed_mid, up, down, bias_up[layer].reshape(tp, 1, hidden_cols)
        )
        saved.append(
            (stream, wide, queries, keys, values, attended, lse, mid, normed_mid, pre, wq, wk, wv, wo)
        )
        stream = mid + fed + bias_down[layer]

    grad = cotangent.astype(f32)
    shards = [None] * layers
    small_grads = [None] * layers
    for layer in reversed(range(layers)):
        _, up, down = weights[layer]
        stream_in, wide, queries, keys, values, attended, lse, mid, normed_mid, pre, wq, wk, wv, wo = (
            saved[layer]
        )
        normed = wide[rows:]
        grad_bias_down = jnp.sum(grad, axis=0)
        grad_low = grad.astype(bf16)
        grad_up, grad_down, grad_bias_up, dn = feed_backward(grad_low, normed_mid, pre, up, down)
        up_shard, down_shard = scatter_grads(grad_up), scatter_grads(grad_down)
        back, gain_second, shift_second = norm_backward(mid, gain_all[layer, 1], dn)
        grad = grad + back
        grad_bias_out = jnp.sum(grad, axis=0)
        grad_low = grad.astype(bf16)
        grad_wo = dot_tn(grad_low, attended).astype(bf16)
        grad_attended = dot_nn(grad_low, wo).astype(bf16)
        dq, dk, dv = attend_backward(seg_q, seg_k, queries, keys, values, attended, lse, grad_attended)
        dn_wide = dot_nt(dk, wk) + dot_nt(dv, wv)
        dn_before = to_previous(dn_wide[:rows].astype(bf16)).astype(f32)
        grad_wq = dot_tn(normed, dq).astype(bf16)
        grad_wk = dot_tn(wide, dk).astype(bf16)
        grad_wv = dot_tn(wide, dv).astype(bf16)
        grad_attn = jnp.stack(
            [
                jnp.concatenate(four, axis=1)
                for four in zip(*(apart(whole, tp) for whole in (grad_wq, grad_wk, grad_wv, grad_wo)))
            ]
        )
        attn_shard = scatter_grads(grad_attn)
        dn = dn_wide[rows:] + dot_nt(dq, wq) + dn_before
        back, gain_first, shift_first = norm_backward(stream_in, gain_all[layer, 0], dn)
        grad = grad + back
        shards[layer] = tuple(attn_shard[:, n * head_cols : (n + 1) * head_cols] for n in range(3)) + (
            attn_shard[:, 3 * head_cols :].T, up_shard, down_shard.T,
        )
        small_grads[layer] = (
            jnp.stack([gain_first, gain_second]),
            jnp.stack([shift_first, shift_second]),
            jnp.stack(
                [jnp.sum(dq.astype(f32), axis=0), jnp.sum(dv.astype(f32), axis=0), grad_bias_out]
            ),
            grad_bias_up.reshape(-1),
            grad_bias_down,
        )

    pieces = []
    for member, part in enumerate(smalls):
        whole = jnp.stack([small_grads[layer][member] for layer in range(layers)])
        last = part.shape[-1]
        split = whole.reshape(part.shape[:-1] + (devices, last))
        pieces.append(jnp.moveaxis(split, -2, 0).reshape(devices, part.size))
    summed = lax.psum_scatter(
        jnp.concatenate(pieces, axis=1), BOTH, scatter_dimension=0, tiled=True
    )
    small_outs, at = [], 0
    for part in smalls:
        small_outs.append(summed[:, at : at + part.size].reshape(part.shape))
        at += part.size
    stacked = [jnp.stack([shards[layer][n] for layer in range(layers)]) for n in range(6)]
    return (stream.astype(bf16), grad, *stacked, *small_outs)


def solution(mesh):
    tokens_spec = P(BOTH, None)
    in_spec, out_spec = P(None, "fsdp", "tp"), P(None, "tp", "fsdp")
    matrices = (in_spec, in_spec, in_spec, out_spec, in_spec, out_spec)
    smalls = (P(None, None, BOTH),) * 3 + (P(None, BOTH),) * 2
    return jax.shard_map(
        on_device,
        mesh=mesh,
        in_specs=(tokens_spec, tokens_spec, P("fsdp", None)) + matrices + smalls,
        out_specs=(tokens_spec, tokens_spec) + matrices + smalls,
        check_vma=False,
    )
```

time: 2290 us -> 1480 us (0.65)
  blocking collectives: 503 us -> 43.7 us
  matrix products: 479 us -> 64.6 us
  Pallas kernels: 0 us -> 116 us
  waiting for transfers between devices: 1100 us -> 985 us
  local copies, waits for them, and re-layouts: 89.1 us -> 162 us
    all_gather x13 -> x1, blocking collectives: 463 us -> 43.7 us  [on_device(): packed_all = lax.all_gather(packed, BOTH, axis=0, tiled=True)]
    dot_general x84 -> x24, matrix products: 479 us -> 64.6 us  [the longest x8 25.5 us: dot_nn(): lax.dot_general(left, right, (((1,), (0,)), ((), ())), preferred_element_...]
    reduce_scatter x18 -> x6, waiting for transfers between devices: 834 us -> 664 us  [scatter_grads(): lax.psum_scatter(parts, BOTH, scatter_dimension=0, tiled=True).astype(f32)]
    pallas_call x0 -> x8, Pallas kernels: none -> 116 us  [the longest x2 36.1 us: attend_backward(): pl.pallas_call(functools.partial(attend_backward_body, rows), grid=(width...]
    all_gather x12 -> x6, waiting for transfers between devices: 209 us -> 268 us  [gather_weights(): lax.all_gather(shard, BOTH, axis=0, tiled=False)]
    unnamed x1 -> x0, blocking collectives: 40.3 us -> none
    transpose x0 -> x17, local copies, waits for them, and re-layouts: none -> 36.8 us  [the longest x6 24.7 us: scatter_grads(): grad.reshape(tp, fsdp, rows, cols).transpose(1, 0, 2, 3).reshape(-1, cols)]
    reduce_sum x31 -> x18, other arithmetic: 51 us -> 24 us  [the longest x2 7.45 us: on_device(): grad_bias_out = jnp.sum(grad, axis=0)]
  transfers between devices with their start and end apart: 33 -> 17, of which waited for: 25 -> 13; matrix products, arithmetic and copies ran while one was open for 15% -> 14% of each run, Pallas kernels for 0% -> 2%
where the time goes in v1:
time: 1480 us; the launch traced here: 1470 us
  waiting for transfers between devices  985 us (67%)
  local copies, waits for them, and re-layouts  162 us (11%)
  Pallas kernels  116 us (8%)
  other arithmetic  68.8 us (5%)
  matrix products  64.6 us (4%)
  blocking collectives  43.7 us (3%)
  between operations  15.8 us (1%)
    reduce_scatter x6, waiting for transfers between devices, scatter_grads(): lax.psum_scatter(parts, BOTH, scatter_dimension=0, tiled=True).astype(f32)  664 us
    all_gather x6, waiting for transfers between devices, gather_weights(): lax.all_gather(shard, BOTH, axis=0, tiled=False)  268 us
    unnamed x14, waiting for transfers between devices  53.1 us
    all_gather x1, blocking collectives, on_device(): packed_all = lax.all_gather(packed, BOTH, axis=0, tiled=True)  43.7 us
    pallas_call x2, Pallas kernels, attend_backward(): pl.pallas_call(functools.partial(attend_backward_body, rows), grid=(width...  36.1 us
    pallas_call x2, Pallas kernels, feed_backward(): pl.pallas_call(feed_backward_body, grid=(parts,), in_specs=[whole_spec((r...  32.5 us
  transfers between devices with their start and end apart: 17, of which 13 were waited for; matrix products, arithmetic and copies ran while one was open for 14% of the time, Pallas kernels for 2%

profile of v1, /device:TPU:0, one launch (start us, length us, event | category | flops | bytes accessed | tf_op | source)
XLA Modules:
  0.0 1465.5 jit_solution(4359192075204129562)
XLA Ops:
  15.2 43.7 %all-gather.4 = f32[32,1,576]{2,1,0:T(1,128)S(1)} all-gather(f32[1,1,576]{2,1,0:T(1,128)S(1)} %bitcast.293), channel_id=1, replica_groups=mesh['fsdp'=8,'tp'=4] {'fsdp','tp'}, dimensions={0}, use_global_device_ids=true | all-gather | bytes 76032 | tf_op jit(solution)/shard_map/all_gather | solution.py:335
  61.4 3.2 collective-permute-start
  71.5 6.4 all-gather.16.cloned.1.call-done
  82.5 4.4 convolution_convert_fusion.1.k_ref
  88.8 3.8 add_convert_fusion.1.v_ref
  92.7 13.3 attend_forward.2
  110.2 38.0 %all-gather.12.cloned.1.call-done = bf16[32,96,768]{2,1,0:T(8,128)(2,1)} async-done(((bf16[1,96,768]{2,1,0:T(8,128)(2,1)}), bf16[32,96,768]{2,1,0:T(8,128)(2,1)}) %all-gather.12.cloned.1.call-update) | async-done | bytes 4718608 | tf_op jit(solution)/shard_map/all_gather | solution.py:292
  148.2 4.9 copy.279
  153.1 61.1 %all-gather.18.cloned.1.call-done = bf16[3072,768]{1,0:T(8,128)(2,1)} async-done(((bf16[96,768]{1,0:T(8,128)(2,1)}), bf16[3072,768]{1,0:T(8,128)(2,1)}) %all-gather.18.cloned.1.call-update) | async-done | bytes 4718608 | tf_op jit(solution)/shard_map/all_gather | solution.py:292
  214.2 4.9 copy.280
  219.1 10.3 feed_forward.2
  229.4 3.0 copy.283
  236.1 3.1 collective-permute-start.1
  240.3 40.9 %all-gather.20.cloned.1.call-done = bf16[3072,768]{1,0:T(8,128)(2,1)} async-done(((bf16[96,768]{1,0:T(8,128)(2,1)}), bf16[3072,768]{1,0:T(8,128)(2,1)}) %all-gather.20.cloned.1.call-update) | async-done | bytes 4718608 | tf_op jit(solution)/shard_map/all_gather | solution.py:292
  281.2 4.8 copy.286
  286.0 61.0 %all-gather.14.cloned.1.call-done = bf16[32,96,768]{2,1,0:T(8,128)(2,1)} async-done(((bf16[1,96,768]{2,1,0:T(8,128)(2,1)}), bf16[32,96,768]{2,1,0:T(8,128)(2,1)}) %all-gather.14.cloned.1.call-update) | async-done | bytes 4718608 | tf_op jit(solution)/shard_map/all_gather | solution.py:292
  347.0 4.8 copy.289
  351.8 61.0 %all-gather.22.cloned.1.call-done = bf16[3072,768]{1,0:T(8,128)(2,1)} async-done(((bf16[96,768]{1,0:T(8,128)(2,1)}), bf16[3072,768]{1,0:T(8,128)(2,1)}) %all-gather.22.cloned.1.call-update) | async-done | bytes 4718608 | tf_op jit(solution)/shard_map/all_gather | solution.py:292
  412.8 5.0 copy.290
  419.8 3.6 add_convert_fusion.4.q_ref
  423.4 4.1 convolution_convert_fusion.k_ref
  427.6 4.0 add_convert_fusion.v_ref
  431.6 13.6 attend_forward.3
  452.6 10.2 feed_forward.3
  462.8 16.3 %feed_backward.2 = (bf16[4,768,768]{2,1,0:T(8,128)(2,1)}, bf16[4,768,768]{2,1,0:T(8,128)(2,1)}, f32[4,1,768]{2,1,0:T(1,128)}, f32[512,768]{1,0:T(8,128)}) custom-call(bf16[512,768]{1,0:T(8,128)(2,1)} %g_ref, bf16[768,512]{1,0:T(8,128)(2,1)} %bitcast.271, bf16[768,512]{1,0:T(8,128)(2,1)} %fusion.78.nt_ref, f32[4,512,768]{2,1,0:T(8,128)} %get-tuple-element.39.pre_ref, ...), custom_call_target="tpu_custom_call" | custom-call | flops 9663676416 | bytes 25165824 | tf_op jit(solution)/shard_map/feed_backward/pallas_call | solution.py:241
  479.1 3.0 copy.296
  485.8 3.1 copy.292
  488.9 4.7 fusion.41
  495.4 17.9 %attend_backward.2 = (bf16[512,768]{1,0:T(8,128)(2,1)}, bf16[1024,768]{1,0:T(8,128)(2,1)}, bf16[1024,768]{1,0:T(8,128)(2,1)}) custom-call(s32[512,1]{1,0:T(8,128)} %copy.277.seg_q_ref, s32[1,1024]{1,0:T(1,128)} %compare_select_fusion.seg_k_ref, bf16[512,768]{1,0:T(8,128)(2,1)} %add_convert_fusion.4.q_ref, bf16[1024,768]{1,0:T(8,128)(2,1)} %convolution_convert_fusion.k_ref, ...), custom_call_target="tpu_custom_call" | custom-call | flops 12079595520 | bytes 9437184 | tf_op jit(solution)/shard_map/attend_backward/pallas_call | solution.py:146
  514.6 3.3 convolution_convert_fusion.5
  527.9 3.3 convolution_convert_fusion.4
  556.6 4.5 multiply_reduce_fusion.1
  565.8 16.2 %feed_backward.3 = (bf16[4,768,768]{2,1,0:T(8,128)(2,1)}, bf16[4,768,768]{2,1,0:T(8,128)(2,1)}, f32[4,1,768]{2,1,0:T(1,128)}, f32[512,768]{1,0:T(8,128)}) custom-call(bf16[512,768]{1,0:T(8,128)(2,1)} %copy.301.g_ref, bf16[768,512]{1,0:T(8,128)(2,1)} %convert_bitcast_fusion.gt_ref, bf16[768,512]{1,0:T(8,128)(2,1)} %fusion.77.nt_ref, ...), custom_call_target="tpu_custom_call" | custom-call | flops 9663676416 | bytes 25165824 | tf_op jit(solution)/shard_map/feed_backward/pallas_call | solution.py:241
  590.6 18.2 %attend_backward.3 = (bf16[512,768]{1,0:T(8,128)(2,1)}, bf16[1024,768]{1,0:T(8,128)(2,1)}, bf16[1024,768]{1,0:T(8,128)(2,1)}) custom-call(s32[512,1]{1,0:T(8,128)} %copy.277.seg_q_ref, s32[1,1024]{1,0:T(1,128)} %compare_select_fusion.seg_k_ref, bf16[512,768]{1,0:T(8,128)(2,1)} %add_convert_fusion.7.q_ref, bf16[1024,768]{1,0:T(8,128)(2,1)} %convolution_convert_fusion.1.k_ref, ...), custom_call_target="tpu_custom_call" | custom-call | flops 12079595520 | bytes 9437184 | tf_op jit(solution)/shard_map/attend_backward/pallas_call | solution.py:146
  648.1 5.1 fusion.12
  700.0 5.0 copy.320
  705.1 4.9 copy.319
  710.0 4.9 copy.318
  715.0 4.9 copy.317
  722.2 3.1 fusion.11
  725.3 3.0 copy.331
  728.3 51.8 %all-reduce.3.cloned.1.call-done = f32[32,576]{1,0:T(8,128)} async-done(((f32[32,576]{1,0:T(8,128)}), f32[32,576]{1,0:T(8,128)}) %all-reduce.3.cloned.1.call-update) | async-done | bytes 73744
  786.6 108.0 %reduce-scatter.9.cloned.1.call-done = bf16[96,768]{1,0:T(8,128)(2,1)} async-done(((bf16[3072,768]{1,0:T(8,128)(2,1)}), bf16[96,768]{1,0:T(8,128)(2,1)}) %reduce-scatter.9.cloned.1.call-update) | async-done | bytes 147472 | tf_op jit(solution)/shard_map/reduce_scatter | solution.py:300
  895.6 111.4 %reduce-scatter.7.cloned.1.call-done = bf16[96,768]{1,0:T(8,128)(2,1)} async-done(((bf16[3072,768]{1,0:T(8,128)(2,1)}), bf16[96,768]{1,0:T(8,128)(2,1)}) %reduce-scatter.7.cloned.1.call-update) | async-done | bytes 147472 | tf_op jit(solution)/shard_map/reduce_scatter | solution.py:300
  1008.9 109.5 %reduce-scatter.17.cloned.1.call-done = bf16[96,768]{1,0:T(8,128)(2,1)} async-done(((bf16[3072,768]{1,0:T(8,128)(2,1)}), bf16[96,768]{1,0:T(8,128)(2,1)}) %reduce-scatter.17.cloned.1.call-update) | async-done | bytes 147472 | tf_op jit(solution)/shard_map/reduce_scatter | solution.py:300
  1118.5 112.5 %reduce-scatter.15.cloned.1.call-done = bf16[96,768]{1,0:T(8,128)(2,1)} async-done(((bf16[3072,768]{1,0:T(8,128)(2,1)}), bf16[96,768]{1,0:T(8,128)(2,1)}) %reduce-scatter.15.cloned.1.call-update) | async-done | bytes 147472 | tf_op jit(solution)/shard_map/reduce_scatter | solution.py:300
  1232.8 109.6 %reduce-scatter.13.cloned.1.call-done = bf16[96,768]{1,0:T(8,128)(2,1)} async-done(((bf16[3072,768]{1,0:T(8,128)(2,1)}), bf16[96,768]{1,0:T(8,128)(2,1)}) %reduce-scatter.13.cloned.1.call-update) | async-done | bytes 147472 | tf_op jit(solution)/shard_map/reduce_scatter | solution.py:300
  1342.5 112.4 %reduce-scatter.11.cloned.1.call-done = bf16[96,768]{1,0:T(8,128)(2,1)} async-done(((bf16[3072,768]{1,0:T(8,128)(2,1)}), bf16[96,768]{1,0:T(8,128)(2,1)}) %reduce-scatter.11.cloned.1.call-update) | async-done | bytes 147472 | tf_op jit(solution)/shard_map/reduce_scatter | solution.py:300
  (495 shorter events, 199.9 us)
Async XLA Ops:
  7.2 70.7 %all-gather.16.cloned.1.call-start = ((), (), s32[]{:S(2)}) async-start(), calls=%async_computation.14 | async-start | bytes 4866048 | tf_op jit(solution)/shard_map/all_gather | solution.py:292
  10.8 137.4 %all-gather.12.cloned.1.call-start = ((), (), s32[]{:S(2)}) async-start(), calls=%async_computation.6 | async-start | bytes 4866048 | tf_op jit(solution)/shard_map/all_gather | solution.py:292
  11.6 47.9 %copy-start.46 = (bf16[512,768]{1,0:T(8,128)(2,1)S(1)}, bf16[512,768]{1,0:T(8,128)(2,1)}, u32[]{:S(2)}) copy-start(bf16[512,768]{1,0:T(8,128)(2,1)} %param.14) | copy-start | bytes 2359300
  11.6 202.5 %all-gather.18.cloned.1.call-start = ((), (), s32[]{:S(2)}) async-start(), calls=%async_computation.15 | async-start | bytes 4866048 | tf_op jit(solution)/shard_map/all_gather | solution.py:292
  12.5 268.7 %all-gather.20.cloned.1.call-start = ((), (), s32[]{:S(2)}) async-start(), calls=%async_computation.16 | async-start | bytes 4866048 | tf_op jit(solution)/shard_map/all_gather | solution.py:292
  13.4 333.6 %all-gather.14.cloned.1.call-start = ((), (), s32[]{:S(2)}) async-start(), calls=%async_computation.7 | async-start | bytes 4866048 | tf_op jit(solution)/shard_map/all_gather | solution.py:292
  14.0 398.8 %all-gather.22.cloned.1.call-start = ((), (), s32[]{:S(2)}) async-start(), calls=%async_computation.17 | async-start | bytes 4866048 | tf_op jit(solution)/shard_map/all_gather | solution.py:292
  14.6 765.6 %all-reduce.3.cloned.1.call-start = ((), (), s32[]{:S(2)}) async-start(), calls=%async_computation.18 | async-start | bytes 163840
  59.8 46.2 %copy-start.6 = (bf16[512,768]{0,1:T(8,128)(2,1)}, bf16[512,768]{0,1:T(8,128)(2,1)S(1)}, u32[]{:S(2)}) copy-start(bf16[512,768]{0,1:T(8,128)(2,1)S(1)} %copy.267) | copy-start | bytes 2359300
  61.0 7.3 copy-start.47
  61.4 27.4 %copy-start.48 = (bf16[512,768]{0,1:T(8,128)(2,1)}, bf16[512,768]{0,1:T(8,128)(2,1)S(1)}, u32[]{:S(2)}) copy-start(bf16[512,768]{0,1:T(8,128)(2,1)S(1)} %fusion.7) | copy-start | bytes 2359300
  61.4 21.1 %collective-permute-start = (bf16[512,768]{0,1:T(8,128)(2,1)S(1)}, bf16[512,768]{0,1:T(8,128)(2,1)}, u32[]{:S(2)}, u32[]{:S(2)}) collective-permute-start(bf16[512,768]{0,1:T(8,128)(2,1)S(1)} %fusion.7), channel_id=1, source_target_pairs={{0,1},{1,2},{2,3},{4,5},{5,6},{6,7},{8,9},{9,10},{10,11},{12,13},{... | collective-permute-start | bytes 2359304 | tf_op jit(solution)/shard_map/ppermute | solution.py:305
  82.4 6.4 copy-start.19
  82.5 23.6 %copy-start.65 = (bf16[768,192]{1,0:T(8,128)(2,1)}, bf16[768,192]{1,0:T(8,128)(2,1)S(1)}, u32[]{:S(2)}) copy-start(bf16[768,192]{1,0:T(8,128)(2,1)S(1)} %get-tuple-element.178) | copy-start | bytes 884740
  82.5 23.6 %copy-start.67 = (bf16[768,192]{1,0:T(8,128)(2,1)}, bf16[768,192]{1,0:T(8,128)(2,1)S(1)}, u32[]{:S(2)}) copy-start(bf16[768,192]{1,0:T(8,128)(2,1)S(1)} %get-tuple-element.179) | copy-start | bytes 884740
  82.5 23.6 %copy-start.69 = (bf16[768,192]{1,0:T(8,128)(2,1)}, bf16[768,192]{1,0:T(8,128)(2,1)S(1)}, u32[]{:S(2)}) copy-start(bf16[768,192]{1,0:T(8,128)(2,1)S(1)} %get-tuple-element.180) | copy-start | bytes 884740
  82.5 23.6 %copy-start.71 = (bf16[768,192]{1,0:T(8,128)(2,1)}, bf16[768,192]{1,0:T(8,128)(2,1)S(1)}, u32[]{:S(2)}) copy-start(bf16[768,192]{1,0:T(8,128)(2,1)S(1)} %get-tuple-element.181) | copy-start | bytes 884740
  108.3 130.8 %copy-start.96 = (f32[512]{0:T(512)}, f32[512]{0:T(512)S(1)}, u32[]{:S(2)}) copy-start(f32[512]{0:T(512)S(1)} %add_rsqrt_fusion.2) | copy-start | bytes 6148
  236.1 187.3 %collective-permute-start.1 = (bf16[512,768]{0,1:T(8,128)(2,1)}, bf16[512,768]{0,1:T(8,128)(2,1)}, u32[]{:S(2)}, u32[]{:S(2)}) collective-permute-start(bf16[512,768]{0,1:T(8,128)(2,1)} %add_convert_fusion.5), channel_id=1, source_target_pairs={{0,1},{1,2},{2,3},{4,5},{5,6},{6,7},{8,9},{9,10},{10,11},{12,13},{... | collective-permute-start | bytes 2359304 | tf_op jit(solution)/shard_map/ppermute | solution.py:305
  419.7 7.9 copy-start.25
  419.7 7.8 copy-start.27
  419.7 7.8 copy-start.29
  419.7 7.8 copy-start.31
  419.7 25.4 %copy-start.85 = (bf16[768,192]{1,0:T(8,128)(2,1)}, bf16[768,192]{1,0:T(8,128)(2,1)S(1)}, u32[]{:S(2)}) copy-start(bf16[768,192]{1,0:T(8,128)(2,1)S(1)} %get-tuple-element.162) | copy-start | bytes 884740
  419.8 25.4 %copy-start.87 = (bf16[768,192]{1,0:T(8,128)(2,1)}, bf16[768,192]{1,0:T(8,128)(2,1)S(1)}, u32[]{:S(2)}) copy-start(bf16[768,192]{1,0:T(8,128)(2,1)S(1)} %get-tuple-element.163) | copy-start | bytes 884740
  419.8 25.4 %copy-start.89 = (bf16[768,192]{1,0:T(8,128)(2,1)}, bf16[768,192]{1,0:T(8,128)(2,1)S(1)}, u32[]{:S(2)}) copy-start(bf16[768,192]{1,0:T(8,128)(2,1)S(1)} %get-tuple-element.164) | copy-start | bytes 884740
  419.8 25.4 %copy-start.91 = (bf16[768,192]{1,0:T(8,128)(2,1)}, bf16[768,192]{1,0:T(8,128)(2,1)S(1)}, u32[]{:S(2)}) copy-start(bf16[768,192]{1,0:T(8,128)(2,1)S(1)} %get-tuple-element.165) | copy-start | bytes 884740
  431.6 13.6 copy-start.2
  431.6 13.6 copy-start.118
  493.6 24.3 %copy-start.8 = (f32[512,768]{0,1:T(8,128)}, f32[512,768]{0,1:T(8,128)S(1)}, u32[]{:S(2)}) copy-start(f32[512,768]{0,1:T(8,128)S(1)} %get-tuple-element.159) | copy-start | bytes 4718596
  525.9 30.6 %collective-permute-start.2 = (bf16[512,768]{0,1:T(8,128)(2,1)}, bf16[512,768]{0,1:T(8,128)(2,1)}, u32[]{:S(2)}, u32[]{:S(2)}) collective-permute-start(bf16[512,768]{0,1:T(8,128)(2,1)} %slice.690), channel_id=1, source_target_pairs={{1,0},{2,1},{3,2},{5,4},{6,5},{7,6},{9,8},{10,9},{11,10},{13,12},{... | collective-permute-start | bytes 2359304 | tf_op jit(solution)/shard_map/ppermute | solution.py:310
  537.9 7.4 copy-start.116
  538.8 7.2 copy-start.17
  590.6 18.3 %copy-start.58 = (bf16[768,192]{1,0:T(8,128)(2,1)S(1)}, bf16[768,192]{1,0:T(8,128)(2,1)}, u32[]{:S(2)}) copy-start(bf16[768,192]{1,0:T(8,128)(2,1)} %copy-done.57) | copy-start | bytes 884740
  590.6 18.3 %copy-start.60 = (bf16[768,192]{1,0:T(8,128)(2,1)S(1)}, bf16[768,192]{1,0:T(8,128)(2,1)}, u32[]{:S(2)}) copy-start(bf16[768,192]{1,0:T(8,128)(2,1)} %copy-done.59) | copy-start | bytes 884740
  590.6 18.3 %copy-start.62 = (bf16[768,192]{1,0:T(8,128)(2,1)S(1)}, bf16[768,192]{1,0:T(8,128)(2,1)}, u32[]{:S(2)}) copy-start(bf16[768,192]{1,0:T(8,128)(2,1)} %copy-done.61) | copy-start | bytes 884740
  590.6 18.3 %copy-start.64 = (bf16[768,192]{1,0:T(8,128)(2,1)S(1)}, bf16[768,192]{1,0:T(8,128)(2,1)}, u32[]{:S(2)}) copy-start(bf16[768,192]{1,0:T(8,128)(2,1)} %copy-done.63) | copy-start | bytes 884740
  614.5 33.6 %collective-permute-start.3 = (bf16[512,768]{0,1:T(8,128)(2,1)}, bf16[512,768]{0,1:T(8,128)(2,1)}, u32[]{:S(2)}, u32[]{:S(2)}) collective-permute-start(bf16[512,768]{0,1:T(8,128)(2,1)} %slice.689), channel_id=1, source_target_pairs={{1,0},{2,1},{3,2},{5,4},{6,5},{7,6},{9,8},{10,9},{11,10},{13,12},{... | collective-permute-start | bytes 2359304 | tf_op jit(solution)/shard_map/ppermute | solution.py:310
  620.3 8.4 copy-start.95
  620.3 27.8 %copy-start.7 = (bf16[512,768]{0,1:T(8,128)(2,1)S(1)}, bf16[512,768]{0,1:T(8,128)(2,1)}, u32[]{:S(2)}) copy-start(bf16[512,768]{0,1:T(8,128)(2,1)} %copy-done.6) | copy-start | bytes 2359300
  620.3 27.8 %copy-start.50 = (bf16[512,768]{1,0:T(8,128)(2,1)S(1)}, bf16[512,768]{1,0:T(8,128)(2,1)}, u32[]{:S(2)}) copy-start(bf16[512,768]{1,0:T(8,128)(2,1)} %get-tuple-element.50) | copy-start | bytes 2359300
  620.3 27.8 %copy-start.53 = (bf16[768,192]{1,0:T(8,128)(2,1)S(1)}, bf16[768,192]{1,0:T(8,128)(2,1)}, u32[]{:S(2)}) copy-start(bf16[768,192]{1,0:T(8,128)(2,1)} %copy-done.52) | copy-start | bytes 884740
  658.1 236.5 %reduce-scatter.9.cloned.1.call-start = ((), (), s32[]{:S(2)}) async-start(), calls=%async_computation.9 | async-start | bytes 4866048 | tf_op jit(solution)/shard_map/reduce_scatter | solution.py:300
  663.3 343.7 %reduce-scatter.7.cloned.1.call-start = ((), (), s32[]{:S(2)}) async-start(), calls=%async_computation.8 | async-start | bytes 4866048 | tf_op jit(solution)/shard_map/reduce_scatter | solution.py:300
  700.0 418.5 %reduce-scatter.17.cloned.1.call-start = ((), (), s32[]{:S(2)}) async-start(), calls=%async_computation.13 | async-start | bytes 4866048 | tf_op jit(solution)/shard_map/reduce_scatter | solution.py:300
  705.0 526.0 %reduce-scatter.15.cloned.1.call-start = ((), (), s32[]{:S(2)}) async-start(), calls=%async_computation.12 | async-start | bytes 4866048 | tf_op jit(solution)/shard_map/reduce_scatter | solution.py:300
  710.0 632.5 %reduce-scatter.13.cloned.1.call-start = ((), (), s32[]{:S(2)}) async-start(), calls=%async_computation.11 | async-start | bytes 4866048 | tf_op jit(solution)/shard_map/reduce_scatter | solution.py:300
  715.0 739.9 %reduce-scatter.11.cloned.1.call-start = ((), (), s32[]{:S(2)}) async-start(), calls=%async_computation.10 | async-start | bytes 4866048 | tf_op jit(solution)/shard_map/reduce_scatter | solution.py:300
  (101 other events, 308.9 us)
Sparse Core Ops, SparseCore 0:
  11.5 66.3 all-gather.15
  81.3 66.8 all-gather.11
  151.7 62.4 all-gather.17
  217.5 63.6 all-gather.19
  284.5 62.4 all-gather.13
  350.3 62.4 all-gather.21
  658.2 121.8 all-reduce.2
  785.6 108.9 reduce-scatter.8
  901.0 106.0 reduce-scatter.6
  1012.4 106.0 reduce-scatter.16
  1124.9 106.0 reduce-scatter.14
  1236.3 106.0 reduce-scatter.12
  1348.8 106.0 reduce-scatter.10

commit v2 on v1

--- a/solution.py
+++ b/solution.py
@@ -29,6 +29,29 @@
 
 def dot_tn(left, right):
     return lax.dot_general(left, right, (((0,), (0,)), ((), ())), preferred_element_type=f32)
+
+
+def tie(value, deps):
+    deps = list(deps)
+    return pl.pallas_call(
+        lambda *refs: None,
+        in_specs=[pl.BlockSpec(memory_space=pl.ANY)] * (1 + len(deps)),
+        out_specs=pl.BlockSpec(memory_space=pl.ANY),
+        out_shape=jax.ShapeDtypeStruct(value.shape, value.dtype),
+        input_output_aliases={0: 0},
+        name="tie",
+    )(value, *deps)
+
+
+def dep_specs(deps):
+    return [pl.BlockSpec(memory_space=pl.ANY)] * len(deps)
+
+
+def skip_deps(body, inputs, count):
+    return lambda *refs: body(*refs[:inputs], *refs[inputs + count :])
+
+
+COST = pl.CostEstimate(flops=1000, bytes_accessed=1000, transcendentals=0)
 
 
 def fill_bias(seg_q_ref, seg_k_ref, bias_ref, rows):
@@ -117,15 +140,15 @@
     return pl.BlockSpec(shape, lambda *_: (0,) * len(shape))
 
 
-def attend_forward(seg_q, seg_k, queries, keys, values):
+def attend_forward(seg_q, seg_k, queries, keys, values, deps):
     rows, width = queries.shape
     return pl.pallas_call(
-        functools.partial(attend_forward_body, rows),
+        skip_deps(functools.partial(attend_forward_body, rows), 5, len(deps)),
         grid=(width // LANES,),
         in_specs=[
             whole_spec(seg_q.shape), whole_spec(seg_k.shape),
             pair_spec(rows), pair_spec(2 * rows), pair_spec(2 * rows),
-        ],
+        ] + dep_specs(deps),
         out_specs=[pair_spec(rows), pair_spec(rows)],
         out_shape=[
             jax.ShapeDtypeStruct((rows, width), bf16),
@@ -133,24 +156,21 @@
         ],
         scratch_shapes=[pltpu.VMEM((rows, rows + QROWS), f32)],
         compiler_params=pltpu.CompilerParams(vmem_limit_bytes=VMEM_BYTES),
-        cost_estimate=pl.CostEstimate(
-            flops=16 * rows * (rows + QROWS) * width, bytes_accessed=6 * rows * width * 2,
-            transcendentals=rows * rows * width // HEAD,
-        ),
+        cost_estimate=COST,
         name="attend_forward",
-    )(seg_q, seg_k, queries, keys, values)
-
-
-def attend_backward(seg_q, seg_k, queries, keys, values, attended, lse, grad_attended):
+    )(seg_q, seg_k, queries, keys, values, *deps)
+
+
+def attend_backward(seg_q, seg_k, queries, keys, values, attended, lse, grad_attended, deps):
     rows, width = queries.shape
     return pl.pallas_call(
-        functools.partial(attend_backward_body, rows),
+        skip_deps(functools.partial(attend_backward_body, rows), 8, len(deps)),
         grid=(width // LANES,),
         in_specs=[
             whole_spec(seg_q.shape), whole_spec(seg_k.shape),
             pair_spec(rows), pair_spec(2 * rows), pair_spec(2 * rows),
             pair_spec(rows), pair_spec(rows), pair_spec(rows),
-        ],
+        ] + dep_specs(deps),
         out_specs=[pair_spec(rows), pair_spec(2 * rows), pair_spec(2 * rows)],
         out_shape=[
             jax.ShapeDtypeStruct((rows, width), bf16),
@@ -163,12 +183,9 @@
             pltpu.VMEM((2 * rows, LANES), f32),
         ],
         compiler_params=pltpu.CompilerParams(vmem_limit_bytes=VMEM_BYTES),
-        cost_estimate=pl.CostEstimate(
-            flops=40 * rows * (rows + QROWS) * width, bytes_accessed=12 * rows * width * 2,
-            transcendentals=rows * rows * width // HEAD,
-        ),
+        cost_estimate=COST,
         name="attend_backward",
-    )(seg_q, seg_k, queries, keys, values, attended, lse, grad_attended)
+    )(seg_q, seg_k, queries, keys, values, attended, lse, grad_attended, *deps)
 
 
 GELU_A = 0.7978845608028654
@@ -194,73 +211,73 @@
     out_ref[...] += dot_nt(hidden, down_ref[0])
 
 
-def feed_forward(normed, up, down, bias):
+def feed_forward(normed, updown, bias, deps):
     rows, width = normed.shape
-    parts, _, cols = up.shape
-    part = pl.BlockSpec((1, width, cols), lambda t: (t, 0, 0))
+    parts, _, cols = updown.shape
+    cols = cols // 2
+    up_part = pl.BlockSpec((1, width, cols), lambda t: (t, 0, 0))
+    down_part = pl.BlockSpec((1, width, cols), lambda t: (t, 0, 1))
     return pl.pallas_call(
-        feed_forward_body,
+        skip_deps(feed_forward_body, 4, len(deps)),
         grid=(parts,),
         in_specs=[
-            whole_spec((rows, width)), part, part,
+            whole_spec((rows, width)), up_part, down_part,
             pl.BlockSpec((1, 1, cols), lambda t: (t, 0, 0)),
-        ],
+        ] + dep_specs(deps),
         out_specs=[pl.BlockSpec((1, rows, cols), lambda t: (t, 0, 0)), whole_spec((rows, width))],
         out_shape=[
             jax.ShapeDtypeStruct((parts, rows, cols), f32),
             jax.ShapeDtypeStruct((rows, width), f32),
         ],
         compiler_params=pltpu.CompilerParams(vmem_limit_bytes=VMEM_BYTES),
-        cost_estimate=pl.CostEstimate(
-            flops=4 * rows * width * cols * parts, bytes_accessed=4 * parts * width * cols + 4 * parts * rows * cols,
-            transcendentals=rows * cols * parts,
-        ),
+        cost_estimate=COST,
         name="feed_forward",
-    )(normed, up, down, bias)
+    )(normed, updown, updown, bias, *deps)
 
 
 def feed_backward_body(
-    g_ref, gt_ref, nt_ref, pre_ref, up_ref, down_ref, gup_ref, gdown_ref, gbias_ref, dn_ref
+    g_ref, gt_ref, nt_ref, pre_ref, up_ref, down_ref, gupdown_ref, gbias_ref, dn_ref
 ):
     @pl.when(pl.program_id(0) == 0)
     def _():
         dn_ref[...] = jnp.zeros_like(dn_ref)
 
     hidden, slope = gelu_parts(pre_ref[0])
-    gdown_ref[0] = dot_nn(gt_ref[...], hidden.astype(bf16)).astype(bf16)
+    cols = hidden.shape[1]
+    gupdown_ref[0, :, cols:] = dot_nn(gt_ref[...], hidden.astype(bf16)).astype(bf16)
     dpre = (dot_nn(g_ref[...], down_ref[0]) * slope).astype(bf16)
     gbias_ref[0] = jnp.sum(dpre.astype(f32), axis=0, keepdims=True)
-    gup_ref[0] = dot_nn(nt_ref[...], dpre).astype(bf16)
+    gupdown_ref[0, :, :cols] = dot_nn(nt_ref[...], dpre).astype(bf16)
     dn_ref[...] += dot_nt(dpre, up_ref[0])
 
 
-def feed_backward(grad_low, normed, pre, up, down):
-    rows, width = normed.shape
-    parts, _, cols = up.shape
-    part = pl.BlockSpec((1, width, cols), lambda t: (t, 0, 0))
+def feed_backward(grad_low, grad_low_t, normed_t, pre, updown, deps):
+    rows, width = grad_low.shape
+    parts, _, cols = updown.shape
+    cols = cols // 2
+    up_part = pl.BlockSpec((1, width, cols), lambda t: (t, 0, 0))
+    down_part = pl.BlockSpec((1, width, cols), lambda t: (t, 0, 1))
     return pl.pallas_call(
-        feed_backward_body,
+        skip_deps(feed_backward_body, 6, len(deps)),
         grid=(parts,),
         in_specs=[
             whole_spec((rows, width)), whole_spec((width, rows)), whole_spec((width, rows)),
-            pl.BlockSpec((1, rows, cols), lambda t: (t, 0, 0)), part, part,
-        ],
+            pl.BlockSpec((1, rows, cols), lambda t: (t, 0, 0)), up_part, down_part,
+        ] + dep_specs(deps),
         out_specs=[
-            part, part, pl.BlockSpec((1, 1, cols), lambda t: (t, 0, 0)), whole_spec((rows, width)),
+            pl.BlockSpec((1, width, 2 * cols), lambda t: (t, 0, 0)),
+            pl.BlockSpec((1, 1, cols), lambda t: (t, 0, 0)),
+            whole_spec((rows, width)),
         ],
         out_shape=[
-            jax.ShapeDtypeStruct((parts, width, cols), bf16),
-            jax.ShapeDtypeStruct((parts, width, cols), bf16),
+            jax.ShapeDtypeStruct((parts, width, 2 * cols), bf16),
             jax.ShapeDtypeStruct((parts, 1, cols), f32),
             jax.ShapeDtypeStruct((rows, width), f32),
         ],
         compiler_params=pltpu.CompilerParams(vmem_limit_bytes=VMEM_BYTES),
-        cost_estimate=pl.CostEstimate(
-            flops=8 * rows * width * cols * parts, bytes_accessed=8 * parts * width * cols + 4 * parts * rows * cols,
-            transcendentals=rows * cols * parts,
-        ),
+        cost_estimate=COST,
         name="feed_backward",
-    )(grad_low, grad_low.T, normed.T, pre, up, down)
+    )(grad_low, grad_low_t, normed_t, pre, updown, updown, *deps)
 
 
 def norm_stats(values):
@@ -286,18 +303,130 @@
     return back, jnp.sum(grad * unit, axis=0), jnp.sum(grad, axis=0)
 
 
-def gather_weights(shard):
-    fsdp, tp = lax.axis_size("fsdp"), lax.axis_size("tp")
-    rows, cols = shard.shape
-    whole = lax.all_gather(shard, BOTH, axis=0, tiled=False).reshape(fsdp, tp, rows, cols)
-    return whole.transpose(1, 0, 2, 3).reshape(tp, fsdp * rows, cols)
-
-
-def scatter_grads(grad):
-    fsdp, tp = lax.axis_size("fsdp"), lax.axis_size("tp")
-    rows, cols = grad.shape[1] // fsdp, grad.shape[2]
-    parts = grad.reshape(tp, fsdp, rows, cols).transpose(1, 0, 2, 3).reshape(-1, cols)
-    return lax.psum_scatter(parts, BOTH, scatter_dimension=0, tiled=True).astype(f32)
+def hop(value, axis, move):
+    count = lax.axis_size(axis)
+    return lax.ppermute(value, axis, [(i, move(i)) for i in range(count)])
+
+
+def hop_x(value):
+    return hop(value, "tp", lambda i: i ^ 2)
+
+
+def hop_core(value):
+    return hop(value, "tp", lambda i: i ^ 1)
+
+
+def hop_y(value):
+    return hop(value, "fsdp", lambda i: i ^ 1)
+
+
+def hop_z(value, step):
+    count = lax.axis_size("fsdp")
+    return hop(value, "fsdp", lambda i: (i + 2 * step) % count)
+
+
+def places():
+    fsdp_index, tp_index = lax.axis_index("fsdp"), lax.axis_index("tp")
+    return tp_index // 2, tp_index % 2, fsdp_index // 2, fsdp_index % 2
+
+
+def gather_line(shard):
+    deep = lax.axis_size("fsdp") // 2
+    z = places()[2]
+    arrived = [hop_z(shard, step) for step in range(1, deep)]
+    line = lax.dynamic_update_slice(
+        jnp.zeros((deep,) + shard.shape, shard.dtype), shard[None], (z,) + (0,) * shard.ndim
+    )
+    for step, piece in enumerate(arrived, 1):
+        line = lax.dynamic_update_slice(line, piece[None], ((z - step) % deep,) + (0,) * shard.ndim)
+    return line, arrived
+
+
+def gather_plane(line):
+    deep, rows, cols = line.shape
+    x, _, _, y = places()
+    half = cols // 2
+    by_x, by_y = hop_x(line), hop_y(line)
+    first, second = hop_x(by_y[:, :, :half]), hop_y(by_x[:, :, half:])
+    mine = jnp.zeros((2, deep, 2, rows, cols), line.dtype)
+
+    def put(whole, piece, at_x, at_y, at_col):
+        return lax.dynamic_update_slice(whole, piece[None, :, None], (at_x, 0, at_y, 0, at_col))
+
+    mine = put(mine, line, x, y, 0)
+    mine = put(mine, by_x, 1 - x, y, 0)
+    mine = put(mine, by_y, x, 1 - y, 0)
+    mine = put(mine, first, 1 - x, 1 - y, 0)
+    mine = put(mine, second, 1 - x, 1 - y, half)
+    return mine.reshape(2, deep * 2 * rows, cols), (by_x, by_y), (first, second)
+
+
+def gather_small(values):
+    deep = lax.axis_size("fsdp") // 2
+    x, core, _, y = places()
+    line = gather_line(values)[0]
+
+    def both(value, index, move, axis):
+        other = move(value)
+        pair = jnp.where(index == 0, jnp.stack([value, other]), jnp.stack([other, value]))
+        return jnp.moveaxis(pair, 0, axis)
+
+    whole = both(both(both(line, y, hop_y, 1), x, hop_x, 2), core, hop_core, 3)
+    return whole.reshape(deep * 8, values.shape[0])
+
+
+def scatter_small(values):
+    deep = lax.axis_size("fsdp") // 2
+    x, core, z, y = places()
+    left = values.reshape(deep, 2, 2, 2, -1)
+    for index, move, axis in ((core, hop_core, 3), (x, hop_x, 2), (y, hop_y, 1)):
+        left = pick(left, index, axis) + move(pick(left, 1 - index, axis))
+    arrived = [hop_z(pick(left, (z + step) % deep, 0), step) for step in range(1, deep)]
+    return sum(arrived, pick(left, z, 0))
+
+
+def add_low(left, right):
+    return (left.astype(f32) + right.astype(f32)).astype(bf16)
+
+
+def pick(value, index, axis):
+    return lax.dynamic_index_in_dim(value, index, axis, keepdims=False)
+
+
+class Scatter:
+    def __init__(self, other):
+        self.parts, self.rest = [hop_core(other)], None
+
+    def keep(self, mine):
+        deep = lax.axis_size("fsdp") // 2
+        cols = mine.shape[2]
+        self.rest = add_low(mine, self.parts[0]).reshape(2, deep, 2, -1, cols)
+        x, _, _, y = places()
+        half = cols // 2
+        self.left, self.right = self.rest[..., :half], self.rest[..., half:]
+        self.parts = [hop_x(pick(self.left, 1 - x, 0)), hop_y(pick(self.right, 1 - y, 2))]
+
+    def cross(self):
+        x, _, _, y = places()
+        self.left = add_low(pick(self.left, x, 0), self.parts[0])
+        self.right = add_low(pick(self.right, y, 2), self.parts[1])
+        self.parts = [hop_y(pick(self.left, 1 - y, 1)), hop_x(pick(self.right, 1 - x, 0))]
+
+    def along(self):
+        deep = lax.axis_size("fsdp") // 2
+        x, _, z, y = places()
+        left = add_low(pick(self.left, y, 1), self.parts[0])
+        right = add_low(pick(self.right, x, 0), self.parts[1])
+        self.line = jnp.concatenate([left, right], axis=2)
+        self.parts = [
+            hop_z(pick(self.line, (z + step) % deep, 0), step) for step in range(1, deep)
+        ]
+
+    def total(self):
+        total = pick(self.line, places()[2], 0).astype(f32)
+        for piece in self.parts:
+            total = total + piece.astype(f32)
+        return total
 
 
 def from_previous(rows):
@@ -331,8 +460,7 @@
     head_cols, hidden_cols = w_query.shape[2], w_up.shape[2]
 
     smalls = [norm_gain, norm_shift, attn_bias, up_bias, down_bias]
-    packed = jnp.concatenate([part.reshape(1, -1) for part in smalls], axis=1)
-    packed_all = lax.all_gather(packed, BOTH, axis=0, tiled=True)
+    packed_all = gather_small(jnp.concatenate([part.reshape(-1) for part in smalls]))
     wholes, at = [], 0
     for part in smalls:
         size, lead, last = part.size, part.shape[:-1], part.shape[-1]
@@ -341,14 +469,34 @@
         at += size
     gain_all, shift_all, bias_attn, bias_up, bias_down = wholes
 
-    weights = []
+    shards = []
     for layer in range(layers):
-        attn_shard = jnp.concatenate(
-            [w_query[layer], w_key[layer], w_value[layer], w_out[layer].T], axis=1
+        shards.append(
+            jnp.concatenate([w_query[layer], w_key[layer], w_value[layer], w_out[layer].T], axis=1)
         )
-        weights.append(
-            (gather_weights(attn_shard), gather_weights(w_up[layer]), gather_weights(w_down[layer].T))
-        )
+        shards.append(jnp.concatenate([w_up[layer], w_down[layer].T], axis=1))
+    lines, planes = [], []
+    for number, shard in enumerate(shards):
+        lines.append(gather_line(tie(shard, lines[-1][1]) if number else shard))
+    for number, (line, _) in enumerate(lines):
+        planes.append(gather_plane(tie(line, planes[-1][2]) if number else line))
+    weights = [(mine, hop_core(mine)) for mine, _, _ in planes]
+
+    _, core, _, _ = places()
+
+    def core_order(values, cols):
+        lead = values.shape[:-1]
+        split = values.reshape(lead + (2, 2, cols))
+        return jnp.stack([pick(split, core, -2), pick(split, 1 - core, -2)], axis=len(lead))
+
+    def part_order(values, cols):
+        split = values.reshape(2, 2, cols)
+        split = jnp.stack([pick(split, core, 0), pick(split, 1 - core, 0)], axis=1)
+        return split.reshape(-1)
+
+    bias_query = core_order(bias_attn[:, 0], head_cols).reshape(layers, width)
+    bias_value = core_order(bias_attn[:, 1], head_cols).reshape(layers, width)
+    bias_hidden = core_order(bias_up, hidden_cols)[:, :, :, None]
 
     seq_ends = jnp.cumsum(lengths[0])
     first_row = tp_index * rows
@@ -360,46 +508,74 @@
     stream = tokens.astype(f32)
     saved = []
     for layer in range(layers):
-        attn_w, up, down = weights[layer]
+        attn_w, feed_w = jnp.concatenate(weights[2 * layer], axis=0), weights[2 * layer + 1]
+        later = 2 * layer + 2
+        ahead = [[], [], []]
+        if layer + 1 < layers:
+            ahead = [lines[later][1], lines[later + 1][1], planes[later][1]]
         wq, wk, wv, wo = (
             side_by_side(attn_w[:, :, n * head_cols : (n + 1) * head_cols]) for n in range(4)
         )
         normed = norm_forward(stream, gain_all[layer, 0], shift_all[layer, 0])
         wide = jnp.concatenate([from_previous(normed), normed], axis=0)
-        queries = (dot_nn(normed, wq) + bias_attn[layer, 0]).astype(bf16)
+        queries = (dot_nn(normed, wq) + bias_query[layer]).astype(bf16)
         keys = dot_nn(wide, wk).astype(bf16)
-        values = (dot_nn(wide, wv) + bias_attn[layer, 1]).astype(bf16)
-        attended, lse = attend_forward(seg_q, seg_k, queries, keys, values)
+        values = (dot_nn(wide, wv) + bias_value[layer]).astype(bf16)
+        attended, lse = attend_forward(seg_q, seg_k, queries, keys, values, ahead[0])
+        if layer:
+            attended = tie(attended, planes[2 * layer + 1][1])
         mid = stream + dot_nt(attended, wo) + bias_attn[layer, 2]
         normed_mid = norm_forward(mid, gain_all[layer, 1], shift_all[layer, 1])
-        pre, fed = feed_forward(
-            normed_mid, up, down, bias_up[layer].reshape(tp, 1, hidden_cols)
+        pre_mine, fed_mine = feed_forward(normed_mid, feed_w[0], bias_hidden[layer, 0], ahead[1])
+        pre_other, fed_other = feed_forward(normed_mid, feed_w[1], bias_hidden[layer, 1], ahead[2])
+        saved.append(
+            (stream, wide, queries, keys, values, attended, lse, mid, normed_mid, pre_mine,
+             pre_other, wq, wk, wv, wo)
         )
-        saved.append(
-            (stream, wide, queries, keys, values, attended, lse, mid, normed_mid, pre, wq, wk, wv, wo)
-        )
-        stream = mid + fed + bias_down[layer]
+        stream = mid + fed_mine + fed_other + bias_down[layer]
 
     grad = cotangent.astype(f32)
-    shards = [None] * layers
     small_grads = [None] * layers
+    feed_sums, attn_sums = [], []
     for layer in reversed(range(layers)):
-        _, up, down = weights[layer]
-        stream_in, wide, queries, keys, values, attended, lse, mid, normed_mid, pre, wq, wk, wv, wo = (
-            saved[layer]
-        )
+        feed_w = weights[2 * layer + 1]
+        top = layer + 1 == layers
+        (stream_in, wide, queries, keys, values, attended, lse, mid, normed_mid, pre_mine, pre_other,
+         wq, wk, wv, wo) = saved[layer]
         normed = wide[rows:]
         grad_bias_down = jnp.sum(grad, axis=0)
         grad_low = grad.astype(bf16)
-        grad_up, grad_down, grad_bias_up, dn = feed_backward(grad_low, normed_mid, pre, up, down)
-        up_shard, down_shard = scatter_grads(grad_up), scatter_grads(grad_down)
+        turned = (grad_low, grad_low.T, normed_mid.T)
+        deps = [] if top else feed_sums[-1].parts
+        grad_other, grad_bias_other, dn_other = feed_backward(*turned, pre_other, feed_w[1], deps)
+        if not top:
+            feed_sums[-1].along()
+        feed_sum = Scatter(grad_other)
+        deps = [] if top else attn_sums[-1].parts
+        grad_mine, grad_bias_mine, dn_mine = feed_backward(*turned, pre_mine, feed_w[0], deps)
+        if not top:
+            attn_sums[-1].keep(attn_mine)
+        feed_sum.keep(grad_mine)
+        feed_sums.append(feed_sum)
+        dn = dn_mine + dn_other
+        grad_bias_up = jnp.stack([grad_bias_mine, grad_bias_other])
         back, gain_second, shift_second = norm_backward(mid, gain_all[layer, 1], dn)
         grad = grad + back
         grad_bias_out = jnp.sum(grad, axis=0)
         grad_low = grad.astype(bf16)
         grad_wo = dot_tn(grad_low, attended).astype(bf16)
         grad_attended = dot_nn(grad_low, wo).astype(bf16)
-        dq, dk, dv = attend_backward(seg_q, seg_k, queries, keys, values, attended, lse, grad_attended)
+        deps = [] if top else attn_sums[-1].parts + feed_sums[-2].parts
+        dq, dk, dv = attend_backward(
+            seg_q, seg_k, queries, keys, values, attended, lse, grad_attended, deps
+        )
+        if not top:
+            attn_sums[-1].cross()
+        dk = tie(dk, feed_sum.parts)
+        feed_sum.cross()
+        if not top:
+            dv = tie(dv, attn_sums[-1].parts)
+            attn_sums[-1].along()
         dn_wide = dot_nt(dk, wk) + dot_nt(dv, wv)
         dn_before = to_previous(dn_wide[:rows].astype(bf16)).astype(f32)
         grad_wq = dot_tn(normed, dq).astype(bf16)
@@ -411,20 +587,22 @@
                 for four in zip(*(apart(whole, tp) for whole in (grad_wq, grad_wk, grad_wv, grad_wo)))
             ]
         )
-        attn_shard = scatter_grads(grad_attn)
+        attn_mine = grad_attn[: tp // 2]
+        attn_sums.append(Scatter(grad_attn[tp // 2 :]))
         dn = dn_wide[rows:] + dot_nt(dq, wq) + dn_before
         back, gain_first, shift_first = norm_backward(stream_in, gain_all[layer, 0], dn)
         grad = grad + back
-        shards[layer] = tuple(attn_shard[:, n * head_cols : (n + 1) * head_cols] for n in range(3)) + (
-            attn_shard[:, 3 * head_cols :].T, up_shard, down_shard.T,
-        )
         small_grads[layer] = (
             jnp.stack([gain_first, gain_second]),
             jnp.stack([shift_first, shift_second]),
             jnp.stack(
-                [jnp.sum(dq.astype(f32), axis=0), jnp.sum(dv.astype(f32), axis=0), grad_bias_out]
+                [
+                    part_order(jnp.sum(dq.astype(f32), axis=0), head_cols),
+                    part_order(jnp.sum(dv.astype(f32), axis=0), head_cols),
+                    grad_bias_out,
+                ]
             ),
-            grad_bias_up.reshape(-1),
+            part_order(grad_bias_up, hidden_cols),
             grad_bias_down,
         )
 
@@ -434,9 +612,19 @@
         last = part.shape[-1]
         split = whole.reshape(part.shape[:-1] + (devices, last))
         pieces.append(jnp.moveaxis(split, -2, 0).reshape(devices, part.size))
-    summed = lax.psum_scatter(
-        jnp.concatenate(pieces, axis=1), BOTH, scatter_dimension=0, tiled=True
-    )
+    summed = scatter_small(jnp.concatenate(pieces, axis=1))[None]
+
+    feed_sums[-1].along()
+    attn_sums[-1].keep(attn_mine)
+    attn_sums[-1].cross()
+    attn_sums[-1].along()
+    shards = [None] * layers
+    for layer in range(layers):
+        attn_shard = attn_sums[layers - 1 - layer].total()
+        feed_shard = feed_sums[layers - 1 - layer].total()
+        shards[layer] = tuple(attn_shard[:, n * head_cols : (n + 1) * head_cols] for n in range(3)) + (
+            attn_shard[:, 3 * head_cols :].T, feed_shard[:, :hidden_cols], feed_shard[:, hidden_cols:].T,
+        )
     small_outs, at = [], 0
     for part in smalls:
         small_outs.append(summed[:, at : at + part.size].reshape(part.shape))

time: 1480 us -> 739 us (0.50)
  waiting for transfers between devices: 985 us -> 166 us
  starting transfers between devices: 9.47 us -> 98.7 us
  blocking collectives: 43.7 us -> 0 us
  local copies, waits for them, and re-layouts: 162 us -> 187 us
  Pallas kernels: 116 us -> 134 us
    reduce_scatter x6 -> x0, waiting for transfers between devices: 664 us -> none  [scatter_grads(): lax.psum_scatter(parts, BOTH, scatter_dimension=0, tiled=True).astype(f32)]
    all_gather x6 -> x0, waiting for transfers between devices: 268 us -> none  [gather_weights(): lax.all_gather(shard, BOTH, axis=0, tiled=False)]
    ppermute x0 -> x76, waiting for transfers between devices: none -> 166 us  [hop(): return lax.ppermute(value, axis, [(i, move(i)) for i in range(count)])]
    ppermute x0 -> x76, starting transfers between devices: none -> 89.6 us  [hop(): return lax.ppermute(value, axis, [(i, move(i)) for i in range(count)])]
    unnamed x14 -> x0, waiting for transfers between devices: 53.1 us -> none
    all_gather x1 -> x0, blocking collectives: 43.7 us -> none  [on_device(): packed_all = lax.all_gather(packed, BOTH, axis=0, tiled=True)]
    dynamic_update_slice x0 -> x39, local copies, waits for them, and re-layouts: none -> 39.4 us  [the longest x20 27.8 us: put(): lax.dynamic_update_slice(whole, piece[None, :, None], (at_x, 0, at_y, 0,...]
    transpose x9 -> x1, local copies, waits for them, and re-layouts: 32.9 us -> 0.02 us  [on_device(): shards.append(jnp.concatenate([w_up[layer], w_down[layer].T], axis=1))]
  transfers between devices with their start and end apart: 17 -> 80, of which waited for: 13 -> 27; matrix products, arithmetic and copies ran while one was open for 14% -> 39% of each run, Pallas kernels for 2% -> 16%
where the time goes in v2:
time: 739 us; the launch traced here: 730 us
  local copies, waits for them, and re-layouts  187 us (25%)
  waiting for transfers between devices  166 us (22%)
  Pallas kernels  134 us (18%)
  starting transfers between devices  98.7 us (13%)
  other arithmetic  77.3 us (10%)
  matrix products  63.6 us (9%)
    ppermute x76, waiting for transfers between devices, hop(): return lax.ppermute(value, axis, [(i, move(i)) for i in range(count)])  166 us
    ppermute x76, starting transfers between devices, hop(): return lax.ppermute(value, axis, [(i, move(i)) for i in range(count)])  89.6 us
    pallas_call x4, Pallas kernels, feed_backward(): pl.pallas_call(skip_deps(feed_backward_body, 6, len(deps)), grid=(parts,)...  43.6 us
    pallas_call x2, Pallas kernels, attend_backward(): pl.pallas_call(skip_deps(functools.partial(attend_backward_body, rows), 8...  35.6 us
    pallas_call x4, Pallas kernels, feed_forward(): pl.pallas_call(skip_deps(feed_forward_body, 4, len(deps)), grid=(parts,),...  28.1 us
    dynamic_update_slice x20, local copies, waits for them, and re-layouts, put(): lax.dynamic_update_slice(whole, piece[None, :, None], (at_x, 0, at_y, 0,...  27.8 us
    unnamed x450, local copies, waits for them, and re-layouts  27.2 us
    pallas_call x2, Pallas kernels, attend_forward(): pl.pallas_call(skip_deps(functools.partial(attend_forward_body, rows), 5,...  26.7 us
  transfers between devices with their start and end apart: 80, of which 27 were waited for; matrix products, arithmetic and copies ran while one was open for 39% of the time, Pallas kernels for 16%

profile of v2, /device:TPU:0, one launch (start us, length us, event | category | flops | bytes accessed | tf_op | source)
XLA Modules:
  0.0 730.1 jit_solution(8682840128833071308)
XLA Ops:
  34.6 3.3 collective-permute-start.14
  46.0 3.9 collective-permute-start.16
  59.0 10.6 %collective-permute-done.16.refs_2_ = bf16[96,1536]{1,0:T(8,128)(2,1)S(1)} collective-permute-done((bf16[96,1536]{1,0:T(8,128)(2,1)}, bf16[96,1536]{1,0:T(8,128)(2,1)S(1)}, u32[]{:S(2)}, u32[]{:S(2)}) %collective-permute-start.16) | collective-permute-done | bytes 294944 | tf_op jit(solution)/shard_map/ppermute | solution.py:308
  71.0 6.1 collective-permute-start.18
  84.1 4.4 collective-permute-done.19.refs_6_.refs_2_
  108.2 6.2 collective-permute-done.26.refs_5_
  122.5 3.9 slice_bitcast_fusion.19
  130.2 14.3 %collective-permute-done.22 = bf16[4,96,1536]{2,1,0:T(8,128)(2,1)S(1)} collective-permute-done((bf16[4,96,1536]{2,1,0:T(8,128)(2,1)}, bf16[4,96,1536]{2,1,0:T(8,128)(2,1)S(1)}, u32[]{:S(2)}, u32[]{:S(2)}) %collective-permute-start.22) | collective-permute-done | bytes 1179680 | tf_op jit(solution)/shard_map/ppermute | solution.py:308
  148.6 10.2 %collective-permute-done.23.refs_1_ = bf16[4,96,768]{2,1,0:T(8,128)(2,1)S(1)} collective-permute-done((bf16[4,96,768]{2,1,0:T(8,128)(2,1)S(1)}, bf16[4,96,768]{2,1,0:T(8,128)(2,1)S(1)}, u32[]{:S(2)}, u32[]{:S(2)}) %collective-permute-start.23) | collective-permute-done | bytes 589856 | tf_op jit(solution)/shard_map/ppermute | solution.py:308
  169.4 4.3 collective-permute-done.30.refs_5_
  179.5 3.6 add_convert_fusion.11.refs_2_
  183.2 4.1 convolution_convert_fusion.1.refs_3_
  187.3 4.1 add_convert_fusion.5.refs_4_
  192.6 13.3 %attend_forward.2 = (bf16[512,768]{1,0:T(8,128)(2,1)}, f32[512,768]{1,0:T(8,128)}) custom-call(s32[512,1]{1,0:T(8,128)} %copy.265.refs_0_, s32[1,1024]{1,0:T(1,128)} %compare_select_fusion.refs_1_, bf16[512,768]{1,0:T(8,128)(2,1)} %add_convert_fusion.11.refs_2_, bf16[1024,768]{1,0:T(8,128)(2,1)} %convolution_convert_fusion.1.refs_3_, ...), custom_call_target="tpu_custom_call" | custom-call | flops 1000 | bytes 1000 | tf_op jit(solution)/shard_map/attend_forward/pallas_call | solution.py:145
  220.4 18.4 %collective-permute-done.36.refs_2_ = bf16[4,96,1536]{2,1,0:T(8,128)(2,1)S(1)} collective-permute-done((bf16[4,96,1536]{2,1,0:T(8,128)(2,1)}, bf16[4,96,1536]{2,1,0:T(8,128)(2,1)S(1)}, u32[]{:S(2)}, u32[]{:S(2)}) %collective-permute-start.36) | collective-permute-done | bytes 1179680 | tf_op jit(solution)/shard_map/ppermute | solution.py:308
  241.7 7.1 collective-permute-done.37
  252.0 7.0 feed_forward.4
  261.0 7.0 feed_forward.5
  277.1 3.6 slice_bitcast_fusion.3
  280.7 4.3 slice_bitcast_fusion.1
  293.6 13.4 %attend_forward.3 = (bf16[512,768]{1,0:T(8,128)(2,1)}, f32[512,768]{1,0:T(8,128)}) custom-call(s32[512,1]{1,0:T(8,128)} %copy.265.refs_0_, s32[1,1024]{1,0:T(1,128)} %compare_select_fusion.refs_1_, bf16[512,768]{1,0:T(8,128)(2,1)} %add_convert_fusion.8.refs_2_, bf16[1024,768]{1,0:T(8,128)(2,1)} %convolution_convert_fusion.refs_3_, ...), custom_call_target="tpu_custom_call" | custom-call | flops 1000 | bytes 1000 | tf_op jit(solution)/shard_map/attend_forward/pallas_call | solution.py:145
  316.9 7.0 feed_forward.7
  323.9 10.6 %feed_backward.5 = (bf16[2,768,1536]{2,1,0:T(8,128)(2,1)}, f32[2,1,768]{2,1,0:T(1,128)}, f32[512,768]{1,0:T(8,128)}) custom-call(bf16[512,768]{1,0:T(8,128)(2,1)} %refs_0_.1, bf16[768,512]{1,0:T(8,128)(2,1)} %bitcast.539, bf16[768,512]{1,0:T(8,128)(2,1)} %fusion.157.refs_2_, f32[2,512,768]{2,1,0:T(8,128)} %get-tuple-element.51.refs_3_, ...), custom_call_target="tpu_custom_call" | custom-call | flops 1000 | bytes 1000 | tf_op jit(solution)/shard_map/feed_backward/pallas_call | solution.py:260
  339.9 7.0 feed_forward.6
  347.0 11.1 %feed_backward.4 = (bf16[2,768,1536]{2,1,0:T(8,128)(2,1)}, f32[2,1,768]{2,1,0:T(1,128)}, f32[512,768]{1,0:T(8,128)}) custom-call(bf16[512,768]{1,0:T(8,128)(2,1)} %refs_0_.1, bf16[768,512]{1,0:T(8,128)(2,1)} %bitcast.540, bf16[768,512]{1,0:T(8,128)(2,1)} %fusion.157.refs_2_, f32[2,512,768]{2,1,0:T(8,128)} %get-tuple-element.49.refs_3_, ...), custom_call_target="tpu_custom_call" | custom-call | flops 1000 | bytes 1000 | tf_op jit(solution)/shard_map/feed_backward/pallas_call | solution.py:260
  364.1 3.1 copy.299
  370.3 3.5 multiply_reduce_fusion
  378.2 17.9 %attend_backward.2 = (bf16[512,768]{1,0:T(8,128)(2,1)}, bf16[1024,768]{1,0:T(8,128)(2,1)}, bf16[1024,768]{1,0:T(8,128)(2,1)}) custom-call(s32[512,1]{1,0:T(8,128)} %copy.265.refs_0_, s32[1,1024]{1,0:T(1,128)} %compare_select_fusion.refs_1_, bf16[512,768]{1,0:T(8,128)(2,1)} %add_convert_fusion.8.refs_2_, bf16[1024,768]{1,0:T(8,128)(2,1)} %convolution_convert_fusion.refs_3_, ...), custom_call_target="tpu_custom_call" | custom-call | flops 1000 | bytes 1000 | tf_op jit(solution)/shard_map/attend_backward/pallas_call | solution.py:166
  415.0 3.6 add_convert_fusion.1
  425.3 3.2 fusion.88
  428.5 19.0 %collective-permute-done.41 = bf16[4,2,96,768]{3,2,0,1:T(8,128)(2,1)S(1)} collective-permute-done((bf16[4,2,96,768]{3,2,0,1:T(8,128)(2,1)S(1)}, bf16[4,2,96,768]{3,2,0,1:T(8,128)(2,1)S(1)}, u32[]{:S(2)}, u32[]{:S(2)}) %collective-permute-start.41) | collective-permute-done | bytes 1179680 | tf_op jit(solution)/shard_map/ppermute | solution.py:308
  450.7 4.2 convolution_add_fusion.1
  471.3 10.1 %collective-permute-done.46.refs_7_ = bf16[4,96,768]{2,1,0:T(8,128)(2,1)S(1)} collective-permute-done((bf16[4,96,768]{2,1,0:T(8,128)(2,1)S(1)}, bf16[4,96,768]{2,1,0:T(8,128)(2,1)S(1)}, u32[]{:S(2)}, u32[]{:S(2)}) %collective-permute-start.46) | collective-permute-done | bytes 589856 | tf_op jit(solution)/shard_map/ppermute | solution.py:308
  483.4 7.0 collective-permute-start.49
  501.0 10.8 %feed_backward.7 = (bf16[2,768,1536]{2,1,0:T(8,128)(2,1)}, f32[2,1,768]{2,1,0:T(1,128)}, f32[512,768]{1,0:T(8,128)}) custom-call(bf16[512,768]{1,0:T(8,128)(2,1)} %copy.311.refs_0_, bf16[768,512]{1,0:T(8,128)(2,1)} %convert_bitcast_fusion.refs_1_, bf16[768,512]{1,0:T(8,128)(2,1)} %fusion.156.refs_2_, f32[2,512,768]{2,1,0:T(8,128)} %get-tuple-element.61.refs_3_, ...), custom_call_target="tpu_custom_call" | custom-call | flops 1000 | bytes 1000 | tf_op jit(solution)/shard_map/feed_backward/pallas_call | solution.py:260
  519.4 11.1 %feed_backward.6 = (bf16[2,768,1536]{2,1,0:T(8,128)(2,1)}, f32[2,1,768]{2,1,0:T(1,128)}, f32[512,768]{1,0:T(8,128)}) custom-call(bf16[512,768]{1,0:T(8,128)(2,1)} %copy.311.refs_0_, bf16[768,512]{1,0:T(8,128)(2,1)} %convert_bitcast_fusion.refs_1_, bf16[768,512]{1,0:T(8,128)(2,1)} %fusion.156.refs_2_, f32[2,512,768]{2,1,0:T(8,128)} %get-tuple-element.59.refs_3_, ...), custom_call_target="tpu_custom_call" | custom-call | flops 1000 | bytes 1000 | tf_op jit(solution)/shard_map/feed_backward/pallas_call | solution.py:260
  538.8 3.1 copy.313
  548.0 3.2 convolution_convert_fusion.10.refs_7_
  561.2 17.8 %attend_backward.3 = (bf16[512,768]{1,0:T(8,128)(2,1)}, bf16[1024,768]{1,0:T(8,128)(2,1)}, bf16[1024,768]{1,0:T(8,128)(2,1)}) custom-call(s32[512,1]{1,0:T(8,128)} %copy.265.refs_0_, s32[1,1024]{1,0:T(1,128)} %compare_select_fusion.refs_1_, bf16[512,768]{1,0:T(8,128)(2,1)} %add_convert_fusion.11.refs_2_, ...), custom_call_target="tpu_custom_call" | custom-call | flops 1000 | bytes 1000 | tf_op jit(solution)/shard_map/attend_backward/pallas_call | solution.py:166
  592.5 5.1 add_convert_fusion
  602.5 3.1 fusion.90
  607.5 17.4 %collective-permute-done.53 = bf16[4,2,96,768]{3,2,0,1:T(8,128)(2,1)S(1)} collective-permute-done((bf16[4,2,96,768]{3,2,0,1:T(8,128)(2,1)S(1)}, bf16[4,2,96,768]{3,2,0,1:T(8,128)(2,1)S(1)}, u32[]{:S(2)}, u32[]{:S(2)}) %collective-permute-start.53) | collective-permute-done | bytes 1179680 | tf_op jit(solution)/shard_map/ppermute | solution.py:308
  627.2 4.3 convolution_add_fusion
  645.7 10.8 %collective-permute-done.70 = bf16[4,96,768]{2,1,0:T(8,128)(2,1)S(1)} collective-permute-done((bf16[4,96,768]{2,1,0:T(8,128)(2,1)S(1)}, bf16[4,96,768]{2,1,0:T(8,128)(2,1)S(1)}, u32[]{:S(2)}, u32[]{:S(2)}) %collective-permute-start.70) | collective-permute-done | bytes 589856 | tf_op jit(solution)/shard_map/ppermute | solution.py:308
  656.8 3.2 fusion.16
  670.6 3.2 collective-permute-done.76
  698.6 9.3 %collective-permute-done.61 = bf16[2,4,96,384]{3,2,1,0:T(8,128)(2,1)S(1)} collective-permute-done((bf16[2,4,96,384]{3,2,1,0:T(8,128)(2,1)S(1)}, bf16[2,4,96,384]{3,2,1,0:T(8,128)(2,1)S(1)}, u32[]{:S(2)}, u32[]{:S(2)}) %collective-permute-start.61) | collective-permute-done | bytes 589856 | tf_op jit(solution)/shard_map/ppermute | solution.py:308
  724.2 3.2 collective-permute-done.64
  (949 shorter events, 360.2 us)
Async XLA Ops:
  5.9 38.2 %collective-permute-start.6 = (bf16[96,768]{1,0:T(8,128)(2,1)S(1)}, bf16[96,768]{1,0:T(8,128)(2,1)S(1)}, u32[]{:S(2)}, u32[]{:S(2)}) collective-permute-start(bf16[96,768]{1,0:T(8,128)(2,1)S(1)} %get-tuple-element.168), channel_id=1, source_target_pairs={{0,8},{4,12},{8,16},{12,20},{16,24},{20,28},{24,0},{28,4},{1,9},{5... | collective-permute-start | bytes 442376 | tf_op jit(solution)/shard_map/ppermute | solution.py:308
  8.9 35.2 %collective-permute-start.7 = (bf16[96,768]{1,0:T(8,128)(2,1)S(1)}, bf16[96,768]{1,0:T(8,128)(2,1)S(1)}, u32[]{:S(2)}, u32[]{:S(2)}) collective-permute-start(bf16[96,768]{1,0:T(8,128)(2,1)S(1)} %get-tuple-element.168), channel_id=1, source_target_pairs={{0,16},{4,20},{8,24},{12,28},{16,0},{20,4},{24,8},{28,12},{1,17},{... | collective-permute-start | bytes 442376 | tf_op jit(solution)/shard_map/ppermute | solution.py:308
  18.9 25.2 %collective-permute-start.8 = (bf16[96,768]{1,0:T(8,128)(2,1)S(1)}, bf16[96,768]{1,0:T(8,128)(2,1)S(1)}, u32[]{:S(2)}, u32[]{:S(2)}) collective-permute-start(bf16[96,768]{1,0:T(8,128)(2,1)S(1)} %get-tuple-element.168), channel_id=1, source_target_pairs={{0,24},{4,28},{8,0},{12,4},{16,8},{20,12},{24,16},{28,20},{1,25},{... | collective-permute-start | bytes 442376 | tf_op jit(solution)/shard_map/ppermute | solution.py:308
  34.6 148.5 %collective-permute-start.14 = (bf16[512,768]{0,1:T(8,128)(2,1)}, bf16[512,768]{0,1:T(8,128)(2,1)}, u32[]{:S(2)}, u32[]{:S(2)}) collective-permute-start(bf16[512,768]{0,1:T(8,128)(2,1)} %fusion.11), channel_id=1, source_target_pairs={{0,1},{1,2},{2,3},{4,5},{5,6},{6,7},{8,9},{9,10},{10,11},{12,13},{... | collective-permute-start | bytes 2359304 | tf_op jit(solution)/shard_map/ppermute | solution.py:434
  46.0 23.7 %collective-permute-start.16 = (bf16[96,1536]{1,0:T(8,128)(2,1)}, bf16[96,1536]{1,0:T(8,128)(2,1)S(1)}, u32[]{:S(2)}, u32[]{:S(2)}) collective-permute-start(bf16[96,1536]{1,0:T(8,128)(2,1)} %tie.10), channel_id=1, source_target_pairs={{0,16},{4,20},{8,24},{12,28},{16,0},{20,4},{24,8},{28,12},{1,17},{... | collective-permute-start | bytes 884744 | tf_op jit(solution)/shard_map/ppermute | solution.py:308
  49.8 19.8 %collective-permute-start.17 = (bf16[96,1536]{1,0:T(8,128)(2,1)}, bf16[96,1536]{1,0:T(8,128)(2,1)S(1)}, u32[]{:S(2)}, u32[]{:S(2)}) collective-permute-start(bf16[96,1536]{1,0:T(8,128)(2,1)} %tie.10), channel_id=1, source_target_pairs={{0,24},{4,28},{8,0},{12,4},{16,8},{20,12},{24,16},{28,20},{1,25},{... | collective-permute-start | bytes 884744 | tf_op jit(solution)/shard_map/ppermute | solution.py:308
  53.9 46.2 %collective-permute-start.10 = (bf16[4,96,768]{2,1,0:T(8,128)(2,1)}, bf16[4,96,768]{2,1,0:T(8,128)(2,1)}, u32[]{:S(2)}, u32[]{:S(2)}) collective-permute-start(bf16[4,96,768]{2,1,0:T(8,128)(2,1)} %bitcast_dynamic-update-slice_fusion.32), channel_id=1, source_target_pairs={{0,4},{4,0},{8,12},{12,8},{16,20},{20,16},{24,28},{28,24},{1,5},{5... | collective-permute-start | bytes 1769480 | tf_op jit(solution)/shard_map/ppermute | solution.py:308
  84.1 17.6 %collective-permute-start.9 = (bf16[4,96,768]{2,1,0:T(8,128)(2,1)}, bf16[4,96,768]{2,1,0:T(8,128)(2,1)}, u32[]{:S(2)}, u32[]{:S(2)}) collective-permute-start(bf16[4,96,768]{2,1,0:T(8,128)(2,1)} %bitcast_dynamic-update-slice_fusion.32), channel_id=1, source_target_pairs={{0,2},{1,3},{2,0},{3,1},{4,6},{5,7},{6,4},{7,5},{8,10},{9,11},{10,... | collective-permute-start | bytes 1769480 | tf_op jit(solution)/shard_map/ppermute | solution.py:308
  89.8 16.8 %collective-permute-start.25 = (bf16[96,1536]{1,0:T(8,128)(2,1)}, bf16[96,1536]{1,0:T(8,128)(2,1)S(1)}, u32[]{:S(2)}, u32[]{:S(2)}) collective-permute-start(bf16[96,1536]{1,0:T(8,128)(2,1)} %tie.13), channel_id=1, source_target_pairs={{0,8},{4,12},{8,16},{12,20},{16,24},{20,28},{24,0},{28,4},{1,9},{5... | collective-permute-start | bytes 884744 | tf_op jit(solution)/shard_map/ppermute | solution.py:308
  92.8 21.6 %collective-permute-start.26 = (bf16[96,1536]{1,0:T(8,128)(2,1)}, bf16[96,1536]{1,0:T(8,128)(2,1)S(1)}, u32[]{:S(2)}, u32[]{:S(2)}) collective-permute-start(bf16[96,1536]{1,0:T(8,128)(2,1)} %tie.13), channel_id=1, source_target_pairs={{0,16},{4,20},{8,24},{12,28},{16,0},{20,4},{24,8},{28,12},{1,17},{... | collective-permute-start | bytes 884744 | tf_op jit(solution)/shard_map/ppermute | solution.py:308
  100.1 15.0 %collective-permute-start.27 = (bf16[96,1536]{1,0:T(8,128)(2,1)S(1)}, bf16[96,1536]{1,0:T(8,128)(2,1)S(1)}, u32[]{:S(2)}, u32[]{:S(2)}) collective-permute-start(bf16[96,1536]{1,0:T(8,128)(2,1)S(1)} %copy-done.37), channel_id=1, source_target_pairs={{0,24},{4,28},{8,0},{12,4},{16,8},{20,12},{24,16},{28,20},{1,25},{... | collective-permute-start | bytes 884744 | tf_op jit(solution)/shard_map/ppermute | solution.py:308
  116.7 27.8 %collective-permute-start.22 = (bf16[4,96,1536]{2,1,0:T(8,128)(2,1)}, bf16[4,96,1536]{2,1,0:T(8,128)(2,1)S(1)}, u32[]{:S(2)}, u32[]{:S(2)}) collective-permute-start(bf16[4,96,1536]{2,1,0:T(8,128)(2,1)} %tie.12), channel_id=1, source_target_pairs={{0,4},{4,0},{8,12},{12,8},{16,20},{20,16},{24,28},{28,24},{1,5},{5... | collective-permute-start | bytes 3538952 | tf_op jit(solution)/shard_map/ppermute | solution.py:308
  118.2 27.6 %collective-permute-start.21 = (bf16[4,96,1536]{2,1,0:T(8,128)(2,1)}, bf16[4,96,1536]{2,1,0:T(8,128)(2,1)S(1)}, u32[]{:S(2)}, u32[]{:S(2)}) collective-permute-start(bf16[4,96,1536]{2,1,0:T(8,128)(2,1)} %tie.12), channel_id=1, source_target_pairs={{0,2},{1,3},{2,0},{3,1},{4,6},{5,7},{6,4},{7,5},{8,10},{9,11},{10,... | collective-permute-start | bytes 3538952 | tf_op jit(solution)/shard_map/ppermute | solution.py:308
  122.5 54.0 %collective-permute-start.13 = (bf16[2,768,768]{2,1,0:T(8,128)(2,1)}, bf16[2,768,768]{2,1,0:T(8,128)(2,1)}, u32[]{:S(2)}, u32[]{:S(2)}) collective-permute-start(bf16[2,768,768]{2,1,0:T(8,128)(2,1)} %bitcast.28), channel_id=1, source_target_pairs={{0,1},{1,0},{2,3},{3,2},{4,5},{5,4},{6,7},{7,6},{8,9},{9,8},{10,11... | collective-permute-start | bytes 7077896 | tf_op jit(solution)/shard_map/ppermute | solution.py:308
  165.9 95.0 %collective-permute-start.28 = (bf16[2,768,1536]{2,1,0:T(8,128)(2,1)}, bf16[2,768,1536]{2,1,0:T(8,128)(2,1)}, u32[]{:S(2)}, u32[]{:S(2)}) collective-permute-start(bf16[2,768,1536]{2,1,0:T(8,128)(2,1)} %bitcast.69.refs_1_.refs_2_.refs_4_.refs_5_), channel_id=1, source_target_pairs={{0,1},{1,0},{2,3},{3,2},{4,5},{5,4},{6,7},{7,6},{8,9},{9,8},{10,11... | collective-permute-start | bytes 14155784 | tf_op jit(solution)/shard_map/ppermute | solution.py:308
  174.6 35.4 %collective-permute-start.31 = (bf16[4,96,384]{2,1,0:T(8,128)(2,1)}, bf16[4,96,384]{2,1,0:T(8,128)(2,1)S(1)}, u32[]{:S(2)}, u32[]{:S(2)}) collective-permute-start(bf16[4,96,384]{2,1,0:T(8,128)(2,1)} %slice.697), channel_id=1, source_target_pairs={{0,2},{1,3},{2,0},{3,1},{4,6},{5,7},{6,4},{7,5},{8,10},{9,11},{10,... | collective-permute-start | bytes 884744 | tf_op jit(solution)/shard_map/ppermute | solution.py:308
  191.4 18.6 %collective-permute-start.32 = (bf16[4,96,384]{2,1,0:T(8,128)(2,1)}, bf16[4,96,384]{2,1,0:T(8,128)(2,1)S(1)}, u32[]{:S(2)}, u32[]{:S(2)}) collective-permute-start(bf16[4,96,384]{2,1,0:T(8,128)(2,1)} %slice.698), channel_id=1, source_target_pairs={{0,4},{4,0},{8,12},{12,8},{16,20},{20,16},{24,28},{28,24},{1,5},{5... | collective-permute-start | bytes 884744 | tf_op jit(solution)/shard_map/ppermute | solution.py:308
  211.4 27.5 %collective-permute-start.35 = (bf16[4,96,1536]{2,1,0:T(8,128)(2,1)}, bf16[4,96,1536]{2,1,0:T(8,128)(2,1)S(1)}, u32[]{:S(2)}, u32[]{:S(2)}) collective-permute-start(bf16[4,96,1536]{2,1,0:T(8,128)(2,1)} %tie.15), channel_id=1, source_target_pairs={{0,2},{1,3},{2,0},{3,1},{4,6},{5,7},{6,4},{7,5},{8,10},{9,11},{10,... | collective-permute-start | bytes 3538952 | tf_op jit(solution)/shard_map/ppermute | solution.py:308
  212.7 26.1 %collective-permute-start.36 = (bf16[4,96,1536]{2,1,0:T(8,128)(2,1)}, bf16[4,96,1536]{2,1,0:T(8,128)(2,1)S(1)}, u32[]{:S(2)}, u32[]{:S(2)}) collective-permute-start(bf16[4,96,1536]{2,1,0:T(8,128)(2,1)} %tie.15), channel_id=1, source_target_pairs={{0,4},{4,0},{8,12},{12,8},{16,20},{20,16},{24,28},{28,24},{1,5},{5... | collective-permute-start | bytes 3538952 | tf_op jit(solution)/shard_map/ppermute | solution.py:308
  216.6 64.1 %collective-permute-start.33 = (bf16[2,768,768]{2,1,0:T(8,128)(2,1)}, bf16[2,768,768]{2,1,0:T(8,128)(2,1)}, u32[]{:S(2)}, u32[]{:S(2)}) collective-permute-start(bf16[2,768,768]{2,1,0:T(8,128)(2,1)} %bitcast.92), channel_id=1, source_target_pairs={{0,1},{1,0},{2,3},{3,2},{4,5},{5,4},{6,7},{7,6},{8,9},{9,8},{10,11... | collective-permute-start | bytes 7077896 | tf_op jit(solution)/shard_map/ppermute | solution.py:308
  250.6 66.3 %collective-permute-start.39 = (bf16[2,768,1536]{2,1,0:T(8,128)(2,1)}, bf16[2,768,1536]{2,1,0:T(8,128)(2,1)}, u32[]{:S(2)}, u32[]{:S(2)}) collective-permute-start(bf16[2,768,1536]{2,1,0:T(8,128)(2,1)} %bitcast.123.refs_1_.refs_2_.refs_4_.refs_5_), channel_id=1, source_target_pairs={{0,1},{1,0},{2,3},{3,2},{4,5},{5,4},{6,7},{7,6},{8,9},{9,8},{10,11... | collective-permute-start | bytes 14155784 | tf_op jit(solution)/shard_map/ppermute | solution.py:308
  334.5 80.4 %collective-permute-start.40 = (bf16[2,768,1536]{2,1,0:T(8,128)(2,1)}, bf16[2,768,1536]{2,1,0:T(8,128)(2,1)}, u32[]{:S(2)}, u32[]{:S(2)}) collective-permute-start(bf16[2,768,1536]{2,1,0:T(8,128)(2,1)} %get-tuple-element.56), channel_id=1, source_target_pairs={{0,1},{1,0},{2,3},{3,2},{4,5},{5,4},{6,7},{7,6},{8,9},{9,8},{10,11... | collective-permute-start | bytes 14155784 | tf_op jit(solution)/shard_map/ppermute | solution.py:308
  419.5 28.0 %collective-permute-start.41 = (bf16[4,2,96,768]{3,2,0,1:T(8,128)(2,1)S(1)}, bf16[4,2,96,768]{3,2,0,1:T(8,128)(2,1)S(1)}, u32[]{:S(2)}, u32[]{:S(2)}) collective-permute-start(bf16[4,2,96,768]{3,2,0,1:T(8,128)(2,1)S(1)} %bitcast.546), channel_id=1, source_target_pairs={{0,2},{1,3},{2,0},{3,1},{4,6},{5,7},{6,4},{7,5},{8,10},{9,11},{10,... | collective-permute-start | bytes 3538952 | tf_op jit(solution)/shard_map/ppermute | solution.py:308
  421.0 28.7 %collective-permute-start.42 = (bf16[2,4,96,768]{3,2,1,0:T(8,128)(2,1)S(1)}, bf16[2,4,96,768]{3,2,1,0:T(8,128)(2,1)}, u32[]{:S(2)}, u32[]{:S(2)}) collective-permute-start(bf16[2,4,96,768]{3,2,1,0:T(8,128)(2,1)S(1)} %dynamic-slice_bitcast_fusion.1), channel_id=1, source_target_pairs={{0,4},{4,0},{8,12},{12,8},{16,20},{20,16},{24,28},{28,24},{1,5},{5... | collective-permute-start | bytes 3538952 | tf_op jit(solution)/shard_map/ppermute | solution.py:308
  455.0 38.0 %collective-permute-start.43 = (bf16[512,768]{0,1:T(8,128)(2,1)S(1)}, bf16[512,768]{0,1:T(8,128)(2,1)S(1)}, u32[]{:S(2)}, u32[]{:S(2)}) collective-permute-start(bf16[512,768]{0,1:T(8,128)(2,1)S(1)} %slice.878), channel_id=1, source_target_pairs={{1,0},{2,1},{3,2},{5,4},{6,5},{7,6},{9,8},{10,9},{11,10},{13,12},{... | collective-permute-start | bytes 2359304 | tf_op jit(solution)/shard_map/ppermute | solution.py:439
  458.3 23.0 %collective-permute-start.46 = (bf16[4,96,768]{2,1,0:T(8,128)(2,1)S(1)}, bf16[4,96,768]{2,1,0:T(8,128)(2,1)S(1)}, u32[]{:S(2)}, u32[]{:S(2)}) collective-permute-start(bf16[4,96,768]{2,1,0:T(8,128)(2,1)S(1)} %dynamic-slice_bitcast_fusion.6), channel_id=1, source_target_pairs={{0,2},{1,3},{2,0},{3,1},{4,6},{5,7},{6,4},{7,5},{8,10},{9,11},{10,... | collective-permute-start | bytes 1769480 | tf_op jit(solution)/shard_map/ppermute | solution.py:308
  461.1 21.1 %collective-permute-start.45 = (bf16[4,96,768]{2,1,0:T(8,128)(2,1)S(1)}, bf16[4,96,768]{2,1,0:T(8,128)(2,1)S(1)}, u32[]{:S(2)}, u32[]{:S(2)}) collective-permute-start(bf16[4,96,768]{2,1,0:T(8,128)(2,1)S(1)} %dynamic-slice_bitcast_fusion.7), channel_id=1, source_target_pairs={{0,4},{4,0},{8,12},{12,8},{16,20},{20,16},{24,28},{28,24},{1,5},{5... | collective-permute-start | bytes 1769480 | tf_op jit(solution)/shard_map/ppermute | solution.py:308
  467.9 51.4 %collective-permute-start.44 = (bf16[2,768,768]{2,1,0:T(8,128)(2,1)}, bf16[2,768,768]{2,1,0:T(8,128)(2,1)}, u32[]{:S(2)}, u32[]{:S(2)}) collective-permute-start(bf16[2,768,768]{2,1,0:T(8,128)(2,1)} %pad_maximum_fusion), channel_id=1, source_target_pairs={{0,1},{1,0},{2,3},{3,2},{4,5},{5,4},{6,7},{7,6},{8,9},{9,8},{10,11... | collective-permute-start | bytes 7077896 | tf_op jit(solution)/shard_map/ppermute | solution.py:308
  483.4 33.6 %collective-permute-start.49 = (bf16[96,1536]{1,0:T(8,128)(2,1)}, bf16[96,1536]{1,0:T(8,128)(2,1)S(1)}, u32[]{:S(2)}, u32[]{:S(2)}) collective-permute-start(bf16[96,1536]{1,0:T(8,128)(2,1)} %get-tuple-element.238), channel_id=1, source_target_pairs={{0,8},{4,12},{8,16},{12,20},{16,24},{20,28},{24,0},{28,4},{1,9},{5... | collective-permute-start | bytes 884744 | tf_op jit(solution)/shard_map/ppermute | solution.py:308
  490.5 26.6 %collective-permute-start.50 = (bf16[96,1536]{1,0:T(8,128)(2,1)}, bf16[96,1536]{1,0:T(8,128)(2,1)}, u32[]{:S(2)}, u32[]{:S(2)}) collective-permute-start(bf16[96,1536]{1,0:T(8,128)(2,1)} %get-tuple-element.239), channel_id=1, source_target_pairs={{0,16},{4,20},{8,24},{12,28},{16,0},{20,4},{24,8},{28,12},{1,17},{... | collective-permute-start | bytes 884744 | tf_op jit(solution)/shard_map/ppermute | solution.py:308
  490.7 26.4 %collective-permute-start.51 = (bf16[96,1536]{1,0:T(8,128)(2,1)}, bf16[96,1536]{1,0:T(8,128)(2,1)}, u32[]{:S(2)}, u32[]{:S(2)}) collective-permute-start(bf16[96,1536]{1,0:T(8,128)(2,1)} %get-tuple-element.237), channel_id=1, source_target_pairs={{0,24},{4,28},{8,0},{12,4},{16,8},{20,12},{24,16},{28,20},{1,25},{... | collective-permute-start | bytes 884744 | tf_op jit(solution)/shard_map/ppermute | solution.py:308
  515.7 76.8 %collective-permute-start.52 = (bf16[2,768,1536]{2,1,0:T(8,128)(2,1)}, bf16[2,768,1536]{2,1,0:T(8,128)(2,1)}, u32[]{:S(2)}, u32[]{:S(2)}) collective-permute-start(bf16[2,768,1536]{2,1,0:T(8,128)(2,1)} %get-tuple-element.66), channel_id=1, source_target_pairs={{0,1},{1,0},{2,3},{3,2},{4,5},{5,4},{6,7},{7,6},{8,9},{9,8},{10,11... | collective-permute-start | bytes 14155784 | tf_op jit(solution)/shard_map/ppermute | solution.py:308
  536.5 16.1 %collective-permute-start.48 = (bf16[2,4,96,384]{3,2,1,0:T(8,128)(2,1)}, bf16[2,4,96,384]{3,2,1,0:T(8,128)(2,1)}, u32[]{:S(2)}, u32[]{:S(2)}) collective-permute-start(bf16[2,4,96,384]{3,2,1,0:T(8,128)(2,1)} %dynamic-slice_bitcast_fusion.5), channel_id=1, source_target_pairs={{0,4},{4,0},{8,12},{12,8},{16,20},{20,16},{24,28},{28,24},{1,5},{5... | collective-permute-start | bytes 1769480 | tf_op jit(solution)/shard_map/ppermute | solution.py:308
  538.8 17.5 %collective-permute-start.47 = (bf16[4,2,96,384]{3,2,0,1:T(8,128)(2,1)}, bf16[4,2,96,384]{3,2,0,1:T(8,128)(2,1)}, u32[]{:S(2)}, u32[]{:S(2)}) collective-permute-start(bf16[4,2,96,384]{3,2,0,1:T(8,128)(2,1)} %bitcast.526), channel_id=1, source_target_pairs={{0,2},{1,3},{2,0},{3,1},{4,6},{5,7},{6,4},{7,5},{8,10},{9,11},{10,... | collective-permute-start | bytes 1769480 | tf_op jit(solution)/shard_map/ppermute | solution.py:308
  554.2 30.2 %collective-permute-start.56 = (bf16[4,96,384]{2,1,0:T(8,128)(2,1)S(1)}, bf16[4,96,384]{2,1,0:T(8,128)(2,1)S(1)}, u32[]{:S(2)}, u32[]{:S(2)}) collective-permute-start(bf16[4,96,384]{2,1,0:T(8,128)(2,1)S(1)} %dynamic-slice_bitcast_fusion.10), channel_id=1, source_target_pairs={{0,2},{1,3},{2,0},{3,1},{4,6},{5,7},{6,4},{7,5},{8,10},{9,11},{10,... | collective-permute-start | bytes 884744 | tf_op jit(solution)/shard_map/ppermute | solution.py:308
  557.6 26.8 %collective-permute-start.55 = (bf16[4,96,384]{2,1,0:T(8,128)(2,1)S(1)}, bf16[4,96,384]{2,1,0:T(8,128)(2,1)S(1)}, u32[]{:S(2)}, u32[]{:S(2)}) collective-permute-start(bf16[4,96,384]{2,1,0:T(8,128)(2,1)S(1)} %dynamic-slice_bitcast_fusion.11), channel_id=1, source_target_pairs={{0,4},{4,0},{8,12},{12,8},{16,20},{20,16},{24,28},{28,24},{1,5},{5... | collective-permute-start | bytes 884744 | tf_op jit(solution)/shard_map/ppermute | solution.py:308
  588.5 18.2 %collective-permute-start.66 = (bf16[96,768]{1,0:T(8,128)(2,1)S(1)}, bf16[96,768]{1,0:T(8,128)(2,1)S(1)}, u32[]{:S(2)}, u32[]{:S(2)}) collective-permute-start(bf16[96,768]{1,0:T(8,128)(2,1)S(1)} %get-tuple-element.264), channel_id=1, source_target_pairs={{0,8},{4,12},{8,16},{12,20},{16,24},{20,28},{24,0},{28,4},{1,9},{5... | collective-permute-start | bytes 442376 | tf_op jit(solution)/shard_map/ppermute | solution.py:308
  588.5 18.1 %collective-permute-start.67 = (bf16[96,768]{1,0:T(8,128)(2,1)S(1)}, bf16[96,768]{1,0:T(8,128)(2,1)S(1)}, u32[]{:S(2)}, u32[]{:S(2)}) collective-permute-start(bf16[96,768]{1,0:T(8,128)(2,1)S(1)} %get-tuple-element.265), channel_id=1, source_target_pairs={{0,16},{4,20},{8,24},{12,28},{16,0},{20,4},{24,8},{28,12},{1,17},{... | collective-permute-start | bytes 442376 | tf_op jit(solution)/shard_map/ppermute | solution.py:308
  591.1 15.6 %collective-permute-start.68 = (bf16[96,768]{1,0:T(8,128)(2,1)S(1)}, bf16[96,768]{1,0:T(8,128)(2,1)S(1)}, u32[]{:S(2)}, u32[]{:S(2)}) collective-permute-start(bf16[96,768]{1,0:T(8,128)(2,1)S(1)} %get-tuple-element.266), channel_id=1, source_target_pairs={{0,24},{4,28},{8,0},{12,4},{16,8},{20,12},{24,16},{28,20},{1,25},{... | collective-permute-start | bytes 442376 | tf_op jit(solution)/shard_map/ppermute | solution.py:308
  598.2 26.8 %collective-permute-start.53 = (bf16[4,2,96,768]{3,2,0,1:T(8,128)(2,1)S(1)}, bf16[4,2,96,768]{3,2,0,1:T(8,128)(2,1)S(1)}, u32[]{:S(2)}, u32[]{:S(2)}) collective-permute-start(bf16[4,2,96,768]{3,2,0,1:T(8,128)(2,1)S(1)} %bitcast.545), channel_id=1, source_target_pairs={{0,2},{1,3},{2,0},{3,1},{4,6},{5,7},{6,4},{7,5},{8,10},{9,11},{10,... | collective-permute-start | bytes 3538952 | tf_op jit(solution)/shard_map/ppermute | solution.py:308
  598.4 28.8 %collective-permute-start.54 = (bf16[2,4,96,768]{3,2,1,0:T(8,128)(2,1)S(1)}, bf16[2,4,96,768]{3,2,1,0:T(8,128)(2,1)}, u32[]{:S(2)}, u32[]{:S(2)}) collective-permute-start(bf16[2,4,96,768]{3,2,1,0:T(8,128)(2,1)S(1)} %dynamic-slice_bitcast_fusion), channel_id=1, source_target_pairs={{0,4},{4,0},{8,12},{12,8},{16,20},{20,16},{24,28},{28,24},{1,5},{5... | collective-permute-start | bytes 3538952 | tf_op jit(solution)/shard_map/ppermute | solution.py:308
  631.6 25.1 %collective-permute-start.57 = (bf16[512,768]{0,1:T(8,128)(2,1)S(1)}, bf16[512,768]{0,1:T(8,128)(2,1)S(1)}, u32[]{:S(2)}, u32[]{:S(2)}) collective-permute-start(bf16[512,768]{0,1:T(8,128)(2,1)S(1)} %slice.877), channel_id=1, source_target_pairs={{1,0},{2,1},{3,2},{5,4},{6,5},{7,6},{9,8},{10,9},{11,10},{13,12},{... | collective-permute-start | bytes 2359304 | tf_op jit(solution)/shard_map/ppermute | solution.py:439
  634.7 21.9 %collective-permute-start.70 = (bf16[4,96,768]{2,1,0:T(8,128)(2,1)S(1)}, bf16[4,96,768]{2,1,0:T(8,128)(2,1)S(1)}, u32[]{:S(2)}, u32[]{:S(2)}) collective-permute-start(bf16[4,96,768]{2,1,0:T(8,128)(2,1)S(1)} %dynamic-slice_bitcast_fusion.2), channel_id=1, source_target_pairs={{0,2},{1,3},{2,0},{3,1},{4,6},{5,7},{6,4},{7,5},{8,10},{9,11},{10,... | collective-permute-start | bytes 1769480 | tf_op jit(solution)/shard_map/ppermute | solution.py:308
  636.0 28.6 %collective-permute-start.69 = (bf16[4,96,768]{2,1,0:T(8,128)(2,1)S(1)}, bf16[4,96,768]{2,1,0:T(8,128)(2,1)}, u32[]{:S(2)}, u32[]{:S(2)}) collective-permute-start(bf16[4,96,768]{2,1,0:T(8,128)(2,1)S(1)} %dynamic-slice_bitcast_fusion.3), channel_id=1, source_target_pairs={{0,4},{4,0},{8,12},{12,8},{16,20},{20,16},{24,28},{28,24},{1,5},{5... | collective-permute-start | bytes 1769480 | tf_op jit(solution)/shard_map/ppermute | solution.py:308
  643.1 44.6 %collective-permute-start.58 = (bf16[2,768,768]{1,2,0:T(8,128)(2,1)}, bf16[2,768,768]{1,2,0:T(8,128)(2,1)}, u32[]{:S(2)}, u32[]{:S(2)}) collective-permute-start(bf16[2,768,768]{1,2,0:T(8,128)(2,1)} %pad_maximum_fusion.1), channel_id=1, source_target_pairs={{0,1},{1,0},{2,3},{3,2},{4,5},{5,4},{6,7},{7,6},{8,9},{9,8},{10,11... | collective-permute-start | bytes 7077896 | tf_op jit(solution)/shard_map/ppermute | solution.py:308
  667.2 30.1 %collective-permute-start.71 = (bf16[96,1536]{1,0:T(8,128)(2,1)}, bf16[96,1536]{1,0:T(8,128)(2,1)}, u32[]{:S(2)}, u32[]{:S(2)}) collective-permute-start(bf16[96,1536]{1,0:T(8,128)(2,1)} %get-tuple-element.214), channel_id=1, source_target_pairs={{0,8},{4,12},{8,16},{12,20},{16,24},{20,28},{24,0},{28,4},{1,9},{5... | collective-permute-start | bytes 884744 | tf_op jit(solution)/shard_map/ppermute | solution.py:308
  681.3 16.0 %collective-permute-start.72 = (bf16[96,1536]{1,0:T(8,128)(2,1)}, bf16[96,1536]{1,0:T(8,128)(2,1)}, u32[]{:S(2)}, u32[]{:S(2)}) collective-permute-start(bf16[96,1536]{1,0:T(8,128)(2,1)} %get-tuple-element.215), channel_id=1, source_target_pairs={{0,16},{4,20},{8,24},{12,28},{16,0},{20,4},{24,8},{28,12},{1,17},{... | collective-permute-start | bytes 884744 | tf_op jit(solution)/shard_map/ppermute | solution.py:308
  682.5 14.8 %collective-permute-start.73 = (bf16[96,1536]{1,0:T(8,128)(2,1)}, bf16[96,1536]{1,0:T(8,128)(2,1)}, u32[]{:S(2)}, u32[]{:S(2)}) collective-permute-start(bf16[96,1536]{1,0:T(8,128)(2,1)} %get-tuple-element.216), channel_id=1, source_target_pairs={{0,24},{4,28},{8,0},{12,4},{16,8},{20,12},{24,16},{28,20},{1,25},{... | collective-permute-start | bytes 884744 | tf_op jit(solution)/shard_map/ppermute | solution.py:308
  (246 other events, 2040.8 us)

commit v3 on v2

v3 whole, which is shorter than its diff:
```python
import functools

import jax
import jax.numpy as jnp
from jax import lax
from jax.experimental import pallas as pl
from jax.experimental.pallas import tpu as pltpu
from jax.sharding import PartitionSpec as P

HEAD = 64
QROWS = 256
QROWS_FORWARD = 256
eps = 1e-05
masked_fill = -1e30
VMEM_BYTES = 56 * 1024 * 1024
BOTH = ("fsdp", "tp")

f32 = jnp.float32
bf16 = jnp.bfloat16


def dot_nn(left, right):
    return lax.dot_general(left, right, (((1,), (0,)), ((), ())), preferred_element_type=f32)


def dot_nt(left, right):
    return lax.dot_general(left, right, (((1,), (1,)), ((), ())), preferred_element_type=f32)


def dot_tn(left, right):
    return lax.dot_general(left, right, (((0,), (0,)), ((), ())), preferred_element_type=f32)


def tie(value, deps):
    deps = list(deps)
    if not deps:
        return value
    return pl.pallas_call(
        lambda *refs: None,
        in_specs=[pl.BlockSpec(memory_space=pl.ANY)] * (1 + len(deps)),
        out_specs=pl.BlockSpec(memory_space=pl.ANY),
        out_shape=jax.ShapeDtypeStruct(value.shape, value.dtype),
        input_output_aliases={0: 0},
        name="tie",
    )(value, *deps)


def dep_specs(deps):
    return [pl.BlockSpec(memory_space=pl.ANY)] * len(deps)


def skip_deps(body, inputs, count):
    return lambda *refs: body(*refs[:inputs], *refs[inputs + count :])


def cost_of(products):
    return pl.CostEstimate(flops=2 * products * 512**3, bytes_accessed=1000, transcendentals=0)


COSTS = dict(
    attend_forward=16, attend_backward=26, feed_forward=9, feed_backward=14, norm_forward=3, norm_backward=6,
    stack_small=2
)


TILE = 2 * HEAD
PROJECTED = 5 * TILE
TILE_A, TILE_B, TILE_C, TILE_D, TILE_E = (slice(n * TILE, (n + 1) * TILE) for n in range(5))
FIRST, SECOND = slice(0, TILE), slice(TILE, 2 * TILE)
HEADS_OF_PART = (
    (TILE_A, TILE_B, TILE_C, 0, 0, SECOND),
    (TILE_A, TILE_B, TILE_C, 1, 1, SECOND),
    (TILE_D, TILE_E, TILE_D, 0, 1, FIRST),
)


def fill_bias(seg_q_ref, seg_k_ref, bias_ref, rows, block):
    window = rows + block
    for first in range(0, rows, block):
        row_pos = rows + first + lax.broadcasted_iota(jnp.int32, (block, window), 0)
        col_pos = first + lax.broadcasted_iota(jnp.int32, (block, window), 1)
        same = seg_q_ref[first : first + block, :] == seg_k_ref[:, first : first + window]
        bias_ref[first : first + block, :] = jnp.where(same & (col_pos <= row_pos), 0.0, masked_fill)


def fill_bias_turned(seg_q_ref, seg_k_ref, bias_ref, rows, block):
    window = rows + block
    for first in range(0, rows, block):
        row_pos = rows + first + lax.broadcasted_iota(jnp.int32, (window, block), 1)
        col_pos = first + lax.broadcasted_iota(jnp.int32, (window, block), 0)
        same = seg_q_ref[:, first : first + block] == seg_k_ref[first : first + window, :]
        bias_ref[first // block] = jnp.where(same & (col_pos <= row_pos), 0.0, masked_fill)


def halves(block):
    low = lax.broadcasted_iota(jnp.int32, (block, TILE), 1) < HEAD
    return low, ~low


def attend_forward_body(
    rows, seg_q_ref, seg_k_ref, halo_ref, own_ref, w_ref, b_ref, acc_ref, row_ref,
    p_ref, att_ref, lse_ref, out_ref, bias_ref,
):
    window = rows + QROWS_FORWARD

    @pl.when(pl.program_id(0) == 0)
    def _():
        fill_bias(seg_q_ref, seg_k_ref, bias_ref, rows, QROWS_FORWARD)
        out_ref[...] = acc_ref[...] + row_ref[...]

    weight = w_ref[0, :, :PROJECTED]
    p_ref[0, :rows] = (dot_nn(halo_ref[...], weight) + b_ref[0]).astype(bf16)
    p_ref[0, rows:] = (dot_nn(own_ref[...], weight) + b_ref[0]).astype(bf16)
    half = halves(QROWS_FORWARD)
    for first in range(0, rows, QROWS_FORWARD):
        here = slice(first, first + QROWS_FORWARD)
        own = slice(rows + first, rows + first + QROWS_FORWARD)
        span = slice(first, first + window)
        bias = bias_ref[here, :]
        outs, lses = [], []
        for q_tile, k_tile, v_tile, q_half, _, _ in HEADS_OF_PART:
            queries = jnp.where(half[q_half], p_ref[0, own, q_tile] * jnp.asarray(HEAD**-0.5, bf16), 0)
            scores = dot_nt(queries, p_ref[0, span, k_tile]) + bias
            top = jnp.max(scores, axis=-1, keepdims=True)
            terms = jnp.exp(scores - top)
            total = jnp.sum(terms, axis=-1, keepdims=True)
            outs.append(dot_nn(terms.astype(bf16), p_ref[0, span, v_tile]) * (1.0 / total))
            lses.append(top + jnp.log(total))
        att_ref[0, here, FIRST] = jnp.where(half[0], 0.0, outs[2]).astype(bf16)
        att_ref[0, here, SECOND] = jnp.where(half[0], outs[0], outs[1]).astype(bf16)
        lse_ref[0, here, FIRST] = jnp.broadcast_to(lses[2], (QROWS_FORWARD, TILE))
        lse_ref[0, here, SECOND] = jnp.where(half[0], lses[0], lses[1])
    out_ref[...] += dot_nt(att_ref[0], w_ref[0, :, 4 * TILE :])


def attend_backward_body(
    rows, first_call, seg_q_ref, seg_k_ref, g_ref, halo_ref, own_ref, w_ref, p_ref, att_ref, lse_ref,
    acc_ref, gw_ref, gb_ref, dn_ref, low_ref, bias_ref, dp_ref,
):
    window = rows + QROWS

    @pl.when(pl.program_id(0) == 0)
    def _():
        fill_bias_turned(seg_q_ref, seg_k_ref, bias_ref, rows, QROWS)
        if first_call:
            dn_ref[...] = jnp.zeros_like(dn_ref)
        else:
            dn_ref[...] = acc_ref[...]

    dp_ref[...] = jnp.zeros_like(dp_ref)
    grads = dot_nn(g_ref[...], w_ref[0, :, 4 * TILE :]).astype(bf16)
    half = halves(QROWS)
    for first in range(0, rows, QROWS):
        here = slice(first, first + QROWS)
        own = slice(rows + first, rows + first + QROWS)
        span = slice(first, first + window)
        bias = bias_ref[first // QROWS]
        lses = [lse_ref[0, here, tile].T for tile in (FIRST, SECOND)]
        products = [
            (grads[here, tile].astype(f32) * att_ref[0, here, tile].astype(f32)).T
            for tile in (FIRST, SECOND)
        ]
        dqs = []
        for head, (q_tile, k_tile, v_tile, q_half, v_half, a_tile) in enumerate(HEADS_OF_PART):
            queries = jnp.where(half[q_half], p_ref[0, own, q_tile] * jnp.asarray(HEAD**-0.5, bf16), 0)
            keys = p_ref[0, span, k_tile]
            grad = jnp.where(half[v_half], grads[here, a_tile], 0)
            which = 0 if a_tile == FIRST else 1
            lanes = slice(v_half * HEAD, v_half * HEAD + HEAD)
            inner = jnp.sum(products[which][lanes], axis=0, keepdims=True)
            lse = lses[which][v_half * HEAD : v_half * HEAD + 1]
            probs = jnp.exp(dot_nt(keys, queries) + bias - lse)
            draw = (probs * (dot_nt(p_ref[0, span, v_tile], grad) - inner)).astype(bf16)
            dp_ref[span, v_tile] += dot_nn(probs.astype(bf16), grad)
            dp_ref[span, k_tile] += dot_nn(draw, queries)
            dqs.append(dot_tn(draw, keys))
        dp_ref[own, TILE_A] = jnp.where(half[0], dqs[0], dqs[1]) * HEAD**-0.5
        dp_ref[own, TILE_D] += jnp.where(half[0], dqs[2], 0.0) * HEAD**-0.5
    dp = dp_ref[...].astype(bf16)
    gb_ref[0, :, :PROJECTED] = jnp.sum(dp.astype(f32), axis=0, keepdims=True)
    gb_ref[0, :, PROJECTED:] = jnp.zeros((1, gb_ref.shape[2] - PROJECTED), f32)
    halo_dp, own_dp = dp[:rows], dp[rows:]
    by_rows = dot_tn(halo_ref[...], halo_dp) + dot_tn(own_ref[...], own_dp)
    shared = dot_tn(g_ref[...], att_ref[0])
    gw_ref[0, :, : 4 * TILE] = by_rows[:, : 4 * TILE].astype(bf16)
    gw_ref[0, :, TILE_E] = (by_rows[:, TILE_E] + shared[:, FIRST]).astype(bf16)
    gw_ref[0, :, 5 * TILE :] = shared[:, SECOND].astype(bf16)
    dn_ref[...] += dot_nt(dp, w_ref[0, :, :PROJECTED])

    @pl.when(pl.program_id(0) == pl.num_programs(0) - 1)
    def _():
        low_ref[...] = dn_ref[:rows].astype(bf16)


def whole_spec(shape):
    return pl.BlockSpec(shape, lambda *_: (0,) * len(shape))


def part_spec(shape):
    return pl.BlockSpec((1,) + shape, lambda t: (t, 0, 0))


def call_parts(body, parts, ins, outs, scratch, name, operands, deps):
    deps = list(deps)
    in_specs = [
        part_spec(value.shape[1:]) if split else whole_spec(value.shape)
        for value, split in zip(operands, ins)
    ]
    return pl.pallas_call(
        skip_deps(body, len(operands), len(deps)),
        grid=(parts,),
        in_specs=in_specs + dep_specs(deps),
        out_specs=[part_spec(shape[1:]) if split else whole_spec(shape) for shape, _, split in outs],
        out_shape=[jax.ShapeDtypeStruct(shape, dtype) for shape, dtype, _ in outs],
        scratch_shapes=scratch,
        compiler_params=pltpu.CompilerParams(vmem_limit_bytes=VMEM_BYTES),
        cost_estimate=cost_of(COSTS[name]),
        name=name,
    )(*operands, *deps)


def attend_forward(seg_q, seg_k, halo, own, weight, bias, acc, row, deps=()):
    parts, width, _ = weight.shape
    rows = own.shape[0]
    return call_parts(
        functools.partial(attend_forward_body, rows),
        parts,
        (False, False, False, False, True, True, False, False),
        [
            ((parts, 2 * rows, PROJECTED), bf16, True),
            ((parts, rows, 2 * TILE), bf16, True),
            ((parts, rows, 2 * TILE), f32, True),
            ((rows, width), f32, False),
        ],
        [pltpu.VMEM((rows, rows + QROWS_FORWARD), f32)],
        "attend_forward",
        (seg_q, seg_k, halo, own, weight, bias, acc, row),
        deps,
    )


def attend_backward(seg_q, seg_k, grad, halo, own, weight, projected, attended, lse, acc, deps=()):
    parts, width, cols = weight.shape
    rows = grad.shape[0]
    first_call = acc is None
    return call_parts(
        functools.partial(attend_backward_body, rows, first_call),
        parts,
        (False, False, False, False, False, True, True, True, True, False),
        [
            ((parts, width, cols), bf16, True),
            ((parts, 1, cols), f32, True),
            ((2 * rows, width), f32, False),
            ((rows, width), bf16, False),
        ],
        [
            pltpu.VMEM((rows // QROWS, rows + QROWS, QROWS), f32),
            pltpu.VMEM((2 * rows, PROJECTED), f32),
        ],
        "attend_backward",
        (seg_q, seg_k, grad, halo, own, weight, projected, attended, lse, seg_q if first_call else acc),
        deps,
    )


GELU_A = 0.7978845608028654
GELU_B = 0.044715


def gelu_parts(pre):
    square = pre * pre
    bend = jnp.tanh(GELU_A * pre * (1.0 + GELU_B * square))
    half = 0.5 * (1.0 + bend)
    slope = half + 0.5 * pre * (1.0 - bend * bend) * (GELU_A * (1.0 + 3.0 * GELU_B * square))
    return pre * half, slope


def feed_forward_body(n_ref, w_ref, bias_ref, acc_ref, row_ref, pre_ref, out_ref):
    @pl.when(pl.program_id(0) == 0)
    def _():
        out_ref[...] = acc_ref[...] + row_ref[...]

    cols = pre_ref.shape[2]
    pre = dot_nn(n_ref[...], w_ref[0, :, :cols]) + bias_ref[0]
    pre_ref[0] = pre
    hidden = gelu_parts(pre)[0].astype(bf16)
    out_ref[...] += dot_nt(hidden, w_ref[0, :, cols:])


def feed_forward(normed, weight, bias, acc, row, deps=()):
    rows, width = normed.shape
    parts, _, cols = weight.shape
    return call_parts(
        feed_forward_body,
        parts,
        (False, True, True, False, False),
        [((parts, rows, cols // 2), f32, True), ((rows, width), f32, False)],
        [],
        "feed_forward",
        (normed, weight, bias, acc, row),
        deps,
    )


def feed_backward_body(first_call, g_ref, n_ref, pre_ref, w_ref, acc_ref, gw_ref, gbias_ref, dn_ref):
    @pl.when(pl.program_id(0) == 0)
    def _():
        if first_call:
            dn_ref[...] = jnp.zeros_like(dn_ref)
        else:
            dn_ref[...] = acc_ref[...]

    hidden, slope = gelu_parts(pre_ref[0])
    cols = hidden.shape[1]
    gw_ref[0, :, cols:] = dot_tn(g_ref[...], hidden.astype(bf16)).astype(bf16)
    dpre = (dot_nn(g_ref[...], w_ref[0, :, cols:]) * slope).astype(bf16)
    gbias_ref[0] = jnp.sum(dpre.astype(f32), axis=0, keepdims=True)
    gw_ref[0, :, :cols] = dot_tn(n_ref[...], dpre).astype(bf16)
    dn_ref[...] += dot_nt(dpre, w_ref[0, :, :cols])


def feed_backward(grad, normed, pre, weight, acc, deps=()):
    rows, width = normed.shape
    parts, _, cols = weight.shape
    first_call = acc is None
    return call_parts(
        functools.partial(feed_backward_body, first_call),
        parts,
        (False, False, True, True, False),
        [
            ((parts, width, cols), bf16, True),
            ((parts, 1, cols // 2), f32, True),
            ((rows, width), f32, False),
        ],
        [],
        "feed_backward",
        (grad, normed, pre, weight, normed if first_call else acc),
        deps,
    )


def norm_stats(values):
    mean = jnp.mean(values, axis=-1, keepdims=True)
    centred = values - mean
    var = jnp.mean(centred * centred, axis=-1, keepdims=True)
    scale = lax.rsqrt(var + eps)
    return centred * scale, scale


def norm_forward_body(x_ref, gain_ref, shift_ref, out_ref):
    out_ref[...] = (norm_stats(x_ref[...])[0] * gain_ref[...] + shift_ref[...]).astype(bf16)


def call_whole(body, outs, name, operands, deps=()):
    deps = list(deps)
    return pl.pallas_call(
        skip_deps(body, len(operands), len(deps)),
        in_specs=[pl.BlockSpec(memory_space=pltpu.VMEM)] * len(operands) + dep_specs(deps),
        out_specs=[pl.BlockSpec(memory_space=pltpu.VMEM)] * len(outs),
        out_shape=[jax.ShapeDtypeStruct(shape, dtype) for shape, dtype in outs],
        compiler_params=pltpu.CompilerParams(vmem_limit_bytes=VMEM_BYTES),
        cost_estimate=cost_of(COSTS[name]),
        name=name,
    )(*operands, *deps)


def norm_forward(values, gain, shift):
    return call_whole(
        norm_forward_body, [(values.shape, bf16)], "norm_forward", (values, gain[None], shift[None])
    )[0]


def norm_backward_body(x_ref, gain_ref, dn_ref, more_ref, g_ref, out_ref, low_ref, sums_ref):
    unit, scale = norm_stats(x_ref[...])
    rows = x_ref.shape[0]
    grad = dn_ref[dn_ref.shape[0] - rows :, :]
    if more_ref is not None:
        grad = grad + more_ref[...].astype(f32)
    inner = grad * gain_ref[...]
    back = scale * (
        inner
        - jnp.mean(inner, axis=-1, keepdims=True)
        - unit * jnp.mean(inner * unit, axis=-1, keepdims=True)
    )
    total = g_ref[...] + back
    out_ref[...] = total
    low_ref[...] = total.astype(bf16)
    sums_ref[0:1] = jnp.sum(grad * unit, axis=0, keepdims=True)
    sums_ref[1:2] = jnp.sum(grad, axis=0, keepdims=True)
    sums_ref[2:3] = jnp.sum(total, axis=0, keepdims=True)


def norm_backward(values, gain, dn, more, grad, deps=()):
    rows, width = values.shape
    outs = [((rows, width), f32), ((rows, width), bf16), ((3, width), f32)]
    if more is None:
        return call_whole(
            lambda x, gain, dn, *rest: norm_backward_body(x, gain, dn, None, *rest),
            outs, "norm_backward", (values, gain[None], dn, grad), deps,
        )
    return call_whole(norm_backward_body, outs, "norm_backward", (values, gain[None], dn, more, grad), deps)


def stack_small_body(core_ref, *refs):
    *row_refs, out_ref = refs
    out_ref[...] = jnp.zeros_like(out_ref)
    first = core_ref[...] == 0
    out_ref[0:1] = row_refs[0][...]
    at = 1
    for start in range(1, len(row_refs), 6):
        proj_mine, proj_other, up_mine, up_other, mid, before = row_refs[start : start + 6]
        for mine, other in ((proj_mine, proj_other), (up_mine, up_other)):
            for part in range(2):
                out_ref[at + part : at + part + 1] = jnp.where(first, mine[part], other[part])
                out_ref[at + 2 + part : at + 3 + part] = jnp.where(first, other[part], mine[part])
            at += 4
        out_ref[at : at + 3] = mid[...]
        out_ref[at + 3 : at + 6] = before[...]
        at += 6


def stack_small(core, rows):
    count = 1 + 14 * (len(rows) // 6)
    shape = (-(-count // 8) * 8, rows[0].shape[1])
    return call_whole(stack_small_body, [(shape, f32)], "stack_small", (core.reshape(1, 1), *rows))[0]


def hop(value, axis, move):
    count = lax.axis_size(axis)
    return lax.ppermute(value, axis, [(i, move(i)) for i in range(count)])


def hop_x(value):
    return hop(value, "tp", lambda i: i ^ 2)


def hop_core(value):
    return hop(value, "tp", lambda i: i ^ 1)


def hop_y(value):
    return hop(value, "fsdp", lambda i: i ^ 1)


def hop_z(value, step):
    count = lax.axis_size("fsdp")
    return hop(value, "fsdp", lambda i: (i + 2 * step) % count)


def places():
    fsdp_index, tp_index = lax.axis_index("fsdp"), lax.axis_index("tp")
    return tp_index // 2, tp_index % 2, fsdp_index // 2, fsdp_index % 2


def gather_line(shard):
    deep = lax.axis_size("fsdp") // 2
    z = places()[2]
    arrived = [hop_z(shard, step) for step in range(1, deep)]
    line = lax.dynamic_update_slice(
        jnp.zeros((deep,) + shard.shape, shard.dtype), shard[None], (z,) + (0,) * shard.ndim
    )
    for step, piece in enumerate(arrived, 1):
        line = lax.dynamic_update_slice(line, piece[None], ((z - step) % deep,) + (0,) * shard.ndim)
    return line, arrived


class Gather:
    def __init__(self, shard, after=()):
        self.line, self.parts = gather_line(tie(shard, after))

    def cross(self, after=()):
        self.line = tie(self.line, after)
        self.parts = [hop_x(self.line), hop_y(self.line)]

    def relay(self, after=()):
        half = self.line.shape[2] // 2
        self.by_x, self.by_y = (tie(part, after) for part in self.parts)
        self.parts = [hop_x(self.by_y[:, :, :half]), hop_y(self.by_x[:, :, half:])]

    def both_cores(self):
        deep, rows, cols = self.line.shape
        x, _, _, y = places()
        mine = jnp.zeros((2, deep, 2, rows, cols), self.line.dtype)
        for piece, at_x, at_y, at_col in (
            (self.line, x, y, 0),
            (self.by_x, 1 - x, y, 0),
            (self.by_y, x, 1 - y, 0),
            (self.parts[0], 1 - x, 1 - y, 0),
            (self.parts[1], 1 - x, 1 - y, cols // 2),
        ):
            mine = lax.dynamic_update_slice(mine, piece[None, :, None], (at_x, 0, at_y, 0, at_col))
        mine = mine.reshape(2, deep * 2 * rows, cols)
        return mine, hop_core(mine)


def gather_small(values):
    deep = lax.axis_size("fsdp") // 2
    x, core, _, y = places()
    line = gather_line(values)[0]

    def both(value, index, move, axis):
        other = move(value)
        pair = jnp.where(index == 0, jnp.stack([value, other]), jnp.stack([other, value]))
        return jnp.moveaxis(pair, 0, axis)

    whole = both(both(both(line, y, hop_y, 1), x, hop_x, 2), core, hop_core, 3)
    return whole.reshape(deep * 8, values.shape[0])


def sum_small(values):
    deep = lax.axis_size("fsdp") // 2
    for move in (hop_core, hop_x, hop_y):
        values = values + move(values)
    return sum((hop_z(values, step) for step in range(1, deep)), values)


def add_low(*values):
    return sum(value.astype(f32) for value in values).astype(bf16)


def pick(value, index, axis):
    return lax.dynamic_index_in_dim(value, index, axis, keepdims=False)


class Scatter:
    def __init__(self, other):
        self.parts = [hop_core(other)]

    def keep(self, mine):
        deep = lax.axis_size("fsdp") // 2
        x, _, _, y = places()
        cols = mine.shape[2]
        half = cols // 2
        both = [part.reshape(2, deep, 2, -1, cols) for part in (mine, self.parts[0])]
        self.left, self.right = [part[..., :half] for part in both], [part[..., half:] for part in both]
        self.sends = [
            add_low(*(pick(part, 1 - x, 0) for part in self.left)),
            add_low(*(pick(part, 1 - y, 2) for part in self.right)),
        ]
        self.parts = [hop_x(self.sends[0]), hop_y(self.sends[1])]

    def cross(self, after=()):
        x, _, _, y = places()
        by_x, by_y = (tie(part, after) for part in self.parts)
        self.left = add_low(*(pick(part, x, 0) for part in self.left), by_x)
        self.right = add_low(*(pick(part, y, 2) for part in self.right), by_y)
        self.parts = [hop_y(pick(self.left, 1 - y, 1)), hop_x(pick(self.right, 1 - x, 0))]

    def along(self, after=()):
        deep = lax.axis_size("fsdp") // 2
        x, _, z, y = places()
        by_y, by_x = (tie(part, after) for part in self.parts)
        left = add_low(pick(self.left, y, 1), by_y)
        right = add_low(pick(self.right, x, 0), by_x)
        self.line = jnp.concatenate([left, right], axis=2)
        self.parts = [
            hop_z(pick(self.line, (z + step) % deep, 0), step) for step in range(1, deep)
        ]

    def total(self, after=()):
        total = pick(self.line, places()[2], 0).astype(f32)
        for piece in (tie(part, after) for part in self.parts):
            total = total + piece.astype(f32)
        return total


def from_previous(rows):
    tp = lax.axis_size("tp")
    return lax.ppermute(rows, "tp", [(i, i + 1) for i in range(tp - 1)])


def to_previous(rows):
    tp = lax.axis_size("tp")
    return lax.ppermute(rows, "tp", [(i + 1, i) for i in range(tp - 1)])


def on_device(
    tokens, cotangent, lengths, w_query, w_key, w_value, w_out, w_up, w_down,
    norm_gain, norm_shift, attn_bias, up_bias, down_bias,
):
    fsdp, tp = lax.axis_size("fsdp"), lax.axis_size("tp")
    devices = fsdp * tp
    tp_index = lax.axis_index("tp")
    rows, width = tokens.shape
    layers = w_query.shape[0]
    head_cols, hidden_cols = w_query.shape[2], w_up.shape[2]

    def attn_columns(q, k, v, out):
        tiles = [q[:, :TILE], k[:, :TILE], v[:, :TILE], q[:, TILE:], v[:, TILE:], k[:, TILE:]]
        return jnp.concatenate(tiles + [out[:, TILE:], out[:, :TILE]], axis=1)

    def apart(value):
        at = [0, TILE, 2 * TILE, 3 * TILE, 3 * TILE + HEAD, 4 * TILE, 4 * TILE + HEAD, 5 * TILE]
        q, k, v, q2, v2, k2, out2, out = (
            value[:, start:end] for start, end in zip(at, at[1:] + [6 * TILE])
        )
        return [jnp.concatenate(two, axis=1) for two in ((q, q2), (k, k2), (v, v2), (out, out2))]

    shards = []
    for layer in range(layers):
        shards.append(attn_columns(w_query[layer], w_key[layer], w_value[layer], w_out[layer].T))
        shards.append(jnp.concatenate([w_up[layer], w_down[layer].T], axis=1))
    attn = Gather(shards[0])

    smalls = [norm_gain, norm_shift, attn_bias, up_bias, down_bias]
    packed = jnp.concatenate([part.reshape(-1) for part in smalls])
    packed_all = gather_small(tie(packed, attn.parts))
    wholes, at = [], 0
    for part in smalls:
        size, lead, last = part.size, part.shape[:-1], part.shape[-1]
        piece = packed_all[:, at : at + size].reshape((devices,) + part.shape)
        wholes.append(jnp.moveaxis(piece, 0, -2).reshape(lead + (devices * last,)))
        at += size
    gain_all, shift_all, bias_attn, bias_up, bias_down = wholes

    _, core, _, _ = places()

    def core_order(values, cols):
        lead = values.shape[:-1]
        split = values.reshape(lead + (2, 2, cols))
        return jnp.stack([pick(split, core, -2), pick(split, 1 - core, -2)], axis=len(lead))

    def part_order(values, cols):
        split = values.reshape(2, 2, cols)
        split = jnp.stack([pick(split, core, 0), pick(split, 1 - core, 0)], axis=1)
        return split.reshape(-1)

    bias_q = core_order(bias_attn[:, 0], head_cols)
    bias_v = core_order(bias_attn[:, 1], head_cols)
    none = jnp.zeros(bias_q.shape[:-1] + (TILE,), f32)
    bias_proj = jnp.concatenate(
        [bias_q[..., :TILE], none, bias_v[..., :TILE], bias_q[..., TILE:], bias_v[..., TILE:], none],
        axis=-1,
    )[:, :, :, None]
    bias_hidden = core_order(bias_up, hidden_cols)[:, :, :, None]
    no_row = jnp.zeros((1, width), f32)

    seq_ends = jnp.cumsum(lengths[0])
    first_row = tp_index * rows
    key_ids = first_row - rows + jnp.arange(2 * rows, dtype=jnp.int32)
    segments = jnp.sum((key_ids[:, None] >= seq_ends[None, :]).astype(jnp.int32), axis=1)
    segments = jnp.where(key_ids >= 0, segments, -1)
    seg_q, seg_k = segments[rows:, None], segments[None, :]
    turned_q, turned_k = segments[None, rows:], segments[:, None]

    stream = tokens.astype(f32)
    saved, weights = [], []
    feed = Gather(shards[1], attn.parts)
    attn.cross()
    attn.relay()
    feed.cross(attn.parts)
    for layer in range(layers):
        more = layer + 1 < layers
        if more:
            next_attn = Gather(shards[2 * layer + 2], feed.parts + attn.parts)
        normed = norm_forward(stream, gain_all[layer, 0], shift_all[layer, 0])
        halo = from_previous(normed)
        attn_w = attn.both_cores()
        *kept_mine, mid = attend_forward(
            seg_q, seg_k, halo, normed, attn_w[0], bias_proj[layer, 0], stream, bias_attn[layer, 2][None],
            [feed.line],
        )
        *kept_other, mid = attend_forward(
            seg_q, seg_k, halo, normed, attn_w[1], bias_proj[layer, 1], mid, no_row
        )
        feed.relay([mid])
        if more:
            next_feed = Gather(shards[2 * layer + 3], next_attn.parts + [mid])
            next_attn.cross(feed.parts)
        normed_mid = norm_forward(mid, gain_all[layer, 1], shift_all[layer, 1])
        feed_w = feed.both_cores()
        pre_mine, fed = feed_forward(
            normed_mid, feed_w[0], bias_hidden[layer, 0], mid, bias_down[layer][None]
        )
        crossed = []
        if more:
            crossed = next_attn.parts
            next_attn.relay([fed])
            next_feed.cross(next_attn.parts)
        pre_other, fed = feed_forward(
            normed_mid, feed_w[1], bias_hidden[layer, 1], fed, no_row, crossed
        )
        saved.append((stream, halo, normed, kept_mine, kept_other, mid, normed_mid, pre_mine, pre_other))
        weights += [attn_w, feed_w]
        stream = fed
        if more:
            attn, feed = next_attn, next_feed

    grad = cotangent.astype(f32)
    grad_low = cotangent
    small_rows = [jnp.sum(grad, axis=0, keepdims=True)]
    feed_sums, attn_sums = [], []
    for layer in reversed(range(layers)):
        attn_w, feed_w = weights[2 * layer], weights[2 * layer + 1]
        stream_in, halo, normed, kept_mine, kept_other, mid, normed_mid, pre_mine, pre_other = saved[layer]
        before_feed, before_attn = (feed_sums[-1], attn_sums[-1]) if feed_sums else (None, None)
        feed_other, up_other, dn = feed_backward(grad_low, normed_mid, pre_other, feed_w[1], None)
        feed_sum = Scatter(feed_other)
        if before_attn:
            crossed = before_attn.parts
            before_attn.cross([dn])
        feed_mine, up_mine, dn = feed_backward(
            grad_low, normed_mid, pre_mine, feed_w[0], dn,
            before_feed.parts + crossed if before_feed else (),
        )
        relayed = []
        if before_attn:
            relayed = before_attn.parts
            before_attn.along([dn])
        feed_sum.keep(feed_mine)
        grad, grad_low, sums_mid = norm_backward(
            mid, gain_all[layer, 1], dn, None, grad, feed_sum.sends
        )
        attn_other, proj_other, dn, _ = attend_backward(
            turned_q, turned_k, grad_low, halo, normed, attn_w[1], *kept_other, None, relayed
        )
        attn_sum = Scatter(attn_other)
        crossed = feed_sum.parts
        feed_sum.cross([dn])
        attn_mine, proj_mine, dn, dn_halo = attend_backward(
            turned_q, turned_k, grad_low, halo, normed, attn_w[0], *kept_mine, dn,
            crossed + (before_attn.parts if before_attn else []),
        )
        relayed = feed_sum.parts
        feed_sum.along([dn])
        attn_sum.keep(attn_mine)
        grad, grad_low, sums_in = norm_backward(
            stream_in, gain_all[layer, 0], dn, to_previous(dn_halo), grad,
            attn_sum.sends + [feed_sum.line],
        )
        feed_sums.append(feed_sum)
        attn_sums.append(attn_sum)
        small_rows += [proj_mine, proj_other, up_mine, up_other, sums_mid, sums_in]

    summed = sum_small(tie(stack_small(core, small_rows), attn_sums[-1].parts))
    picked, hidden_rows = [], []
    for layer in range(layers):
        at = 1 + 14 * (layers - 1 - layer)
        by_part = summed[at : at + 8].reshape(2, 2, 2, width).swapaxes(1, 2).reshape(2, 4, width)
        proj, up = by_part[0], by_part[1]
        mid, before = summed[at + 8 : at + 11], summed[at + 11 : at + 14]
        grad_q = jnp.concatenate([proj[:, TILE_A], proj[:, 3 * TILE : 3 * TILE + HEAD]], axis=1)
        grad_v = jnp.concatenate([proj[:, TILE_C], proj[:, 3 * TILE + HEAD : 4 * TILE]], axis=1)
        down = summed[:1] if layer + 1 == layers else summed[at - 1 : at]
        picked += [
            before[0:1], mid[0:1], before[1:2], mid[1:2],
            grad_q.reshape(1, width), grad_v.reshape(1, width), mid[2:3], down,
        ]
        hidden_rows.append(up.reshape(1, -1))
    device = lax.axis_index("fsdp") * tp + tp_index
    last, last_hidden = norm_gain.shape[-1], up_bias.shape[-1]
    shard = lax.dynamic_slice_in_dim(jnp.concatenate(picked, axis=0), device * last, last, 1)
    shard = shard.reshape(layers, 8, last)
    hidden_shard = lax.dynamic_slice_in_dim(
        jnp.concatenate(hidden_rows, axis=0), device * last_hidden, last_hidden, 1
    )
    small_outs = [shard[:, 0:2], shard[:, 2:4], shard[:, 4:7], hidden_shard, shard[:, 7]]

    attn_sums[-1].cross([grad])
    attn_sums[-1].along(feed_sums[-1].parts)
    shards = [None] * layers
    for layer in range(layers):
        attn_shard = attn_sums[layers - 1 - layer].total()
        feed_shard = feed_sums[layers - 1 - layer].total()
        q, k, v, out = apart(attn_shard)
        shards[layer] = (q, k, v, out.T, feed_shard[:, :hidden_cols], feed_shard[:, hidden_cols:].T)
    stacked = [jnp.stack([shards[layer][n] for layer in range(layers)]) for n in range(6)]
    return (stream.astype(bf16), grad, *stacked, *small_outs)


def solution(mesh):
    tokens_spec = P(BOTH, None)
    in_spec, out_spec = P(None, "fsdp", "tp"), P(None, "tp", "fsdp")
    matrices = (in_spec, in_spec, in_spec, out_spec, in_spec, out_spec)
    smalls = (P(None, None, BOTH),) * 3 + (P(None, BOTH),) * 2
    return jax.shard_map(
        on_device,
        mesh=mesh,
        in_specs=(tokens_spec, tokens_spec, P("fsdp", None)) + matrices + smalls,
        out_specs=(tokens_spec, tokens_spec) + matrices + smalls,
        check_vma=False,
    )
```

time: 739 us -> 666 us (0.901)
  Pallas kernels: 134 us -> 236 us
  matrix products: 63.6 us -> 0 us
  local copies, waits for them, and re-layouts: 187 us -> 125 us
  waiting for transfers between devices: 166 us -> 131 us
  other arithmetic: 77.3 us -> 48.8 us
  starting transfers between devices: 98.7 us -> 116 us
    pallas_call x12 -> x25, Pallas kernels: 134 us -> 236 us  [the longest x16 202 us: call_parts(): pl.pallas_call(skip_deps(body, len(operands), len(deps)), grid=(parts,),...]
    dot_general x24 -> x0, matrix products: 63.6 us -> none  [the longest x8 25.2 us: dot_nt(): lax.dot_general(left, right, (((1,), (1,)), ((), ())), preferred_element_...]
    ppermute x76, waiting for transfers between devices: 166 us -> 131 us  [hop(): return lax.ppermute(value, axis, [(i, move(i)) for i in range(count)])]
    pallas_call x8 -> x0, local copies, waits for them, and re-layouts: 23.2 us -> none  [the longest x4 12.2 us: feed_backward(): pl.pallas_call(skip_deps(feed_backward_body, 6, len(deps)), grid=(parts,)...]
    ppermute x76, starting transfers between devices: 89.6 us -> 108 us  [hop(): return lax.ppermute(value, axis, [(i, move(i)) for i in range(count)])]
    reduce_sum x15 -> x1, other arithmetic: 19.1 us -> 1.28 us  [on_device(): small_rows = [jnp.sum(grad, axis=0, keepdims=True)]]
    another operation x34 -> x12, local copies, waits for them, and re-layouts: 22.2 us -> 5.07 us
    squeeze x4 -> x3, local copies, waits for them, and re-layouts: 14.7 us -> 0.65 us  [the longest x1 0.61 us: on_device(): bias_proj[layer, 0]]
  transfers between devices with their start and end apart: 80 -> 80, of which waited for: 27 -> 28; matrix products, arithmetic and copies ran while one was open for 39% -> 20% of each run, Pallas kernels for 16% -> 28%
where the time goes in v3:
time: 666 us; the launch traced here: 660 us
  Pallas kernels  236 us (35%)
  waiting for transfers between devices  131 us (20%)
  local copies, waits for them, and re-layouts  125 us (19%)
  starting transfers between devices  116 us (17%)
  other arithmetic  48.8 us (7%)
    pallas_call x16, Pallas kernels, call_parts(): pl.pallas_call(skip_deps(body, len(operands), len(deps)), grid=(parts,),...  202 us
    ppermute x76, waiting for transfers between devices, hop(): return lax.ppermute(value, axis, [(i, move(i)) for i in range(count)])  131 us
    ppermute x76, starting transfers between devices, hop(): return lax.ppermute(value, axis, [(i, move(i)) for i in range(count)])  108 us
    pallas_call x9, Pallas kernels, call_whole(): pl.pallas_call(skip_deps(body, len(operands), len(deps)), in_specs=[pl.Bl...  34 us
    unnamed x230, local copies, waits for them, and re-layouts  32.2 us
    convert_element_type x24, other arithmetic, add_low(): return sum((value.astype(f32) for value in values)).astype(bf16)  22 us
    dynamic_update_slice x20, local copies, waits for them, and re-layouts, both_cores(): lax.dynamic_update_slice(mine, piece[None, :, None], (at_x, 0, at_y, 0, a...  19.9 us
  transfers between devices with their start and end apart: 80, of which 28 were waited for; matrix products, arithmetic and copies ran while one was open for 20% of the time, Pallas kernels for 28%

profile of v3, /device:TPU:0, one launch (start us, length us, event | category | flops | bytes accessed | tf_op | source)
XLA Modules:
  0.0 660.1 jit_solution(3529699238993870831)
XLA Ops:
  4.4 3.1 collective-permute-start
  21.1 3.0 collective-permute-start.3
  38.0 8.6 %collective-permute-done.7 = f32[4,2,576]{2,1,0:T(2,128)S(1)} collective-permute-done((f32[4,2,576]{2,1,0:T(2,128)S(1)}, f32[4,2,576]{2,1,0:T(2,128)S(1)}, u32[]{:S(2)}, u32[]{:S(2)}) %collective-permute-start.7) | collective-permute-done | bytes 18464 | tf_op jit(solution)/shard_map/ppermute | solution.py:430
  64.2 5.2 collective-permute-done.12.refs_1_.refs_3_
  80.3 12.6 %attend_forward.4 = (bf16[2,1024,640]{2,1,0:T(8,128)(2,1)}, bf16[2,512,256]{2,1,0:T(8,128)(2,1)}, f32[2,512,256]{2,1,0:T(8,128)}, f32[512,768]{1,0:T(8,128)}) custom-call(s32[512,1]{1,0:T(8,128)} %copy.207.refs_0_, s32[1,1024]{1,0:T(1,128)} %compare_select_fusion.refs_1_, bf16[512,768]{1,0:T(8,128)(2,1)} %collective-permute-done.9.refs_2_.refs_3_, ...), custom_call_target="tpu_custom_call" | custom-call | flops 4294967296 | bytes 1000 | tf_op jit(solution)/shard_map/attend_forward/pallas_call | solution.py:209
  94.3 12.6 %collective-permute-done.18.refs_0_.refs_1_ = bf16[4,96,1536]{2,1,0:T(8,128)(2,1)S(1)} collective-permute-done((bf16[4,96,1536]{2,1,0:T(8,128)(2,1)}, bf16[4,96,1536]{2,1,0:T(8,128)(2,1)S(1)}, u32[]{:S(2)}, u32[]{:S(2)}) %collective-permute-start.18) | collective-permute-done | bytes 1179680 | tf_op jit(solution)/shard_map/ppermute | solution.py:430
  109.5 12.6 %attend_forward.5 = (bf16[2,1024,640]{2,1,0:T(8,128)(2,1)}, bf16[2,512,256]{2,1,0:T(8,128)(2,1)}, f32[2,512,256]{2,1,0:T(8,128)}, f32[512,768]{1,0:T(8,128)}) custom-call(s32[512,1]{1,0:T(8,128)} %copy.207.refs_0_, s32[1,1024]{1,0:T(1,128)} %compare_select_fusion.refs_1_, bf16[512,768]{1,0:T(8,128)(2,1)} %collective-permute-done.9.refs_2_.refs_3_, ...), custom_call_target="tpu_custom_call" | custom-call | flops 4294967296 | bytes 1000 | tf_op jit(solution)/shard_map/attend_forward/pallas_call | solution.py:209
  129.2 10.3 %collective-permute-done.20.refs_1_ = bf16[4,96,768]{2,1,0:T(8,128)(2,1)S(1)} collective-permute-done((bf16[4,96,768]{2,1,0:T(8,128)(2,1)S(1)}, bf16[4,96,768]{2,1,0:T(8,128)(2,1)S(1)}, u32[]{:S(2)}, u32[]{:S(2)}) %collective-permute-start.20) | collective-permute-done | bytes 589856 | tf_op jit(solution)/shard_map/ppermute | solution.py:430
  147.5 3.0 collective-permute-start.25
  150.6 4.7 collective-permute-done.23.refs_1_
  155.3 5.4 collective-permute-done.24.refs_2_
  162.2 3.6 collective-permute-start.32
  167.7 2.9 norm_forward.5.refs_0_.refs_1_.refs_4_
  170.6 6.8 %feed_forward.4 = (f32[2,512,768]{2,1,0:T(8,128)}, f32[512,768]{1,0:T(8,128)}) custom-call(bf16[512,768]{1,0:T(8,128)(2,1)} %norm_forward.5.refs_0_.refs_1_.refs_4_, bf16[2,768,1536]{2,1,0:T(8,128)(2,1)} %bitcast.450, f32[2,1,768]{2,1,0:T(1,128)} %get-tuple-element.274.refs_2_, f32[512,768]{1,0:T(8,128)} %get-tuple-element.75.refs_0_.refs_1_.refs_3_.refs_4_, ...), custom_call_target="tpu_custom_call" | custom-call | flops 2415919104 | bytes 1000 | tf_op jit(solution)/shard_map/feed_forward/pallas_call | solution.py:209
  183.7 6.8 %feed_forward.5 = (f32[2,512,768]{2,1,0:T(8,128)}, f32[512,768]{1,0:T(8,128)}) custom-call(bf16[512,768]{1,0:T(8,128)(2,1)} %norm_forward.5.refs_0_.refs_1_.refs_4_, bf16[2,768,1536]{2,1,0:T(8,128)(2,1)} %collective-permute-done.22.refs_1_.refs_3_, f32[2,1,768]{2,1,0:T(1,128)} %get-tuple-element.275.refs_2_, f32[512,768]{1,0:T(8,128)} %get-tuple-element.76.refs_3_.refs_1_, ...), custom_call_target="tpu_custom_call" | custom-call | flops 2415919104 | bytes 1000 | tf_op jit(solution)/shard_map/feed_forward/pallas_call | solution.py:209
  205.5 3.4 collective-permute-start.28
  213.5 12.6 %attend_forward.6 = (bf16[2,1024,640]{2,1,0:T(8,128)(2,1)}, bf16[2,512,256]{2,1,0:T(8,128)(2,1)}, f32[2,512,256]{2,1,0:T(8,128)}, f32[512,768]{1,0:T(8,128)}) custom-call(s32[512,1]{1,0:T(8,128)} %copy.207.refs_0_, s32[1,1024]{1,0:T(1,128)} %compare_select_fusion.refs_1_, bf16[512,768]{1,0:T(8,128)(2,1)} %collective-permute-done.28.refs_2_.refs_3_, ...), custom_call_target="tpu_custom_call" | custom-call | flops 4294967296 | bytes 1000 | tf_op jit(solution)/shard_map/attend_forward/pallas_call | solution.py:209
  226.2 12.6 %attend_forward.7 = (bf16[2,1024,640]{2,1,0:T(8,128)(2,1)}, bf16[2,512,256]{2,1,0:T(8,128)(2,1)}, f32[2,512,256]{2,1,0:T(8,128)}, f32[512,768]{1,0:T(8,128)}) custom-call(s32[512,1]{1,0:T(8,128)} %copy.207.refs_0_, s32[1,1024]{1,0:T(1,128)} %compare_select_fusion.refs_1_, bf16[512,768]{1,0:T(8,128)(2,1)} %collective-permute-done.28.refs_2_.refs_3_, ...), custom_call_target="tpu_custom_call" | custom-call | flops 4294967296 | bytes 1000 | tf_op jit(solution)/shard_map/attend_forward/pallas_call | solution.py:209
  240.9 12.2 %collective-permute-start.37 = (bf16[4,96,768]{2,1,0:T(8,128)(2,1)S(1)}, bf16[4,96,768]{2,1,0:T(8,128)(2,1)S(1)}, u32[]{:S(2)}, u32[]{:S(2)}) collective-permute-start(bf16[4,96,768]{2,1,0:T(8,128)(2,1)S(1)} %slice.617), channel_id=1, source_target_pairs={{0,2},{1,3},{2,0},{3,1},{4,6},{5,7},{6,4},{7,5},{8,10},{9,11},{10,... | collective-permute-start | bytes 1769480 | tf_op jit(solution)/shard_map/ppermute | solution.py:430
  259.0 6.9 %collective-permute-done.37 = bf16[4,96,768]{2,1,0:T(8,128)(2,1)S(1)} collective-permute-done((bf16[4,96,768]{2,1,0:T(8,128)(2,1)S(1)}, bf16[4,96,768]{2,1,0:T(8,128)(2,1)S(1)}, u32[]{:S(2)}, u32[]{:S(2)}) %collective-permute-start.37) | collective-permute-done | bytes 589856 | tf_op jit(solution)/shard_map/ppermute | solution.py:430
  274.1 6.8 %feed_forward.6 = (f32[2,512,768]{2,1,0:T(8,128)}, f32[512,768]{1,0:T(8,128)}) custom-call(bf16[512,768]{1,0:T(8,128)(2,1)} %norm_forward.7.refs_0_.refs_1_.refs_4_, bf16[2,768,1536]{2,1,0:T(8,128)(2,1)} %bitcast.447, f32[2,1,768]{2,1,0:T(1,128)} %get-tuple-element.272.refs_2_, f32[512,768]{1,0:T(8,128)} %get-tuple-element.79.refs_0_.refs_1_.refs_3_, ...), custom_call_target="tpu_custom_call" | custom-call | flops 2415919104 | bytes 1000 | tf_op jit(solution)/shard_map/feed_forward/pallas_call | solution.py:209
  280.9 7.0 %feed_forward.7 = (f32[2,512,768]{2,1,0:T(8,128)}, f32[512,768]{1,0:T(8,128)}) custom-call(bf16[512,768]{1,0:T(8,128)(2,1)} %norm_forward.7.refs_0_.refs_1_.refs_4_, bf16[2,768,1536]{2,1,0:T(8,128)(2,1)} %collective-permute-done.39.refs_1_.refs_3_, f32[2,1,768]{2,1,0:T(1,128)} %get-tuple-element.273.refs_2_, f32[512,768]{1,0:T(8,128)} %get-tuple-element.80.refs_3_, ...), custom_call_target="tpu_custom_call" | custom-call | flops 2415919104 | bytes 1000 | tf_op jit(solution)/shard_map/feed_forward/pallas_call | solution.py:209
  287.9 11.4 %feed_backward.4 = (bf16[2,768,1536]{2,1,0:T(8,128)(2,1)}, f32[2,1,768]{2,1,0:T(1,128)}, f32[512,768]{1,0:T(8,128)}) custom-call(bf16[512,768]{1,0:T(8,128)(2,1)} %refs_0_.3, bf16[512,768]{1,0:T(8,128)(2,1)} %norm_forward.7.refs_0_.refs_1_.refs_4_, f32[2,512,768]{2,1,0:T(8,128)} %get-tuple-element.83.refs_2_, ...), custom_call_target="tpu_custom_call" | custom-call | flops 3758096384 | bytes 1000 | tf_op jit(solution)/shard_map/feed_backward/pallas_call | solution.py:209
  299.9 10.7 %feed_backward.5 = (bf16[2,768,1536]{2,1,0:T(8,128)(2,1)}, f32[2,1,768]{2,1,0:T(1,128)}, f32[512,768]{1,0:T(8,128)}) custom-call(bf16[512,768]{1,0:T(8,128)(2,1)} %refs_0_.3, bf16[512,768]{1,0:T(8,128)(2,1)} %norm_forward.7.refs_0_.refs_1_.refs_4_, f32[2,512,768]{2,1,0:T(8,128)} %get-tuple-element.82.refs_2_, bf16[2,768,1536]{2,1,0:T(8,128)(2,1)} %bitcast.448, ...), custom_call_target="tpu_custom_call" | custom-call | flops 3758096384 | bytes 1000 | tf_op jit(solution)/shard_map/feed_backward/pallas_call | solution.py:209
  325.7 4.9 norm_backward.4
  330.6 19.7 %attend_backward.4 = (bf16[2,768,768]{2,1,0:T(8,128)(2,1)}, f32[2,1,768]{2,1,0:T(1,128)}, f32[1024,768]{1,0:T(8,128)}, bf16[512,768]{1,0:T(8,128)(2,1)}) custom-call(s32[1,512]{1,0:T(1,128)} %bitcast.479, s32[1024,1]{1,0:T(8,128)} %fusion.28.refs_1_, bf16[512,768]{1,0:T(8,128)(2,1)} %get-tuple-element.88.refs_2_, ...), custom_call_target="tpu_custom_call" | custom-call | flops 6979321856 | bytes 1000 | tf_op jit(solution)/shard_map/attend_backward/pallas_call | solution.py:209
  352.8 20.5 %attend_backward.5 = (bf16[2,768,768]{2,1,0:T(8,128)(2,1)}, f32[2,1,768]{2,1,0:T(1,128)}, f32[1024,768]{1,0:T(8,128)}, bf16[512,768]{1,0:T(8,128)(2,1)}) custom-call(s32[1,512]{1,0:T(1,128)} %bitcast.481, s32[1024,1]{1,0:T(8,128)} %fusion.28.refs_1_, bf16[512,768]{1,0:T(8,128)(2,1)} %get-tuple-element.88.refs_2_, ...), custom_call_target="tpu_custom_call" | custom-call | flops 6979321856 | bytes 1000 | tf_op jit(solution)/shard_map/attend_backward/pallas_call | solution.py:209
  382.4 9.0 %collective-permute-done.46.refs_0_ = bf16[4,96,768]{2,1,0:T(8,128)(2,1)S(1)} collective-permute-done((bf16[4,96,768]{2,1,0:T(8,128)(2,1)S(1)}, bf16[4,96,768]{2,1,0:T(8,128)(2,1)S(1)}, u32[]{:S(2)}, u32[]{:S(2)}) %collective-permute-start.46) | collective-permute-done | bytes 589856 | tf_op jit(solution)/shard_map/ppermute | solution.py:430
  402.8 5.7 norm_backward.5
  408.5 11.5 %feed_backward.6 = (bf16[2,768,1536]{2,1,0:T(8,128)(2,1)}, f32[2,1,768]{2,1,0:T(1,128)}, f32[512,768]{1,0:T(8,128)}) custom-call(bf16[512,768]{1,0:T(8,128)(2,1)} %get-tuple-element.101.refs_0_, bf16[512,768]{1,0:T(8,128)(2,1)} %norm_forward.5.refs_0_.refs_1_.refs_4_, f32[2,512,768]{2,1,0:T(8,128)} %get-tuple-element.103.refs_2_, ...), custom_call_target="tpu_custom_call" | custom-call | flops 3758096384 | bytes 1000 | tf_op jit(solution)/shard_map/feed_backward/pallas_call | solution.py:209
  425.9 7.3 %collective-permute-done.47.refs_5_ = bf16[96,1536]{1,0:T(8,128)(2,1)} collective-permute-done((bf16[96,1536]{1,0:T(8,128)(2,1)}, bf16[96,1536]{1,0:T(8,128)(2,1)}, u32[]{:S(2)}, u32[]{:S(2)}) %collective-permute-start.47) | collective-permute-done | bytes 294944 | tf_op jit(solution)/shard_map/ppermute | solution.py:430
  438.9 6.0 collective-permute-done.48.refs_6_
  449.0 10.5 %feed_backward.7 = (bf16[2,768,1536]{2,1,0:T(8,128)(2,1)}, f32[2,1,768]{2,1,0:T(1,128)}, f32[512,768]{1,0:T(8,128)}) custom-call(bf16[512,768]{1,0:T(8,128)(2,1)} %get-tuple-element.101.refs_0_, bf16[512,768]{1,0:T(8,128)(2,1)} %norm_forward.5.refs_0_.refs_1_.refs_4_, f32[2,512,768]{2,1,0:T(8,128)} %get-tuple-element.102.refs_2_, ...), custom_call_target="tpu_custom_call" | custom-call | flops 3758096384 | bytes 1000 | tf_op jit(solution)/shard_map/feed_backward/pallas_call | solution.py:209
  479.9 4.9 norm_backward.6
  485.5 19.6 %attend_backward.6 = (bf16[2,768,768]{2,1,0:T(8,128)(2,1)}, f32[2,1,768]{2,1,0:T(1,128)}, f32[1024,768]{1,0:T(8,128)}, bf16[512,768]{1,0:T(8,128)(2,1)}) custom-call(s32[1,512]{1,0:T(1,128)} %bitcast.482, s32[1024,1]{1,0:T(8,128)} %fusion.28.refs_1_, bf16[512,768]{1,0:T(8,128)(2,1)} %get-tuple-element.109.refs_2_, ...), custom_call_target="tpu_custom_call" | custom-call | flops 6979321856 | bytes 1000 | tf_op jit(solution)/shard_map/attend_backward/pallas_call | solution.py:209
  509.2 6.5 collective-permute-start.57
  521.2 4.2 collective-permute-done.58.refs_13_
  530.6 20.3 %attend_backward.7 = (bf16[2,768,768]{2,1,0:T(8,128)(2,1)}, f32[2,1,768]{2,1,0:T(1,128)}, f32[1024,768]{1,0:T(8,128)}, bf16[512,768]{1,0:T(8,128)(2,1)}) custom-call(s32[1,512]{1,0:T(1,128)} %bitcast.484, s32[1024,1]{1,0:T(8,128)} %fusion.28.refs_1_, bf16[512,768]{1,0:T(8,128)(2,1)} %get-tuple-element.109.refs_2_, ...), custom_call_target="tpu_custom_call" | custom-call | flops 6979321856 | bytes 1000 | tf_op jit(solution)/shard_map/attend_backward/pallas_call | solution.py:209
  561.7 6.6 collective-permute-done.63.refs_0_
  568.2 3.3 collective-permute-done.62.refs_0_
  574.2 3.8 collective-permute-start.66
  587.7 8.9 %collective-permute-done.67.refs_2_ = bf16[96,1536]{1,0:T(8,128)(2,1)S(1)} collective-permute-done((bf16[96,1536]{1,0:T(8,128)(2,1)S(1)}, bf16[96,1536]{1,0:T(8,128)(2,1)S(1)}, u32[]{:S(2)}, u32[]{:S(2)}) %collective-permute-start.67) | collective-permute-done | bytes 294944 | tf_op jit(solution)/shard_map/ppermute | solution.py:430
  600.2 5.7 norm_backward.7
  619.5 3.5 collective-permute-done.75
  624.3 3.4 collective-permute-done.76
  627.7 8.9 %collective-permute-start.79 = (f32[32,768]{1,0:T(8,128)S(1)}, f32[32,768]{1,0:T(8,128)S(1)}, u32[]{:S(2)}, u32[]{:S(2)}) collective-permute-start(f32[32,768]{1,0:T(8,128)S(1)} %add.564), channel_id=1, source_target_pairs={{0,24},{4,28},{8,0},{12,4},{16,8},{20,12},{24,16},{28,20},{1,25},{... | collective-permute-start | bytes 294920 | tf_op jit(solution)/shard_map/ppermute | solution.py:430
  640.8 3.2 collective-permute-start.73
  648.6 7.8 %collective-permute-done.72 = bf16[96,768]{1,0:T(8,128)(2,1)S(1)} collective-permute-done((bf16[96,768]{1,0:T(8,128)(2,1)S(1)}, bf16[96,768]{1,0:T(8,128)(2,1)S(1)}, u32[]{:S(2)}, u32[]{:S(2)}) %collective-permute-start.72) | collective-permute-done | bytes 147488 | tf_op jit(solution)/shard_map/ppermute | solution.py:430
  (677 shorter events, 266.6 us)
Async XLA Ops:
  4.4 14.9 %collective-permute-start = (bf16[96,768]{1,0:T(8,128)(2,1)S(1)}, bf16[96,768]{1,0:T(8,128)(2,1)S(1)}, u32[]{:S(2)}, u32[]{:S(2)}) collective-permute-start(bf16[96,768]{1,0:T(8,128)(2,1)S(1)} %concatenate.73), channel_id=1, source_target_pairs={{0,8},{4,12},{8,16},{12,20},{16,24},{20,28},{24,0},{28,4},{1,9},{5... | collective-permute-start | bytes 442376 | tf_op jit(solution)/shard_map/ppermute | solution.py:430
  32.7 29.1 %collective-permute-start.10 = (bf16[4,96,768]{2,1,0:T(8,128)(2,1)S(1)}, bf16[4,96,768]{2,1,0:T(8,128)(2,1)S(1)}, u32[]{:S(2)}, u32[]{:S(2)}) collective-permute-start(bf16[4,96,768]{2,1,0:T(8,128)(2,1)S(1)} %bitcast_dynamic-update-slice_fusion.32), channel_id=1, source_target_pairs={{0,2},{1,3},{2,0},{3,1},{4,6},{5,7},{6,4},{7,5},{8,10},{9,11},{10,... | collective-permute-start | bytes 1769480 | tf_op jit(solution)/shard_map/ppermute | solution.py:430
  34.2 25.2 %collective-permute-start.11 = (bf16[4,96,768]{2,1,0:T(8,128)(2,1)S(1)}, bf16[4,96,768]{2,1,0:T(8,128)(2,1)S(1)}, u32[]{:S(2)}, u32[]{:S(2)}) collective-permute-start(bf16[4,96,768]{2,1,0:T(8,128)(2,1)S(1)} %bitcast_dynamic-update-slice_fusion.32), channel_id=1, source_target_pairs={{0,4},{4,0},{8,12},{12,8},{16,20},{20,16},{24,28},{28,24},{1,5},{5... | collective-permute-start | bytes 1769480 | tf_op jit(solution)/shard_map/ppermute | solution.py:430
  34.7 40.1 %collective-permute-start.15 = (bf16[96,1536]{1,0:T(8,128)(2,1)}, bf16[96,1536]{1,0:T(8,128)(2,1)}, u32[]{:S(2)}, u32[]{:S(2)}) collective-permute-start(bf16[96,1536]{1,0:T(8,128)(2,1)} %tie.31), channel_id=1, source_target_pairs={{0,8},{4,12},{8,16},{12,20},{16,24},{20,28},{24,0},{28,4},{1,9},{5... | collective-permute-start | bytes 884744 | tf_op jit(solution)/shard_map/ppermute | solution.py:430
  35.7 40.1 %collective-permute-start.16 = (bf16[96,1536]{1,0:T(8,128)(2,1)}, bf16[96,1536]{1,0:T(8,128)(2,1)}, u32[]{:S(2)}, u32[]{:S(2)}) collective-permute-start(bf16[96,1536]{1,0:T(8,128)(2,1)} %tie.31), channel_id=1, source_target_pairs={{0,16},{4,20},{8,24},{12,28},{16,0},{20,4},{24,8},{28,12},{1,17},{... | collective-permute-start | bytes 884744 | tf_op jit(solution)/shard_map/ppermute | solution.py:430
  49.4 27.4 %collective-permute-start.17 = (bf16[96,1536]{1,0:T(8,128)(2,1)S(1)}, bf16[96,1536]{1,0:T(8,128)(2,1)}, u32[]{:S(2)}, u32[]{:S(2)}) collective-permute-start(bf16[96,1536]{1,0:T(8,128)(2,1)S(1)} %copy-done.37), channel_id=1, source_target_pairs={{0,24},{4,28},{8,0},{12,4},{16,8},{20,12},{24,16},{28,20},{1,25},{... | collective-permute-start | bytes 884744 | tf_op jit(solution)/shard_map/ppermute | solution.py:430
  73.4 35.5 %collective-permute-start.14 = (bf16[2,768,768]{2,1,0:T(8,128)(2,1)}, bf16[2,768,768]{2,1,0:T(8,128)(2,1)}, u32[]{:S(2)}, u32[]{:S(2)}) collective-permute-start(bf16[2,768,768]{2,1,0:T(8,128)(2,1)} %bitcast.31.refs_4_.refs_5_), channel_id=1, source_target_pairs={{0,1},{1,0},{2,3},{3,2},{4,5},{5,4},{6,7},{7,6},{8,9},{9,8},{10,11... | collective-permute-start | bytes 7077896 | tf_op jit(solution)/shard_map/ppermute | solution.py:430
  78.8 28.1 %collective-permute-start.18 = (bf16[4,96,1536]{2,1,0:T(8,128)(2,1)}, bf16[4,96,1536]{2,1,0:T(8,128)(2,1)S(1)}, u32[]{:S(2)}, u32[]{:S(2)}) collective-permute-start(bf16[4,96,1536]{2,1,0:T(8,128)(2,1)} %tie.32.refs_8_), channel_id=1, source_target_pairs={{0,2},{1,3},{2,0},{3,1},{4,6},{5,7},{6,4},{7,5},{8,10},{9,11},{10,... | collective-permute-start | bytes 3538952 | tf_op jit(solution)/shard_map/ppermute | solution.py:430
  78.8 28.2 %collective-permute-start.19 = (bf16[4,96,1536]{2,1,0:T(8,128)(2,1)}, bf16[4,96,1536]{2,1,0:T(8,128)(2,1)S(1)}, u32[]{:S(2)}, u32[]{:S(2)}) collective-permute-start(bf16[4,96,1536]{2,1,0:T(8,128)(2,1)} %tie.32.refs_8_), channel_id=1, source_target_pairs={{0,4},{4,0},{8,12},{12,8},{16,20},{20,16},{24,28},{28,24},{1,5},{5... | collective-permute-start | bytes 3538952 | tf_op jit(solution)/shard_map/ppermute | solution.py:430
  123.3 16.2 %collective-permute-start.20 = (bf16[4,96,768]{2,1,0:T(8,128)(2,1)S(1)}, bf16[4,96,768]{2,1,0:T(8,128)(2,1)S(1)}, u32[]{:S(2)}, u32[]{:S(2)}) collective-permute-start(bf16[4,96,768]{2,1,0:T(8,128)(2,1)S(1)} %slice.593), channel_id=1, source_target_pairs={{0,2},{1,3},{2,0},{3,1},{4,6},{5,7},{6,4},{7,5},{8,10},{9,11},{10,... | collective-permute-start | bytes 1769480 | tf_op jit(solution)/shard_map/ppermute | solution.py:430
  126.9 16.0 %collective-permute-start.21 = (bf16[4,96,768]{2,1,0:T(8,128)(2,1)S(1)}, bf16[4,96,768]{2,1,0:T(8,128)(2,1)S(1)}, u32[]{:S(2)}, u32[]{:S(2)}) collective-permute-start(bf16[4,96,768]{2,1,0:T(8,128)(2,1)S(1)} %slice.594), channel_id=1, source_target_pairs={{0,4},{4,0},{8,12},{12,8},{16,20},{20,16},{24,28},{28,24},{1,5},{5... | collective-permute-start | bytes 1769480 | tf_op jit(solution)/shard_map/ppermute | solution.py:430
  143.8 39.1 %collective-permute-start.22 = (bf16[2,768,1536]{2,1,0:T(8,128)(2,1)}, bf16[2,768,1536]{2,1,0:T(8,128)(2,1)}, u32[]{:S(2)}, u32[]{:S(2)}) collective-permute-start(bf16[2,768,1536]{2,1,0:T(8,128)(2,1)} %bitcast.449), channel_id=1, source_target_pairs={{0,1},{1,0},{2,3},{3,2},{4,5},{5,4},{6,7},{7,6},{8,9},{9,8},{10,11... | collective-permute-start | bytes 14155784 | tf_op jit(solution)/shard_map/ppermute | solution.py:430
  162.2 40.4 %collective-permute-start.32 = (bf16[96,1536]{1,0:T(8,128)(2,1)}, bf16[96,1536]{1,0:T(8,128)(2,1)S(1)}, u32[]{:S(2)}, u32[]{:S(2)}) collective-permute-start(bf16[96,1536]{1,0:T(8,128)(2,1)} %tie.39), channel_id=1, source_target_pairs={{0,8},{4,12},{8,16},{12,20},{16,24},{20,28},{24,0},{28,4},{1,9},{5... | collective-permute-start | bytes 884744 | tf_op jit(solution)/shard_map/ppermute | solution.py:430
  165.8 36.9 %collective-permute-start.33 = (bf16[96,1536]{1,0:T(8,128)(2,1)}, bf16[96,1536]{1,0:T(8,128)(2,1)S(1)}, u32[]{:S(2)}, u32[]{:S(2)}) collective-permute-start(bf16[96,1536]{1,0:T(8,128)(2,1)} %tie.39), channel_id=1, source_target_pairs={{0,16},{4,20},{8,24},{12,28},{16,0},{20,4},{24,8},{28,12},{1,17},{... | collective-permute-start | bytes 884744 | tf_op jit(solution)/shard_map/ppermute | solution.py:430
  166.1 14.4 %collective-permute-start.26 = (bf16[4,96,768]{2,1,0:T(8,128)(2,1)}, bf16[4,96,768]{2,1,0:T(8,128)(2,1)S(1)}, u32[]{:S(2)}, u32[]{:S(2)}) collective-permute-start(bf16[4,96,768]{2,1,0:T(8,128)(2,1)} %tie.36), channel_id=1, source_target_pairs={{0,2},{1,3},{2,0},{3,1},{4,6},{5,7},{6,4},{7,5},{8,10},{9,11},{10,... | collective-permute-start | bytes 1769480 | tf_op jit(solution)/shard_map/ppermute | solution.py:430
  167.1 15.8 %collective-permute-start.27 = (bf16[4,96,768]{2,1,0:T(8,128)(2,1)}, bf16[4,96,768]{2,1,0:T(8,128)(2,1)S(1)}, u32[]{:S(2)}, u32[]{:S(2)}) collective-permute-start(bf16[4,96,768]{2,1,0:T(8,128)(2,1)} %tie.36), channel_id=1, source_target_pairs={{0,4},{4,0},{8,12},{12,8},{16,20},{20,16},{24,28},{28,24},{1,5},{5... | collective-permute-start | bytes 1769480 | tf_op jit(solution)/shard_map/ppermute | solution.py:430
  180.5 28.3 %collective-permute-start.34 = (bf16[96,1536]{1,0:T(8,128)(2,1)S(1)}, bf16[96,1536]{1,0:T(8,128)(2,1)S(1)}, u32[]{:S(2)}, u32[]{:S(2)}) collective-permute-start(bf16[96,1536]{1,0:T(8,128)(2,1)S(1)} %copy-done.36), channel_id=1, source_target_pairs={{0,24},{4,28},{8,0},{12,4},{16,8},{20,12},{24,16},{28,20},{1,25},{... | collective-permute-start | bytes 884744 | tf_op jit(solution)/shard_map/ppermute | solution.py:430
  202.6 23.6 %collective-permute-start.31 = (bf16[2,768,768]{2,1,0:T(8,128)(2,1)}, bf16[2,768,768]{2,1,0:T(8,128)(2,1)}, u32[]{:S(2)}, u32[]{:S(2)}) collective-permute-start(bf16[2,768,768]{2,1,0:T(8,128)(2,1)} %bitcast.452), channel_id=1, source_target_pairs={{0,1},{1,0},{2,3},{3,2},{4,5},{5,4},{6,7},{7,6},{8,9},{9,8},{10,11... | collective-permute-start | bytes 7077896 | tf_op jit(solution)/shard_map/ppermute | solution.py:430
  209.9 43.2 %collective-permute-start.35 = (bf16[4,96,1536]{2,1,0:T(8,128)(2,1)}, bf16[4,96,1536]{2,1,0:T(8,128)(2,1)S(1)}, u32[]{:S(2)}, u32[]{:S(2)}) collective-permute-start(bf16[4,96,1536]{2,1,0:T(8,128)(2,1)} %tie.40.refs_8_), channel_id=1, source_target_pairs={{0,2},{1,3},{2,0},{3,1},{4,6},{5,7},{6,4},{7,5},{8,10},{9,11},{10,... | collective-permute-start | bytes 3538952 | tf_op jit(solution)/shard_map/ppermute | solution.py:430
  209.9 28.9 %collective-permute-start.36 = (bf16[4,96,1536]{2,1,0:T(8,128)(2,1)}, bf16[4,96,1536]{2,1,0:T(8,128)(2,1)S(1)}, u32[]{:S(2)}, u32[]{:S(2)}) collective-permute-start(bf16[4,96,1536]{2,1,0:T(8,128)(2,1)} %tie.40.refs_8_), channel_id=1, source_target_pairs={{0,4},{4,0},{8,12},{12,8},{16,20},{20,16},{24,28},{28,24},{1,5},{5... | collective-permute-start | bytes 3538952 | tf_op jit(solution)/shard_map/ppermute | solution.py:430
  240.9 25.0 %collective-permute-start.37 = (bf16[4,96,768]{2,1,0:T(8,128)(2,1)S(1)}, bf16[4,96,768]{2,1,0:T(8,128)(2,1)S(1)}, u32[]{:S(2)}, u32[]{:S(2)}) collective-permute-start(bf16[4,96,768]{2,1,0:T(8,128)(2,1)S(1)} %slice.617), channel_id=1, source_target_pairs={{0,2},{1,3},{2,0},{3,1},{4,6},{5,7},{6,4},{7,5},{8,10},{9,11},{10,... | collective-permute-start | bytes 1769480 | tf_op jit(solution)/shard_map/ppermute | solution.py:430
  299.3 15.2 %collective-permute-start.40 = (bf16[2,768,1536]{2,1,0:T(8,128)(2,1)}, bf16[2,768,1536]{2,1,0:T(8,128)(2,1)S(1)}, u32[]{:S(2)}, u32[]{:S(2)}) collective-permute-start(bf16[2,768,1536]{2,1,0:T(8,128)(2,1)} %get-tuple-element.87), channel_id=1, source_target_pairs={{0,1},{1,0},{2,3},{3,2},{4,5},{5,4},{6,7},{7,6},{8,9},{9,8},{10,11... | collective-permute-start | bytes 14155784 | tf_op jit(solution)/shard_map/ppermute | solution.py:430
  316.7 33.7 %collective-permute-start.41 = (bf16[4,2,96,768]{3,2,0,1:T(8,128)(2,1)S(1)}, bf16[4,2,96,768]{3,2,0,1:T(8,128)(2,1)}, u32[]{:S(2)}, u32[]{:S(2)}) collective-permute-start(bf16[4,2,96,768]{3,2,0,1:T(8,128)(2,1)S(1)} %fusion.4), channel_id=1, source_target_pairs={{0,2},{1,3},{2,0},{3,1},{4,6},{5,7},{6,4},{7,5},{8,10},{9,11},{10,... | collective-permute-start | bytes 3538952 | tf_op jit(solution)/shard_map/ppermute | solution.py:430
  319.8 33.0 %collective-permute-start.42 = (bf16[2,4,96,768]{3,2,1,0:T(8,128)(2,1)}, bf16[2,4,96,768]{3,2,1,0:T(8,128)(2,1)}, u32[]{:S(2)}, u32[]{:S(2)}) collective-permute-start(bf16[2,4,96,768]{3,2,1,0:T(8,128)(2,1)} %fusion.5.refs_5_), channel_id=1, source_target_pairs={{0,4},{4,0},{8,12},{12,8},{16,20},{20,16},{24,28},{28,24},{1,5},{5... | collective-permute-start | bytes 3538952 | tf_op jit(solution)/shard_map/ppermute | solution.py:430
  350.3 47.4 %collective-permute-start.44 = (bf16[2,768,768]{2,1,0:T(8,128)(2,1)}, bf16[2,768,768]{2,1,0:T(8,128)(2,1)}, u32[]{:S(2)}, u32[]{:S(2)}) collective-permute-start(bf16[2,768,768]{2,1,0:T(8,128)(2,1)} %get-tuple-element.100), channel_id=1, source_target_pairs={{0,1},{1,0},{2,3},{3,2},{4,5},{5,4},{6,7},{7,6},{8,9},{9,8},{10,11... | collective-permute-start | bytes 7077896 | tf_op jit(solution)/shard_map/ppermute | solution.py:430
  375.7 15.8 %collective-permute-start.46 = (bf16[4,96,768]{2,1,0:T(8,128)(2,1)S(1)}, bf16[4,96,768]{2,1,0:T(8,128)(2,1)S(1)}, u32[]{:S(2)}, u32[]{:S(2)}) collective-permute-start(bf16[4,96,768]{2,1,0:T(8,128)(2,1)S(1)} %dynamic-slice_bitcast_fusion.2), channel_id=1, source_target_pairs={{0,2},{1,3},{2,0},{3,1},{4,6},{5,7},{6,4},{7,5},{8,10},{9,11},{10,... | collective-permute-start | bytes 1769480 | tf_op jit(solution)/shard_map/ppermute | solution.py:430
  378.3 15.9 %collective-permute-start.45 = (bf16[4,96,768]{2,1,0:T(8,128)(2,1)}, bf16[4,96,768]{2,1,0:T(8,128)(2,1)S(1)}, u32[]{:S(2)}, u32[]{:S(2)}) collective-permute-start(bf16[4,96,768]{2,1,0:T(8,128)(2,1)} %dynamic-slice_bitcast_fusion.3), channel_id=1, source_target_pairs={{0,4},{4,0},{8,12},{12,8},{16,20},{20,16},{24,28},{28,24},{1,5},{5... | collective-permute-start | bytes 1769480 | tf_op jit(solution)/shard_map/ppermute | solution.py:430
  379.7 23.1 %collective-permute-start.43 = (bf16[512,768]{1,0:T(8,128)(2,1)}, bf16[512,768]{1,0:T(8,128)(2,1)}, u32[]{:S(2)}, u32[]{:S(2)}) collective-permute-start(bf16[512,768]{1,0:T(8,128)(2,1)} %get-tuple-element.97), channel_id=1, source_target_pairs={{1,0},{2,1},{3,2},{5,4},{6,5},{7,6},{9,8},{10,9},{11,10},{13,12},{... | collective-permute-start | bytes 2359304 | tf_op jit(solution)/shard_map/ppermute | solution.py:574
  420.1 51.0 %collective-permute-start.52 = (bf16[2,768,1536]{2,1,0:T(8,128)(2,1)}, bf16[2,768,1536]{2,1,0:T(8,128)(2,1)}, u32[]{:S(2)}, u32[]{:S(2)}) collective-permute-start(bf16[2,768,1536]{2,1,0:T(8,128)(2,1)} %get-tuple-element.108), channel_id=1, source_target_pairs={{0,1},{1,0},{2,3},{3,2},{4,5},{5,4},{6,7},{7,6},{8,9},{9,8},{10,11... | collective-permute-start | bytes 14155784 | tf_op jit(solution)/shard_map/ppermute | solution.py:430
  421.2 23.7 %collective-permute-start.48 = (bf16[96,1536]{1,0:T(8,128)(2,1)}, bf16[96,1536]{1,0:T(8,128)(2,1)}, u32[]{:S(2)}, u32[]{:S(2)}) collective-permute-start(bf16[96,1536]{1,0:T(8,128)(2,1)} %get-tuple-element.211), channel_id=1, source_target_pairs={{0,16},{4,20},{8,24},{12,28},{16,0},{20,4},{24,8},{28,12},{1,17},{... | collective-permute-start | bytes 884744 | tf_op jit(solution)/shard_map/ppermute | solution.py:430
  423.5 21.3 %collective-permute-start.49 = (bf16[96,1536]{1,0:T(8,128)(2,1)}, bf16[96,1536]{1,0:T(8,128)(2,1)}, u32[]{:S(2)}, u32[]{:S(2)}) collective-permute-start(bf16[96,1536]{1,0:T(8,128)(2,1)} %get-tuple-element.209), channel_id=1, source_target_pairs={{0,24},{4,28},{8,0},{12,4},{16,8},{20,12},{24,16},{28,20},{1,25},{... | collective-permute-start | bytes 884744 | tf_op jit(solution)/shard_map/ppermute | solution.py:430
  425.3 21.6 %collective-permute-start.50 = (bf16[4,2,96,384]{3,2,0,1:T(8,128)(2,1)}, bf16[4,2,96,384]{3,2,0,1:T(8,128)(2,1)}, u32[]{:S(2)}, u32[]{:S(2)}) collective-permute-start(bf16[4,2,96,384]{3,2,0,1:T(8,128)(2,1)} %copy-done.42), channel_id=1, source_target_pairs={{0,2},{1,3},{2,0},{3,1},{4,6},{5,7},{6,4},{7,5},{8,10},{9,11},{10,... | collective-permute-start | bytes 1769480 | tf_op jit(solution)/shard_map/ppermute | solution.py:430
  433.2 15.7 %collective-permute-start.51 = (bf16[2,4,96,384]{3,2,1,0:T(8,128)(2,1)}, bf16[2,4,96,384]{3,2,1,0:T(8,128)(2,1)}, u32[]{:S(2)}, u32[]{:S(2)}) collective-permute-start(bf16[2,4,96,384]{3,2,1,0:T(8,128)(2,1)} %fusion.17.refs_6_), channel_id=1, source_target_pairs={{0,4},{4,0},{8,12},{12,8},{16,20},{20,16},{24,28},{28,24},{1,5},{5... | collective-permute-start | bytes 1769480 | tf_op jit(solution)/shard_map/ppermute | solution.py:430
  463.6 21.2 %collective-permute-start.53 = (bf16[4,96,384]{2,1,0:T(8,128)(2,1)}, bf16[4,96,384]{2,1,0:T(8,128)(2,1)}, u32[]{:S(2)}, u32[]{:S(2)}) collective-permute-start(bf16[4,96,384]{2,1,0:T(8,128)(2,1)} %dynamic-slice_bitcast_fusion.7), channel_id=1, source_target_pairs={{0,4},{4,0},{8,12},{12,8},{16,20},{20,16},{24,28},{28,24},{1,5},{5... | collective-permute-start | bytes 884744 | tf_op jit(solution)/shard_map/ppermute | solution.py:430
  466.3 18.4 %collective-permute-start.54 = (bf16[4,96,384]{2,1,0:T(8,128)(2,1)S(1)}, bf16[4,96,384]{2,1,0:T(8,128)(2,1)S(1)}, u32[]{:S(2)}, u32[]{:S(2)}) collective-permute-start(bf16[4,96,384]{2,1,0:T(8,128)(2,1)S(1)} %dynamic-slice_bitcast_fusion.6), channel_id=1, source_target_pairs={{0,2},{1,3},{2,0},{3,1},{4,6},{5,7},{6,4},{7,5},{8,10},{9,11},{10,... | collective-permute-start | bytes 884744 | tf_op jit(solution)/shard_map/ppermute | solution.py:430
  476.6 51.7 %collective-permute-start.55 = (bf16[4,2,96,768]{3,2,0,1:T(8,128)(2,1)S(1)}, bf16[4,2,96,768]{3,2,0,1:T(8,128)(2,1)}, u32[]{:S(2)}, u32[]{:S(2)}) collective-permute-start(bf16[4,2,96,768]{3,2,0,1:T(8,128)(2,1)S(1)} %fusion.6), channel_id=1, source_target_pairs={{0,2},{1,3},{2,0},{3,1},{4,6},{5,7},{6,4},{7,5},{8,10},{9,11},{10,... | collective-permute-start | bytes 3538952 | tf_op jit(solution)/shard_map/ppermute | solution.py:430
  479.2 51.4 %collective-permute-start.56 = (bf16[2,4,96,768]{3,2,1,0:T(8,128)(2,1)}, bf16[2,4,96,768]{3,2,1,0:T(8,128)(2,1)}, u32[]{:S(2)}, u32[]{:S(2)}) collective-permute-start(bf16[2,4,96,768]{3,2,1,0:T(8,128)(2,1)} %fusion.7.refs_5_), channel_id=1, source_target_pairs={{0,4},{4,0},{8,12},{12,8},{16,20},{20,16},{24,28},{28,24},{1,5},{5... | collective-permute-start | bytes 3538952 | tf_op jit(solution)/shard_map/ppermute | solution.py:430
  521.2 60.6 %collective-permute-start.61 = (bf16[2,768,768]{2,1,0:T(8,128)(2,1)}, bf16[2,768,768]{2,1,0:T(8,128)(2,1)}, u32[]{:S(2)}, u32[]{:S(2)}) collective-permute-start(bf16[2,768,768]{2,1,0:T(8,128)(2,1)} %get-tuple-element.121), channel_id=1, source_target_pairs={{0,1},{1,0},{2,3},{3,2},{4,5},{5,4},{6,7},{7,6},{8,9},{9,8},{10,11... | collective-permute-start | bytes 7077896 | tf_op jit(solution)/shard_map/ppermute | solution.py:430
  553.1 15.1 %collective-permute-start.63 = (bf16[4,96,768]{2,1,0:T(8,128)(2,1)S(1)}, bf16[4,96,768]{2,1,0:T(8,128)(2,1)}, u32[]{:S(2)}, u32[]{:S(2)}) collective-permute-start(bf16[4,96,768]{2,1,0:T(8,128)(2,1)S(1)} %dynamic-slice_bitcast_fusion), channel_id=1, source_target_pairs={{0,2},{1,3},{2,0},{3,1},{4,6},{5,7},{6,4},{7,5},{8,10},{9,11},{10,... | collective-permute-start | bytes 1769480 | tf_op jit(solution)/shard_map/ppermute | solution.py:430
  556.4 15.2 %collective-permute-start.62 = (bf16[4,96,768]{2,1,0:T(8,128)(2,1)}, bf16[4,96,768]{2,1,0:T(8,128)(2,1)S(1)}, u32[]{:S(2)}, u32[]{:S(2)}) collective-permute-start(bf16[4,96,768]{2,1,0:T(8,128)(2,1)} %dynamic-slice_bitcast_fusion.1), channel_id=1, source_target_pairs={{0,4},{4,0},{8,12},{12,8},{16,20},{20,16},{24,28},{28,24},{1,5},{5... | collective-permute-start | bytes 1769480 | tf_op jit(solution)/shard_map/ppermute | solution.py:430
  559.1 41.1 %collective-permute-start.60 = (bf16[512,768]{1,0:T(8,128)(2,1)}, bf16[512,768]{1,0:T(8,128)(2,1)}, u32[]{:S(2)}, u32[]{:S(2)}) collective-permute-start(bf16[512,768]{1,0:T(8,128)(2,1)} %get-tuple-element.118), channel_id=1, source_target_pairs={{1,0},{2,1},{3,2},{5,4},{6,5},{7,6},{9,8},{10,9},{11,10},{13,12},{... | collective-permute-start | bytes 2359304 | tf_op jit(solution)/shard_map/ppermute | solution.py:574
  577.9 18.6 %collective-permute-start.67 = (bf16[96,1536]{1,0:T(8,128)(2,1)S(1)}, bf16[96,1536]{1,0:T(8,128)(2,1)S(1)}, u32[]{:S(2)}, u32[]{:S(2)}) collective-permute-start(bf16[96,1536]{1,0:T(8,128)(2,1)S(1)} %get-tuple-element.200), channel_id=1, source_target_pairs={{0,16},{4,20},{8,24},{12,28},{16,0},{20,4},{24,8},{28,12},{1,17},{... | collective-permute-start | bytes 884744 | tf_op jit(solution)/shard_map/ppermute | solution.py:430
  577.9 18.6 %collective-permute-start.68 = (bf16[96,1536]{1,0:T(8,128)(2,1)S(1)}, bf16[96,1536]{1,0:T(8,128)(2,1)S(1)}, u32[]{:S(2)}, u32[]{:S(2)}) collective-permute-start(bf16[96,1536]{1,0:T(8,128)(2,1)S(1)} %get-tuple-element.198), channel_id=1, source_target_pairs={{0,24},{4,28},{8,0},{12,4},{16,8},{20,12},{24,16},{28,20},{1,25},{... | collective-permute-start | bytes 884744 | tf_op jit(solution)/shard_map/ppermute | solution.py:430
  584.8 22.7 %collective-permute-start.64 = (bf16[4,2,96,384]{3,2,0,1:T(8,128)(2,1)S(1)}, bf16[4,2,96,384]{3,2,0,1:T(8,128)(2,1)S(1)}, u32[]{:S(2)}, u32[]{:S(2)}) collective-permute-start(bf16[4,2,96,384]{3,2,0,1:T(8,128)(2,1)S(1)} %fusion.18), channel_id=1, source_target_pairs={{0,2},{1,3},{2,0},{3,1},{4,6},{5,7},{6,4},{7,5},{8,10},{9,11},{10,... | collective-permute-start | bytes 1769480 | tf_op jit(solution)/shard_map/ppermute | solution.py:430
  586.1 22.2 %collective-permute-start.69 = (bf16[2,4,96,384]{3,2,1,0:T(8,128)(2,1)S(1)}, bf16[2,4,96,384]{3,2,1,0:T(8,128)(2,1)S(1)}, u32[]{:S(2)}, u32[]{:S(2)}) collective-permute-start(bf16[2,4,96,384]{3,2,1,0:T(8,128)(2,1)S(1)} %fusion.19.refs_6_), channel_id=1, source_target_pairs={{0,4},{4,0},{8,12},{12,8},{16,20},{20,16},{24,28},{28,24},{1,5},{5... | collective-permute-start | bytes 1769480 | tf_op jit(solution)/shard_map/ppermute | solution.py:430
  613.3 24.0 %collective-permute-start.65 = (bf16[4,96,384]{2,1,0:T(8,128)(2,1)}, bf16[4,96,384]{2,1,0:T(8,128)(2,1)S(1)}, u32[]{:S(2)}, u32[]{:S(2)}) collective-permute-start(bf16[4,96,384]{2,1,0:T(8,128)(2,1)} %dynamic-slice_bitcast_fusion.5), channel_id=1, source_target_pairs={{0,4},{4,0},{8,12},{12,8},{16,20},{20,16},{24,28},{28,24},{1,5},{5... | collective-permute-start | bytes 884744 | tf_op jit(solution)/shard_map/ppermute | solution.py:430
  618.4 20.6 %collective-permute-start.70 = (bf16[4,96,384]{2,1,0:T(8,128)(2,1)S(1)}, bf16[4,96,384]{2,1,0:T(8,128)(2,1)S(1)}, u32[]{:S(2)}, u32[]{:S(2)}) collective-permute-start(bf16[4,96,384]{2,1,0:T(8,128)(2,1)S(1)} %dynamic-slice_bitcast_fusion.4), channel_id=1, source_target_pairs={{0,2},{1,3},{2,0},{3,1},{4,6},{5,7},{6,4},{7,5},{8,10},{9,11},{10,... | collective-permute-start | bytes 884744 | tf_op jit(solution)/shard_map/ppermute | solution.py:430
  627.7 17.5 %collective-permute-start.79 = (f32[32,768]{1,0:T(8,128)S(1)}, f32[32,768]{1,0:T(8,128)S(1)}, u32[]{:S(2)}, u32[]{:S(2)}) collective-permute-start(f32[32,768]{1,0:T(8,128)S(1)} %add.564), channel_id=1, source_target_pairs={{0,24},{4,28},{8,0},{12,4},{16,8},{20,12},{24,16},{28,20},{1,25},{... | collective-permute-start | bytes 294920 | tf_op jit(solution)/shard_map/ppermute | solution.py:430
  (142 other events, 644.8 us)

commit v4 on v3

--- a/solution.py
+++ b/solution.py
@@ -494,17 +494,14 @@
 
 
 def gather_small(values):
-    deep = lax.axis_size("fsdp") // 2
     x, core, _, y = places()
-    line = gather_line(values)[0]
-
-    def both(value, index, move, axis):
+
+    def both(value, index, move):
         other = move(value)
-        pair = jnp.where(index == 0, jnp.stack([value, other]), jnp.stack([other, value]))
-        return jnp.moveaxis(pair, 0, axis)
-
-    whole = both(both(both(line, y, hop_y, 1), x, hop_x, 2), core, hop_core, 3)
-    return whole.reshape(deep * 8, values.shape[0])
+        return jnp.where(index == 0, jnp.stack([value, other]), jnp.stack([other, value]))
+
+    whole = gather_line(both(both(both(values, core, hop_core), x, hop_x), y, hop_y))[0]
+    return whole.reshape(-1, values.shape[0])
 
 
 def sum_small(values):
@@ -604,7 +601,7 @@
 
     smalls = [norm_gain, norm_shift, attn_bias, up_bias, down_bias]
     packed = jnp.concatenate([part.reshape(-1) for part in smalls])
-    packed_all = gather_small(tie(packed, attn.parts))
+    packed_all = gather_small(packed)
     wholes, at = [], 0
     for part in smalls:
         size, lead, last = part.size, part.shape[:-1], part.shape[-1]
@@ -648,11 +645,12 @@
     feed = Gather(shards[1], attn.parts)
     attn.cross()
     attn.relay()
+    along = feed.parts
     feed.cross(attn.parts)
     for layer in range(layers):
         more = layer + 1 < layers
         if more:
-            next_attn = Gather(shards[2 * layer + 2], feed.parts + attn.parts)
+            next_attn = Gather(shards[2 * layer + 2], along + attn.parts)
         normed = norm_forward(stream, gain_all[layer, 0], shift_all[layer, 0])
         halo = from_previous(normed)
         attn_w = attn.both_cores()
@@ -661,7 +659,8 @@
             [feed.line],
         )
         *kept_other, mid = attend_forward(
-            seg_q, seg_k, halo, normed, attn_w[1], bias_proj[layer, 1], mid, no_row
+            seg_q, seg_k, halo, normed, attn_w[1], bias_proj[layer, 1], mid, no_row,
+            next_attn.parts if more else (),
         )
         feed.relay([mid])
         if more:
@@ -674,7 +673,7 @@
         )
         crossed = []
         if more:
-            crossed = next_attn.parts
+            crossed, along = next_attn.parts + next_feed.parts, next_feed.parts
             next_attn.relay([fed])
             next_feed.cross(next_attn.parts)
         pre_other, fed = feed_forward(
@@ -694,14 +693,16 @@
         attn_w, feed_w = weights[2 * layer], weights[2 * layer + 1]
         stream_in, halo, normed, kept_mine, kept_other, mid, normed_mid, pre_mine, pre_other = saved[layer]
         before_feed, before_attn = (feed_sums[-1], attn_sums[-1]) if feed_sums else (None, None)
-        feed_other, up_other, dn = feed_backward(grad_low, normed_mid, pre_other, feed_w[1], None)
+        feed_other, up_other, dn = feed_backward(
+            grad_low, normed_mid, pre_other, feed_w[1], None, before_feed.parts if before_feed else ()
+        )
         feed_sum = Scatter(feed_other)
         if before_attn:
             crossed = before_attn.parts
             before_attn.cross([dn])
         feed_mine, up_mine, dn = feed_backward(
             grad_low, normed_mid, pre_mine, feed_w[0], dn,
-            before_feed.parts + crossed if before_feed else (),
+            crossed if before_feed else (),
         )
         relayed = []
         if before_attn:

time: 666 us -> 661 us (level)
    unnamed x230 -> x256, local copies, waits for them, and re-layouts: 32.2 us -> 32.6 us
  transfers between devices with their start and end apart: 80 -> 80, of which waited for: 28 -> 29; matrix products, arithmetic and copies ran while one was open for 20% -> 19% of each run, Pallas kernels for 28% -> 30%
where the time goes in v4:
time: 661 us; the launch traced here: 655 us
  Pallas kernels  236 us (36%)
  waiting for transfers between devices  127 us (19%)
  starting transfers between devices  122 us (18%)
  local copies, waits for them, and re-layouts  121 us (18%)
  other arithmetic  45.5 us (7%)
    pallas_call x16, Pallas kernels, call_parts(): pl.pallas_call(skip_deps(body, len(operands), len(deps)), grid=(parts,),...  202 us
    ppermute x76, waiting for transfers between devices, hop(): return lax.ppermute(value, axis, [(i, move(i)) for i in range(count)])  127 us
    ppermute x76, starting transfers between devices, hop(): return lax.ppermute(value, axis, [(i, move(i)) for i in range(count)])  114 us
    pallas_call x9, Pallas kernels, call_whole(): pl.pallas_call(skip_deps(body, len(operands), len(deps)), in_specs=[pl.Bl...  34.1 us
    unnamed x256, local copies, waits for them, and re-layouts  32.6 us
    convert_element_type x24, other arithmetic, add_low(): return sum((value.astype(f32) for value in values)).astype(bf16)  22 us
    dynamic_update_slice x20, local copies, waits for them, and re-layouts, both_cores(): lax.dynamic_update_slice(mine, piece[None, :, None], (at_x, 0, at_y, 0, a...  20.7 us
    slice x8, local copies, waits for them, and re-layouts, keep(): part[..., half:]  14.7 us
  transfers between devices with their start and end apart: 80, of which 29 were waited for; matrix products, arithmetic and copies ran while one was open for 19% of the time, Pallas kernels for 30%

profile of v4, /device:TPU:0, one launch (start us, length us, event | category | flops | bytes accessed | tf_op | source)
XLA Modules:
  0.0 654.8 jit_solution(15630799026187088468)
XLA Ops:
  4.4 3.1 collective-permute-start.7
  26.9 4.6 collective-permute-done.3
  31.5 3.7 collective-permute-done.5
  51.4 8.2 %collective-permute-done.11 = bf16[4,96,768]{2,1,0:T(8,128)(2,1)S(1)} collective-permute-done((bf16[4,96,768]{2,1,0:T(8,128)(2,1)S(1)}, bf16[4,96,768]{2,1,0:T(8,128)(2,1)S(1)}, u32[]{:S(2)}, u32[]{:S(2)}) %collective-permute-start.11) | collective-permute-done | bytes 589856 | tf_op jit(solution)/shard_map/ppermute | solution.py:430
  64.5 4.2 collective-permute-done.12.refs_1_.refs_4_
  72.1 3.8 collective-permute-start.14
  84.9 3.3 collective-permute-start.19
  91.5 12.6 %attend_forward.4 = (bf16[2,1024,640]{2,1,0:T(8,128)(2,1)}, bf16[2,512,256]{2,1,0:T(8,128)(2,1)}, f32[2,512,256]{2,1,0:T(8,128)}, f32[512,768]{1,0:T(8,128)}) custom-call(s32[512,1]{1,0:T(8,128)} %copy.285.refs_0_, s32[1,1024]{1,0:T(1,128)} %compare_select_fusion.refs_1_, bf16[512,768]{1,0:T(8,128)(2,1)} %collective-permute-done.6.refs_2_.refs_3_, ...), custom_call_target="tpu_custom_call" | custom-call | flops 4294967296 | bytes 1000 | tf_op jit(solution)/shard_map/attend_forward/pallas_call | solution.py:209
  104.8 12.6 %attend_forward.5 = (bf16[2,1024,640]{2,1,0:T(8,128)(2,1)}, bf16[2,512,256]{2,1,0:T(8,128)(2,1)}, f32[2,512,256]{2,1,0:T(8,128)}, f32[512,768]{1,0:T(8,128)}) custom-call(s32[512,1]{1,0:T(8,128)} %copy.285.refs_0_, s32[1,1024]{1,0:T(1,128)} %compare_select_fusion.refs_1_, bf16[512,768]{1,0:T(8,128)(2,1)} %collective-permute-done.6.refs_2_.refs_3_, ...), custom_call_target="tpu_custom_call" | custom-call | flops 4294967296 | bytes 1000 | tf_op jit(solution)/shard_map/attend_forward/pallas_call | solution.py:209
  125.6 9.7 %collective-permute-done.23.refs_1_ = bf16[4,96,768]{2,1,0:T(8,128)(2,1)S(1)} collective-permute-done((bf16[4,96,768]{2,1,0:T(8,128)(2,1)S(1)}, bf16[4,96,768]{2,1,0:T(8,128)(2,1)S(1)}, u32[]{:S(2)}, u32[]{:S(2)}) %collective-permute-start.23) | collective-permute-done | bytes 589856 | tf_op jit(solution)/shard_map/ppermute | solution.py:430
  149.7 5.8 collective-permute-done.28.refs_7_
  156.0 6.8 %feed_forward.4 = (f32[2,512,768]{2,1,0:T(8,128)}, f32[512,768]{1,0:T(8,128)}) custom-call(bf16[512,768]{1,0:T(8,128)(2,1)} %norm_forward.5.refs_0_.refs_1_.refs_4_, bf16[2,768,1536]{2,1,0:T(8,128)(2,1)} %bitcast.458, f32[2,1,768]{2,1,0:T(1,128)} %get-tuple-element.287.refs_2_, f32[512,768]{1,0:T(8,128)} %get-tuple-element.75.refs_0_.refs_1_.refs_3_.refs_4_, ...), custom_call_target="tpu_custom_call" | custom-call | flops 2415919104 | bytes 1000 | tf_op jit(solution)/shard_map/feed_forward/pallas_call | solution.py:209
  170.6 6.8 %feed_forward.5 = (f32[2,512,768]{2,1,0:T(8,128)}, f32[512,768]{1,0:T(8,128)}) custom-call(bf16[512,768]{1,0:T(8,128)(2,1)} %norm_forward.5.refs_0_.refs_1_.refs_4_, bf16[2,768,1536]{2,1,0:T(8,128)(2,1)} %collective-permute-done.25.refs_1_.refs_3_, f32[2,1,768]{2,1,0:T(1,128)} %get-tuple-element.288.refs_2_, f32[512,768]{1,0:T(8,128)} %get-tuple-element.76.refs_3_.refs_1_, ...), custom_call_target="tpu_custom_call" | custom-call | flops 2415919104 | bytes 1000 | tf_op jit(solution)/shard_map/feed_forward/pallas_call | solution.py:209
  201.1 12.6 %attend_forward.6 = (bf16[2,1024,640]{2,1,0:T(8,128)(2,1)}, bf16[2,512,256]{2,1,0:T(8,128)(2,1)}, f32[2,512,256]{2,1,0:T(8,128)}, f32[512,768]{1,0:T(8,128)}) custom-call(s32[512,1]{1,0:T(8,128)} %copy.285.refs_0_, s32[1,1024]{1,0:T(1,128)} %compare_select_fusion.refs_1_, bf16[512,768]{1,0:T(8,128)(2,1)} %copy-done.120, ...), custom_call_target="tpu_custom_call" | custom-call | flops 4294967296 | bytes 1000 | tf_op jit(solution)/shard_map/attend_forward/pallas_call | solution.py:209
  213.7 12.6 %attend_forward.7 = (bf16[2,1024,640]{2,1,0:T(8,128)(2,1)}, bf16[2,512,256]{2,1,0:T(8,128)(2,1)}, f32[2,512,256]{2,1,0:T(8,128)}, f32[512,768]{1,0:T(8,128)}) custom-call(s32[512,1]{1,0:T(8,128)} %copy.285.refs_0_, s32[1,1024]{1,0:T(1,128)} %compare_select_fusion.refs_1_, bf16[512,768]{1,0:T(8,128)(2,1)} %copy-done.120, ...), custom_call_target="tpu_custom_call" | custom-call | flops 4294967296 | bytes 1000 | tf_op jit(solution)/shard_map/attend_forward/pallas_call | solution.py:209
  228.5 13.1 %collective-permute-start.37 = (bf16[4,96,768]{2,1,0:T(8,128)(2,1)S(1)}, bf16[4,96,768]{2,1,0:T(8,128)(2,1)S(1)}, u32[]{:S(2)}, u32[]{:S(2)}) collective-permute-start(bf16[4,96,768]{2,1,0:T(8,128)(2,1)S(1)} %slice.617), channel_id=1, source_target_pairs={{0,2},{1,3},{2,0},{3,1},{4,6},{5,7},{6,4},{7,5},{8,10},{9,11},{10,... | collective-permute-start | bytes 1769480 | tf_op jit(solution)/shard_map/ppermute | solution.py:430
  247.5 7.0 %collective-permute-done.37 = bf16[4,96,768]{2,1,0:T(8,128)(2,1)S(1)} collective-permute-done((bf16[4,96,768]{2,1,0:T(8,128)(2,1)S(1)}, bf16[4,96,768]{2,1,0:T(8,128)(2,1)S(1)}, u32[]{:S(2)}, u32[]{:S(2)}) %collective-permute-start.37) | collective-permute-done | bytes 589856 | tf_op jit(solution)/shard_map/ppermute | solution.py:430
  262.7 6.8 %feed_forward.6 = (f32[2,512,768]{2,1,0:T(8,128)}, f32[512,768]{1,0:T(8,128)}) custom-call(bf16[512,768]{1,0:T(8,128)(2,1)} %norm_forward.7.refs_0_.refs_1_.refs_4_, bf16[2,768,1536]{2,1,0:T(8,128)(2,1)} %bitcast.455, f32[2,1,768]{2,1,0:T(1,128)} %get-tuple-element.285.refs_2_, f32[512,768]{1,0:T(8,128)} %get-tuple-element.79.refs_0_.refs_1_.refs_3_, ...), custom_call_target="tpu_custom_call" | custom-call | flops 2415919104 | bytes 1000 | tf_op jit(solution)/shard_map/feed_forward/pallas_call | solution.py:209
  269.5 7.0 %feed_forward.7 = (f32[2,512,768]{2,1,0:T(8,128)}, f32[512,768]{1,0:T(8,128)}) custom-call(bf16[512,768]{1,0:T(8,128)(2,1)} %norm_forward.7.refs_0_.refs_1_.refs_4_, bf16[2,768,1536]{2,1,0:T(8,128)(2,1)} %collective-permute-done.39.refs_1_.refs_3_, f32[2,1,768]{2,1,0:T(1,128)} %get-tuple-element.286.refs_2_, f32[512,768]{1,0:T(8,128)} %get-tuple-element.80.refs_3_, ...), custom_call_target="tpu_custom_call" | custom-call | flops 2415919104 | bytes 1000 | tf_op jit(solution)/shard_map/feed_forward/pallas_call | solution.py:209
  276.4 11.4 %feed_backward.4 = (bf16[2,768,1536]{2,1,0:T(8,128)(2,1)}, f32[2,1,768]{2,1,0:T(1,128)}, f32[512,768]{1,0:T(8,128)}) custom-call(bf16[512,768]{1,0:T(8,128)(2,1)} %refs_0_.3, bf16[512,768]{1,0:T(8,128)(2,1)} %norm_forward.7.refs_0_.refs_1_.refs_4_, f32[2,512,768]{2,1,0:T(8,128)} %get-tuple-element.83.refs_2_, ...), custom_call_target="tpu_custom_call" | custom-call | flops 3758096384 | bytes 1000 | tf_op jit(solution)/shard_map/feed_backward/pallas_call | solution.py:209
  288.4 10.7 %feed_backward.5 = (bf16[2,768,1536]{2,1,0:T(8,128)(2,1)}, f32[2,1,768]{2,1,0:T(1,128)}, f32[512,768]{1,0:T(8,128)}) custom-call(bf16[512,768]{1,0:T(8,128)(2,1)} %refs_0_.3, bf16[512,768]{1,0:T(8,128)(2,1)} %norm_forward.7.refs_0_.refs_1_.refs_4_, f32[2,512,768]{2,1,0:T(8,128)} %get-tuple-element.82.refs_2_, bf16[2,768,1536]{2,1,0:T(8,128)(2,1)} %bitcast.456, ...), custom_call_target="tpu_custom_call" | custom-call | flops 3758096384 | bytes 1000 | tf_op jit(solution)/shard_map/feed_backward/pallas_call | solution.py:209
  314.2 4.9 norm_backward.4
  319.1 19.5 %attend_backward.4 = (bf16[2,768,768]{2,1,0:T(8,128)(2,1)}, f32[2,1,768]{2,1,0:T(1,128)}, f32[1024,768]{1,0:T(8,128)}, bf16[512,768]{1,0:T(8,128)(2,1)}) custom-call(s32[1,512]{1,0:T(1,128)} %bitcast.489, s32[1024,1]{1,0:T(8,128)} %fusion.28.refs_1_, bf16[512,768]{1,0:T(8,128)(2,1)} %get-tuple-element.88.refs_2_, bf16[512,768]{1,0:T(8,128)(2,1)} %copy-done.120, ...), custom_call_target="tpu_custom_call" | custom-call | flops 6979321856 | bytes 1000 | tf_op jit(solution)/shard_map/attend_backward/pallas_call | solution.py:209
  341.0 20.5 %attend_backward.5 = (bf16[2,768,768]{2,1,0:T(8,128)(2,1)}, f32[2,1,768]{2,1,0:T(1,128)}, f32[1024,768]{1,0:T(8,128)}, bf16[512,768]{1,0:T(8,128)(2,1)}) custom-call(s32[1,512]{1,0:T(1,128)} %bitcast.491, s32[1024,1]{1,0:T(8,128)} %fusion.28.refs_1_, bf16[512,768]{1,0:T(8,128)(2,1)} %get-tuple-element.88.refs_2_, bf16[512,768]{1,0:T(8,128)(2,1)} %copy-done.120, ...), custom_call_target="tpu_custom_call" | custom-call | flops 6979321856 | bytes 1000 | tf_op jit(solution)/shard_map/attend_backward/pallas_call | solution.py:209
  373.6 7.0 %collective-permute-done.46.refs_0_ = bf16[4,96,768]{2,1,0:T(8,128)(2,1)S(1)} collective-permute-done((bf16[4,96,768]{2,1,0:T(8,128)(2,1)}, bf16[4,96,768]{2,1,0:T(8,128)(2,1)S(1)}, u32[]{:S(2)}, u32[]{:S(2)}) %collective-permute-start.46) | collective-permute-done | bytes 589856 | tf_op jit(solution)/shard_map/ppermute | solution.py:430
  386.1 5.7 collective-permute-start.47
  400.4 5.7 norm_backward.5
  406.1 4.6 collective-permute-done.48.refs_6_
  411.6 11.6 %feed_backward.6 = (bf16[2,768,1536]{2,1,0:T(8,128)(2,1)}, f32[2,1,768]{2,1,0:T(1,128)}, f32[512,768]{1,0:T(8,128)}) custom-call(bf16[512,768]{1,0:T(8,128)(2,1)} %get-tuple-element.101.refs_0_, bf16[512,768]{1,0:T(8,128)(2,1)} %norm_forward.5.refs_0_.refs_1_.refs_4_, f32[2,512,768]{2,1,0:T(8,128)} %get-tuple-element.103.refs_2_, ...), custom_call_target="tpu_custom_call" | custom-call | flops 3758096384 | bytes 1000 | tf_op jit(solution)/shard_map/feed_backward/pallas_call | solution.py:209
  430.9 8.4 %collective-permute-done.50 = bf16[4,2,96,384]{3,2,0,1:T(8,128)(2,1)} collective-permute-done((bf16[4,2,96,384]{3,2,0,1:T(8,128)(2,1)}, bf16[4,2,96,384]{3,2,0,1:T(8,128)(2,1)}, u32[]{:S(2)}, u32[]{:S(2)}) %collective-permute-start.50) | collective-permute-done | bytes 589856 | tf_op jit(solution)/shard_map/ppermute | solution.py:430
  441.3 10.6 %feed_backward.7 = (bf16[2,768,1536]{2,1,0:T(8,128)(2,1)}, f32[2,1,768]{2,1,0:T(1,128)}, f32[512,768]{1,0:T(8,128)}) custom-call(bf16[512,768]{1,0:T(8,128)(2,1)} %get-tuple-element.101.refs_0_, bf16[512,768]{1,0:T(8,128)(2,1)} %norm_forward.5.refs_0_.refs_1_.refs_4_, f32[2,512,768]{2,1,0:T(8,128)} %get-tuple-element.102.refs_2_, ...), custom_call_target="tpu_custom_call" | custom-call | flops 3758096384 | bytes 1000 | tf_op jit(solution)/shard_map/feed_backward/pallas_call | solution.py:209
  472.2 4.9 norm_backward.6
  477.9 19.6 %attend_backward.6 = (bf16[2,768,768]{2,1,0:T(8,128)(2,1)}, f32[2,1,768]{2,1,0:T(1,128)}, f32[1024,768]{1,0:T(8,128)}, bf16[512,768]{1,0:T(8,128)(2,1)}) custom-call(s32[1,512]{1,0:T(1,128)} %bitcast.492, s32[1024,1]{1,0:T(8,128)} %fusion.28.refs_1_, bf16[512,768]{1,0:T(8,128)(2,1)} %get-tuple-element.109.refs_2_, ...), custom_call_target="tpu_custom_call" | custom-call | flops 6979321856 | bytes 1000 | tf_op jit(solution)/shard_map/attend_backward/pallas_call | solution.py:209
  501.5 6.7 %collective-permute-start.57 = (bf16[96,768]{1,0:T(8,128)(2,1)S(1)}, bf16[96,768]{1,0:T(8,128)(2,1)S(1)}, u32[]{:S(2)}, u32[]{:S(2)}) collective-permute-start(bf16[96,768]{1,0:T(8,128)(2,1)S(1)} %get-tuple-element.233), channel_id=1, source_target_pairs={{0,8},{4,12},{8,16},{12,20},{16,24},{20,28},{24,0},{28,4},{1,9},{5... | collective-permute-start | bytes 442376 | tf_op jit(solution)/shard_map/ppermute | solution.py:430
  508.3 3.1 collective-permute-start.58
  512.2 3.4 collective-permute-done.57.refs_12_
  515.7 4.1 collective-permute-done.58.refs_13_
  524.9 20.4 %attend_backward.7 = (bf16[2,768,768]{2,1,0:T(8,128)(2,1)}, f32[2,1,768]{2,1,0:T(1,128)}, f32[1024,768]{1,0:T(8,128)}, bf16[512,768]{1,0:T(8,128)(2,1)}) custom-call(s32[1,512]{1,0:T(1,128)} %bitcast.494, s32[1024,1]{1,0:T(8,128)} %fusion.28.refs_1_, bf16[512,768]{1,0:T(8,128)(2,1)} %get-tuple-element.109.refs_2_, ...), custom_call_target="tpu_custom_call" | custom-call | flops 6979321856 | bytes 1000 | tf_op jit(solution)/shard_map/attend_backward/pallas_call | solution.py:209
  556.1 6.7 %collective-permute-done.63.refs_0_ = bf16[4,96,768]{2,1,0:T(8,128)(2,1)} collective-permute-done((bf16[4,96,768]{2,1,0:T(8,128)(2,1)S(1)}, bf16[4,96,768]{2,1,0:T(8,128)(2,1)}, u32[]{:S(2)}, u32[]{:S(2)}) %collective-permute-start.63) | collective-permute-done | bytes 589856 | tf_op jit(solution)/shard_map/ppermute | solution.py:430
  562.8 3.3 collective-permute-done.62.refs_0_
  568.8 3.8 collective-permute-start.66
  582.2 9.1 %collective-permute-done.67.refs_2_ = bf16[96,1536]{1,0:T(8,128)(2,1)S(1)} collective-permute-done((bf16[96,1536]{1,0:T(8,128)(2,1)S(1)}, bf16[96,1536]{1,0:T(8,128)(2,1)S(1)}, u32[]{:S(2)}, u32[]{:S(2)}) %collective-permute-start.67) | collective-permute-done | bytes 294944 | tf_op jit(solution)/shard_map/ppermute | solution.py:430
  595.0 5.7 norm_backward.7
  614.1 3.5 collective-permute-done.75
  619.1 3.2 collective-permute-done.76
  622.3 8.9 %collective-permute-start.79 = (f32[32,768]{1,0:T(8,128)S(1)}, f32[32,768]{1,0:T(8,128)S(1)}, u32[]{:S(2)}, u32[]{:S(2)}) collective-permute-start(f32[32,768]{1,0:T(8,128)S(1)} %add.564), channel_id=1, source_target_pairs={{0,24},{4,28},{8,0},{12,4},{16,8},{20,12},{24,16},{28,20},{1,25},{... | collective-permute-start | bytes 294920 | tf_op jit(solution)/shard_map/ppermute | solution.py:430
  635.4 3.2 collective-permute-start.73
  643.2 7.8 %collective-permute-done.72 = bf16[96,768]{1,0:T(8,128)(2,1)S(1)} collective-permute-done((bf16[96,768]{1,0:T(8,128)(2,1)S(1)}, bf16[96,768]{1,0:T(8,128)(2,1)S(1)}, u32[]{:S(2)}, u32[]{:S(2)}) %collective-permute-start.72) | collective-permute-done | bytes 147488 | tf_op jit(solution)/shard_map/ppermute | solution.py:430
  (700 shorter events, 268.9 us)
Async XLA Ops:
  4.4 38.3 %collective-permute-start.7 = (bf16[96,768]{1,0:T(8,128)(2,1)S(1)}, bf16[96,768]{1,0:T(8,128)(2,1)S(1)}, u32[]{:S(2)}, u32[]{:S(2)}) collective-permute-start(bf16[96,768]{1,0:T(8,128)(2,1)S(1)} %concatenate.151), channel_id=1, source_target_pairs={{0,8},{4,12},{8,16},{12,20},{16,24},{20,28},{24,0},{28,4},{1,9},{5... | collective-permute-start | bytes 442376 | tf_op jit(solution)/shard_map/ppermute | solution.py:430
  7.5 35.3 %collective-permute-start.8 = (bf16[96,768]{1,0:T(8,128)(2,1)S(1)}, bf16[96,768]{1,0:T(8,128)(2,1)S(1)}, u32[]{:S(2)}, u32[]{:S(2)}) collective-permute-start(bf16[96,768]{1,0:T(8,128)(2,1)S(1)} %concatenate.151), channel_id=1, source_target_pairs={{0,16},{4,20},{8,24},{12,28},{16,0},{20,4},{24,8},{28,12},{1,17},{... | collective-permute-start | bytes 442376 | tf_op jit(solution)/shard_map/ppermute | solution.py:430
  10.1 32.7 %collective-permute-start.9 = (bf16[96,768]{1,0:T(8,128)(2,1)S(1)}, bf16[96,768]{1,0:T(8,128)(2,1)S(1)}, u32[]{:S(2)}, u32[]{:S(2)}) collective-permute-start(bf16[96,768]{1,0:T(8,128)(2,1)S(1)} %concatenate.151), channel_id=1, source_target_pairs={{0,24},{4,28},{8,0},{12,4},{16,8},{20,12},{24,16},{28,20},{1,25},{... | collective-permute-start | bytes 442376 | tf_op jit(solution)/shard_map/ppermute | solution.py:430
  40.6 44.3 %collective-permute-start.6 = (bf16[512,768]{1,0:T(8,128)(2,1)}, bf16[512,768]{1,0:T(8,128)(2,1)}, u32[]{:S(2)}, u32[]{:S(2)}) collective-permute-start(bf16[512,768]{1,0:T(8,128)(2,1)} %norm_forward.4.refs_3_.refs_4_), channel_id=1, source_target_pairs={{0,1},{1,2},{2,3},{4,5},{5,6},{6,7},{8,9},{9,10},{10,11},{12,13},{... | collective-permute-start | bytes 2359304 | tf_op jit(solution)/shard_map/ppermute | solution.py:566
  42.9 18.3 %collective-permute-start.10 = (bf16[4,96,768]{2,1,0:T(8,128)(2,1)S(1)}, bf16[4,96,768]{2,1,0:T(8,128)(2,1)S(1)}, u32[]{:S(2)}, u32[]{:S(2)}) collective-permute-start(bf16[4,96,768]{2,1,0:T(8,128)(2,1)S(1)} %bitcast_dynamic-update-slice_fusion.32), channel_id=1, source_target_pairs={{0,2},{1,3},{2,0},{3,1},{4,6},{5,7},{6,4},{7,5},{8,10},{9,11},{10,... | collective-permute-start | bytes 1769480 | tf_op jit(solution)/shard_map/ppermute | solution.py:430
  44.2 15.4 %collective-permute-start.11 = (bf16[4,96,768]{2,1,0:T(8,128)(2,1)S(1)}, bf16[4,96,768]{2,1,0:T(8,128)(2,1)S(1)}, u32[]{:S(2)}, u32[]{:S(2)}) collective-permute-start(bf16[4,96,768]{2,1,0:T(8,128)(2,1)S(1)} %bitcast_dynamic-update-slice_fusion.32), channel_id=1, source_target_pairs={{0,4},{4,0},{8,12},{12,8},{16,20},{20,16},{24,28},{28,24},{1,5},{5... | collective-permute-start | bytes 1769480 | tf_op jit(solution)/shard_map/ppermute | solution.py:430
  46.5 29.4 %collective-permute-start.15 = (bf16[96,1536]{1,0:T(8,128)(2,1)}, bf16[96,1536]{1,0:T(8,128)(2,1)S(1)}, u32[]{:S(2)}, u32[]{:S(2)}) collective-permute-start(bf16[96,1536]{1,0:T(8,128)(2,1)} %tie.29), channel_id=1, source_target_pairs={{0,8},{4,12},{8,16},{12,20},{16,24},{20,28},{24,0},{28,4},{1,9},{5... | collective-permute-start | bytes 884744 | tf_op jit(solution)/shard_map/ppermute | solution.py:430
  46.6 29.4 %collective-permute-start.16 = (bf16[96,1536]{1,0:T(8,128)(2,1)}, bf16[96,1536]{1,0:T(8,128)(2,1)S(1)}, u32[]{:S(2)}, u32[]{:S(2)}) collective-permute-start(bf16[96,1536]{1,0:T(8,128)(2,1)} %tie.29), channel_id=1, source_target_pairs={{0,16},{4,20},{8,24},{12,28},{16,0},{20,4},{24,8},{28,12},{1,17},{... | collective-permute-start | bytes 884744 | tf_op jit(solution)/shard_map/ppermute | solution.py:430
  72.1 32.1 %collective-permute-start.14 = (bf16[2,768,768]{2,1,0:T(8,128)(2,1)}, bf16[2,768,768]{2,1,0:T(8,128)(2,1)}, u32[]{:S(2)}, u32[]{:S(2)}) collective-permute-start(bf16[2,768,768]{2,1,0:T(8,128)(2,1)} %bitcast.37.refs_4_.refs_5_), channel_id=1, source_target_pairs={{0,1},{1,0},{2,3},{3,2},{4,5},{5,4},{6,7},{7,6},{8,9},{9,8},{10,11... | collective-permute-start | bytes 7077896 | tf_op jit(solution)/shard_map/ppermute | solution.py:430
  77.3 42.3 %collective-permute-start.21 = (bf16[4,96,1536]{2,1,0:T(8,128)(2,1)}, bf16[4,96,1536]{2,1,0:T(8,128)(2,1)S(1)}, u32[]{:S(2)}, u32[]{:S(2)}) collective-permute-start(bf16[4,96,1536]{2,1,0:T(8,128)(2,1)} %tie.30.refs_8_), channel_id=1, source_target_pairs={{0,2},{1,3},{2,0},{3,1},{4,6},{5,7},{6,4},{7,5},{8,10},{9,11},{10,... | collective-permute-start | bytes 3538952 | tf_op jit(solution)/shard_map/ppermute | solution.py:430
  79.8 37.6 %collective-permute-start.22 = (bf16[4,96,1536]{2,1,0:T(8,128)(2,1)}, bf16[4,96,1536]{2,1,0:T(8,128)(2,1)S(1)}, u32[]{:S(2)}, u32[]{:S(2)}) collective-permute-start(bf16[4,96,1536]{2,1,0:T(8,128)(2,1)} %tie.30.refs_8_), channel_id=1, source_target_pairs={{0,4},{4,0},{8,12},{12,8},{16,20},{20,16},{24,28},{28,24},{1,5},{5... | collective-permute-start | bytes 3538952 | tf_op jit(solution)/shard_map/ppermute | solution.py:430
  84.9 19.2 %collective-permute-start.19 = (bf16[96,768]{1,0:T(8,128)(2,1)S(1)}, bf16[96,768]{1,0:T(8,128)(2,1)S(1)}, u32[]{:S(2)}, u32[]{:S(2)}) collective-permute-start(bf16[96,768]{1,0:T(8,128)(2,1)S(1)} %copy-done.63), channel_id=1, source_target_pairs={{0,16},{4,20},{8,24},{12,28},{16,0},{20,4},{24,8},{28,12},{1,17},{... | collective-permute-start | bytes 442376 | tf_op jit(solution)/shard_map/ppermute | solution.py:430
  119.6 15.7 %collective-permute-start.23 = (bf16[4,96,768]{2,1,0:T(8,128)(2,1)S(1)}, bf16[4,96,768]{2,1,0:T(8,128)(2,1)S(1)}, u32[]{:S(2)}, u32[]{:S(2)}) collective-permute-start(bf16[4,96,768]{2,1,0:T(8,128)(2,1)S(1)} %slice.601), channel_id=1, source_target_pairs={{0,2},{1,3},{2,0},{3,1},{4,6},{5,7},{6,4},{7,5},{8,10},{9,11},{10,... | collective-permute-start | bytes 1769480 | tf_op jit(solution)/shard_map/ppermute | solution.py:430
  123.2 15.7 %collective-permute-start.24 = (bf16[4,96,768]{2,1,0:T(8,128)(2,1)S(1)}, bf16[4,96,768]{2,1,0:T(8,128)(2,1)S(1)}, u32[]{:S(2)}, u32[]{:S(2)}) collective-permute-start(bf16[4,96,768]{2,1,0:T(8,128)(2,1)S(1)} %slice.602), channel_id=1, source_target_pairs={{0,4},{4,0},{8,12},{12,8},{16,20},{20,16},{24,28},{28,24},{1,5},{5... | collective-permute-start | bytes 1769480 | tf_op jit(solution)/shard_map/ppermute | solution.py:430
  139.9 29.6 %collective-permute-start.25 = (bf16[2,768,1536]{2,1,0:T(8,128)(2,1)}, bf16[2,768,1536]{2,1,0:T(8,128)(2,1)}, u32[]{:S(2)}, u32[]{:S(2)}) collective-permute-start(bf16[2,768,1536]{2,1,0:T(8,128)(2,1)} %bitcast.457), channel_id=1, source_target_pairs={{0,1},{1,0},{2,3},{3,2},{4,5},{5,4},{6,7},{7,6},{8,9},{9,8},{10,11... | collective-permute-start | bytes 14155784 | tf_op jit(solution)/shard_map/ppermute | solution.py:430
  143.6 23.6 %collective-permute-start.29 = (bf16[96,1536]{1,0:T(8,128)(2,1)}, bf16[96,1536]{1,0:T(8,128)(2,1)S(1)}, u32[]{:S(2)}, u32[]{:S(2)}) collective-permute-start(bf16[96,1536]{1,0:T(8,128)(2,1)} %tie.35), channel_id=1, source_target_pairs={{0,16},{4,20},{8,24},{12,28},{16,0},{20,4},{24,8},{28,12},{1,17},{... | collective-permute-start | bytes 884744 | tf_op jit(solution)/shard_map/ppermute | solution.py:430
  144.5 25.0 %collective-permute-start.26 = (bf16[4,96,768]{2,1,0:T(8,128)(2,1)}, bf16[4,96,768]{2,1,0:T(8,128)(2,1)S(1)}, u32[]{:S(2)}, u32[]{:S(2)}) collective-permute-start(bf16[4,96,768]{2,1,0:T(8,128)(2,1)} %tie.34), channel_id=1, source_target_pairs={{0,2},{1,3},{2,0},{3,1},{4,6},{5,7},{6,4},{7,5},{8,10},{9,11},{10,... | collective-permute-start | bytes 1769480 | tf_op jit(solution)/shard_map/ppermute | solution.py:430
  146.2 23.2 %collective-permute-start.27 = (bf16[4,96,768]{2,1,0:T(8,128)(2,1)}, bf16[4,96,768]{2,1,0:T(8,128)(2,1)S(1)}, u32[]{:S(2)}, u32[]{:S(2)}) collective-permute-start(bf16[4,96,768]{2,1,0:T(8,128)(2,1)} %tie.34), channel_id=1, source_target_pairs={{0,4},{4,0},{8,12},{12,8},{16,20},{20,16},{24,28},{28,24},{1,5},{5... | collective-permute-start | bytes 1769480 | tf_op jit(solution)/shard_map/ppermute | solution.py:430
  190.1 23.6 %collective-permute-start.34 = (bf16[2,768,768]{2,1,0:T(8,128)(2,1)}, bf16[2,768,768]{2,1,0:T(8,128)(2,1)}, u32[]{:S(2)}, u32[]{:S(2)}) collective-permute-start(bf16[2,768,768]{2,1,0:T(8,128)(2,1)} %bitcast.93.refs_4_.refs_5_), channel_id=1, source_target_pairs={{0,1},{1,0},{2,3},{3,2},{4,5},{5,4},{6,7},{7,6},{8,9},{9,8},{10,11... | collective-permute-start | bytes 7077896 | tf_op jit(solution)/shard_map/ppermute | solution.py:430
  196.6 45.0 %collective-permute-start.35 = (bf16[4,96,1536]{2,1,0:T(8,128)(2,1)}, bf16[4,96,1536]{2,1,0:T(8,128)(2,1)S(1)}, u32[]{:S(2)}, u32[]{:S(2)}) collective-permute-start(bf16[4,96,1536]{2,1,0:T(8,128)(2,1)} %tie.38.refs_8_), channel_id=1, source_target_pairs={{0,2},{1,3},{2,0},{3,1},{4,6},{5,7},{6,4},{7,5},{8,10},{9,11},{10,... | collective-permute-start | bytes 3538952 | tf_op jit(solution)/shard_map/ppermute | solution.py:430
  196.9 29.5 %collective-permute-start.36 = (bf16[4,96,1536]{2,1,0:T(8,128)(2,1)}, bf16[4,96,1536]{2,1,0:T(8,128)(2,1)S(1)}, u32[]{:S(2)}, u32[]{:S(2)}) collective-permute-start(bf16[4,96,1536]{2,1,0:T(8,128)(2,1)} %tie.38.refs_8_), channel_id=1, source_target_pairs={{0,4},{4,0},{8,12},{12,8},{16,20},{20,16},{24,28},{28,24},{1,5},{5... | collective-permute-start | bytes 3538952 | tf_op jit(solution)/shard_map/ppermute | solution.py:430
  228.5 26.1 %collective-permute-start.37 = (bf16[4,96,768]{2,1,0:T(8,128)(2,1)S(1)}, bf16[4,96,768]{2,1,0:T(8,128)(2,1)S(1)}, u32[]{:S(2)}, u32[]{:S(2)}) collective-permute-start(bf16[4,96,768]{2,1,0:T(8,128)(2,1)S(1)} %slice.617), channel_id=1, source_target_pairs={{0,2},{1,3},{2,0},{3,1},{4,6},{5,7},{6,4},{7,5},{8,10},{9,11},{10,... | collective-permute-start | bytes 1769480 | tf_op jit(solution)/shard_map/ppermute | solution.py:430
  305.3 33.3 %collective-permute-start.41 = (bf16[4,2,96,768]{3,2,0,1:T(8,128)(2,1)S(1)}, bf16[4,2,96,768]{3,2,0,1:T(8,128)(2,1)}, u32[]{:S(2)}, u32[]{:S(2)}) collective-permute-start(bf16[4,2,96,768]{3,2,0,1:T(8,128)(2,1)S(1)} %fusion.4), channel_id=1, source_target_pairs={{0,2},{1,3},{2,0},{3,1},{4,6},{5,7},{6,4},{7,5},{8,10},{9,11},{10,... | collective-permute-start | bytes 3538952 | tf_op jit(solution)/shard_map/ppermute | solution.py:430
  308.4 32.6 %collective-permute-start.42 = (bf16[2,4,96,768]{3,2,1,0:T(8,128)(2,1)}, bf16[2,4,96,768]{3,2,1,0:T(8,128)(2,1)}, u32[]{:S(2)}, u32[]{:S(2)}) collective-permute-start(bf16[2,4,96,768]{3,2,1,0:T(8,128)(2,1)} %fusion.5.refs_5_), channel_id=1, source_target_pairs={{0,4},{4,0},{8,12},{12,8},{16,20},{20,16},{24,28},{28,24},{1,5},{5... | collective-permute-start | bytes 3538952 | tf_op jit(solution)/shard_map/ppermute | solution.py:430
  338.5 56.8 %collective-permute-start.44 = (bf16[2,768,768]{2,1,0:T(8,128)(2,1)}, bf16[2,768,768]{2,1,0:T(8,128)(2,1)}, u32[]{:S(2)}, u32[]{:S(2)}) collective-permute-start(bf16[2,768,768]{2,1,0:T(8,128)(2,1)} %get-tuple-element.100), channel_id=1, source_target_pairs={{0,1},{1,0},{2,3},{3,2},{4,5},{5,4},{6,7},{7,6},{8,9},{9,8},{10,11... | collective-permute-start | bytes 7077896 | tf_op jit(solution)/shard_map/ppermute | solution.py:430
  364.7 15.9 %collective-permute-start.46 = (bf16[4,96,768]{2,1,0:T(8,128)(2,1)}, bf16[4,96,768]{2,1,0:T(8,128)(2,1)S(1)}, u32[]{:S(2)}, u32[]{:S(2)}) collective-permute-start(bf16[4,96,768]{2,1,0:T(8,128)(2,1)} %dynamic-slice_bitcast_fusion.2), channel_id=1, source_target_pairs={{0,2},{1,3},{2,0},{3,1},{4,6},{5,7},{6,4},{7,5},{8,10},{9,11},{10,... | collective-permute-start | bytes 1769480 | tf_op jit(solution)/shard_map/ppermute | solution.py:430
  367.7 15.9 %collective-permute-start.45 = (bf16[4,96,768]{2,1,0:T(8,128)(2,1)}, bf16[4,96,768]{2,1,0:T(8,128)(2,1)S(1)}, u32[]{:S(2)}, u32[]{:S(2)}) collective-permute-start(bf16[4,96,768]{2,1,0:T(8,128)(2,1)} %dynamic-slice_bitcast_fusion.3), channel_id=1, source_target_pairs={{0,4},{4,0},{8,12},{12,8},{16,20},{20,16},{24,28},{28,24},{1,5},{5... | collective-permute-start | bytes 1769480 | tf_op jit(solution)/shard_map/ppermute | solution.py:430
  369.2 31.2 %collective-permute-start.43 = (bf16[512,768]{1,0:T(8,128)(2,1)}, bf16[512,768]{1,0:T(8,128)(2,1)}, u32[]{:S(2)}, u32[]{:S(2)}) collective-permute-start(bf16[512,768]{1,0:T(8,128)(2,1)} %get-tuple-element.97), channel_id=1, source_target_pairs={{1,0},{2,1},{3,2},{5,4},{6,5},{7,6},{9,8},{10,9},{11,10},{13,12},{... | collective-permute-start | bytes 2359304 | tf_op jit(solution)/shard_map/ppermute | solution.py:571
  386.1 20.0 %collective-permute-start.47 = (bf16[96,1536]{1,0:T(8,128)(2,1)S(1)}, bf16[96,1536]{1,0:T(8,128)(2,1)S(1)}, u32[]{:S(2)}, u32[]{:S(2)}) collective-permute-start(bf16[96,1536]{1,0:T(8,128)(2,1)S(1)} %get-tuple-element.223), channel_id=1, source_target_pairs={{0,8},{4,12},{8,16},{12,20},{16,24},{20,28},{24,0},{28,4},{1,9},{5... | collective-permute-start | bytes 884744 | tf_op jit(solution)/shard_map/ppermute | solution.py:430
  391.8 19.0 %collective-permute-start.48 = (bf16[96,1536]{1,0:T(8,128)(2,1)S(1)}, bf16[96,1536]{1,0:T(8,128)(2,1)S(1)}, u32[]{:S(2)}, u32[]{:S(2)}) collective-permute-start(bf16[96,1536]{1,0:T(8,128)(2,1)S(1)} %get-tuple-element.224), channel_id=1, source_target_pairs={{0,16},{4,20},{8,24},{12,28},{16,0},{20,4},{24,8},{28,12},{1,17},{... | collective-permute-start | bytes 884744 | tf_op jit(solution)/shard_map/ppermute | solution.py:430
  391.8 19.0 %collective-permute-start.49 = (bf16[96,1536]{1,0:T(8,128)(2,1)S(1)}, bf16[96,1536]{1,0:T(8,128)(2,1)S(1)}, u32[]{:S(2)}, u32[]{:S(2)}) collective-permute-start(bf16[96,1536]{1,0:T(8,128)(2,1)S(1)} %get-tuple-element.222), channel_id=1, source_target_pairs={{0,24},{4,28},{8,0},{12,4},{16,8},{20,12},{24,16},{28,20},{1,25},{... | collective-permute-start | bytes 884744 | tf_op jit(solution)/shard_map/ppermute | solution.py:430
  423.2 40.5 %collective-permute-start.52 = (bf16[2,768,1536]{2,1,0:T(8,128)(2,1)}, bf16[2,768,1536]{2,1,0:T(8,128)(2,1)}, u32[]{:S(2)}, u32[]{:S(2)}) collective-permute-start(bf16[2,768,1536]{2,1,0:T(8,128)(2,1)} %get-tuple-element.108), channel_id=1, source_target_pairs={{0,1},{1,0},{2,3},{3,2},{4,5},{5,4},{6,7},{7,6},{8,9},{9,8},{10,11... | collective-permute-start | bytes 14155784 | tf_op jit(solution)/shard_map/ppermute | solution.py:430
  423.3 16.1 %collective-permute-start.50 = (bf16[4,2,96,384]{3,2,0,1:T(8,128)(2,1)}, bf16[4,2,96,384]{3,2,0,1:T(8,128)(2,1)}, u32[]{:S(2)}, u32[]{:S(2)}) collective-permute-start(bf16[4,2,96,384]{3,2,0,1:T(8,128)(2,1)} %copy-done.42), channel_id=1, source_target_pairs={{0,2},{1,3},{2,0},{3,1},{4,6},{5,7},{6,4},{7,5},{8,10},{9,11},{10,... | collective-permute-start | bytes 1769480 | tf_op jit(solution)/shard_map/ppermute | solution.py:430
  424.1 17.2 %collective-permute-start.51 = (bf16[2,4,96,384]{3,2,1,0:T(8,128)(2,1)}, bf16[2,4,96,384]{3,2,1,0:T(8,128)(2,1)}, u32[]{:S(2)}, u32[]{:S(2)}) collective-permute-start(bf16[2,4,96,384]{3,2,1,0:T(8,128)(2,1)} %fusion.17.refs_6_), channel_id=1, source_target_pairs={{0,4},{4,0},{8,12},{12,8},{16,20},{20,16},{24,28},{28,24},{1,5},{5... | collective-permute-start | bytes 1769480 | tf_op jit(solution)/shard_map/ppermute | solution.py:430
  456.0 21.1 %collective-permute-start.53 = (bf16[4,96,384]{2,1,0:T(8,128)(2,1)}, bf16[4,96,384]{2,1,0:T(8,128)(2,1)}, u32[]{:S(2)}, u32[]{:S(2)}) collective-permute-start(bf16[4,96,384]{2,1,0:T(8,128)(2,1)} %dynamic-slice_bitcast_fusion.7), channel_id=1, source_target_pairs={{0,4},{4,0},{8,12},{12,8},{16,20},{20,16},{24,28},{28,24},{1,5},{5... | collective-permute-start | bytes 884744 | tf_op jit(solution)/shard_map/ppermute | solution.py:430
  458.9 18.3 %collective-permute-start.54 = (bf16[4,96,384]{2,1,0:T(8,128)(2,1)S(1)}, bf16[4,96,384]{2,1,0:T(8,128)(2,1)S(1)}, u32[]{:S(2)}, u32[]{:S(2)}) collective-permute-start(bf16[4,96,384]{2,1,0:T(8,128)(2,1)S(1)} %dynamic-slice_bitcast_fusion.6), channel_id=1, source_target_pairs={{0,2},{1,3},{2,0},{3,1},{4,6},{5,7},{6,4},{7,5},{8,10},{9,11},{10,... | collective-permute-start | bytes 884744 | tf_op jit(solution)/shard_map/ppermute | solution.py:430
  469.1 53.5 %collective-permute-start.55 = (bf16[4,2,96,768]{3,2,0,1:T(8,128)(2,1)S(1)}, bf16[4,2,96,768]{3,2,0,1:T(8,128)(2,1)}, u32[]{:S(2)}, u32[]{:S(2)}) collective-permute-start(bf16[4,2,96,768]{3,2,0,1:T(8,128)(2,1)S(1)} %fusion.6), channel_id=1, source_target_pairs={{0,2},{1,3},{2,0},{3,1},{4,6},{5,7},{6,4},{7,5},{8,10},{9,11},{10,... | collective-permute-start | bytes 3538952 | tf_op jit(solution)/shard_map/ppermute | solution.py:430
  471.7 53.3 %collective-permute-start.56 = (bf16[2,4,96,768]{3,2,1,0:T(8,128)(2,1)}, bf16[2,4,96,768]{3,2,1,0:T(8,128)(2,1)}, u32[]{:S(2)}, u32[]{:S(2)}) collective-permute-start(bf16[2,4,96,768]{3,2,1,0:T(8,128)(2,1)} %fusion.7.refs_5_), channel_id=1, source_target_pairs={{0,4},{4,0},{8,12},{12,8},{16,20},{20,16},{24,28},{28,24},{1,5},{5... | collective-permute-start | bytes 3538952 | tf_op jit(solution)/shard_map/ppermute | solution.py:430
  515.7 60.7 %collective-permute-start.61 = (bf16[2,768,768]{2,1,0:T(8,128)(2,1)}, bf16[2,768,768]{2,1,0:T(8,128)(2,1)}, u32[]{:S(2)}, u32[]{:S(2)}) collective-permute-start(bf16[2,768,768]{2,1,0:T(8,128)(2,1)} %get-tuple-element.121), channel_id=1, source_target_pairs={{0,1},{1,0},{2,3},{3,2},{4,5},{5,4},{6,7},{7,6},{8,9},{9,8},{10,11... | collective-permute-start | bytes 7077896 | tf_op jit(solution)/shard_map/ppermute | solution.py:430
  550.8 15.4 %collective-permute-start.62 = (bf16[4,96,768]{2,1,0:T(8,128)(2,1)}, bf16[4,96,768]{2,1,0:T(8,128)(2,1)S(1)}, u32[]{:S(2)}, u32[]{:S(2)}) collective-permute-start(bf16[4,96,768]{2,1,0:T(8,128)(2,1)} %dynamic-slice_bitcast_fusion.1), channel_id=1, source_target_pairs={{0,4},{4,0},{8,12},{12,8},{16,20},{20,16},{24,28},{28,24},{1,5},{5... | collective-permute-start | bytes 1769480 | tf_op jit(solution)/shard_map/ppermute | solution.py:430
  553.6 41.4 %collective-permute-start.60 = (bf16[512,768]{1,0:T(8,128)(2,1)}, bf16[512,768]{1,0:T(8,128)(2,1)}, u32[]{:S(2)}, u32[]{:S(2)}) collective-permute-start(bf16[512,768]{1,0:T(8,128)(2,1)} %get-tuple-element.118), channel_id=1, source_target_pairs={{1,0},{2,1},{3,2},{5,4},{6,5},{7,6},{9,8},{10,9},{11,10},{13,12},{... | collective-permute-start | bytes 2359304 | tf_op jit(solution)/shard_map/ppermute | solution.py:571
  572.5 18.9 %collective-permute-start.67 = (bf16[96,1536]{1,0:T(8,128)(2,1)S(1)}, bf16[96,1536]{1,0:T(8,128)(2,1)S(1)}, u32[]{:S(2)}, u32[]{:S(2)}) collective-permute-start(bf16[96,1536]{1,0:T(8,128)(2,1)S(1)} %get-tuple-element.213), channel_id=1, source_target_pairs={{0,16},{4,20},{8,24},{12,28},{16,0},{20,4},{24,8},{28,12},{1,17},{... | collective-permute-start | bytes 884744 | tf_op jit(solution)/shard_map/ppermute | solution.py:430
  572.5 18.9 %collective-permute-start.68 = (bf16[96,1536]{1,0:T(8,128)(2,1)S(1)}, bf16[96,1536]{1,0:T(8,128)(2,1)S(1)}, u32[]{:S(2)}, u32[]{:S(2)}) collective-permute-start(bf16[96,1536]{1,0:T(8,128)(2,1)S(1)} %get-tuple-element.211), channel_id=1, source_target_pairs={{0,24},{4,28},{8,0},{12,4},{16,8},{20,12},{24,16},{28,20},{1,25},{... | collective-permute-start | bytes 884744 | tf_op jit(solution)/shard_map/ppermute | solution.py:430
  579.4 22.9 %collective-permute-start.64 = (bf16[4,2,96,384]{3,2,0,1:T(8,128)(2,1)S(1)}, bf16[4,2,96,384]{3,2,0,1:T(8,128)(2,1)S(1)}, u32[]{:S(2)}, u32[]{:S(2)}) collective-permute-start(bf16[4,2,96,384]{3,2,0,1:T(8,128)(2,1)S(1)} %fusion.18), channel_id=1, source_target_pairs={{0,2},{1,3},{2,0},{3,1},{4,6},{5,7},{6,4},{7,5},{8,10},{9,11},{10,... | collective-permute-start | bytes 1769480 | tf_op jit(solution)/shard_map/ppermute | solution.py:430
  580.7 22.4 %collective-permute-start.69 = (bf16[2,4,96,384]{3,2,1,0:T(8,128)(2,1)S(1)}, bf16[2,4,96,384]{3,2,1,0:T(8,128)(2,1)S(1)}, u32[]{:S(2)}, u32[]{:S(2)}) collective-permute-start(bf16[2,4,96,384]{3,2,1,0:T(8,128)(2,1)S(1)} %fusion.19.refs_6_), channel_id=1, source_target_pairs={{0,4},{4,0},{8,12},{12,8},{16,20},{20,16},{24,28},{28,24},{1,5},{5... | collective-permute-start | bytes 1769480 | tf_op jit(solution)/shard_map/ppermute | solution.py:430
  608.1 23.8 %collective-permute-start.65 = (bf16[4,96,384]{2,1,0:T(8,128)(2,1)}, bf16[4,96,384]{2,1,0:T(8,128)(2,1)S(1)}, u32[]{:S(2)}, u32[]{:S(2)}) collective-permute-start(bf16[4,96,384]{2,1,0:T(8,128)(2,1)} %dynamic-slice_bitcast_fusion.5), channel_id=1, source_target_pairs={{0,4},{4,0},{8,12},{12,8},{16,20},{20,16},{24,28},{28,24},{1,5},{5... | collective-permute-start | bytes 884744 | tf_op jit(solution)/shard_map/ppermute | solution.py:430
  613.0 20.6 %collective-permute-start.70 = (bf16[4,96,384]{2,1,0:T(8,128)(2,1)S(1)}, bf16[4,96,384]{2,1,0:T(8,128)(2,1)S(1)}, u32[]{:S(2)}, u32[]{:S(2)}) collective-permute-start(bf16[4,96,384]{2,1,0:T(8,128)(2,1)S(1)} %dynamic-slice_bitcast_fusion.4), channel_id=1, source_target_pairs={{0,2},{1,3},{2,0},{3,1},{4,6},{5,7},{6,4},{7,5},{8,10},{9,11},{10,... | collective-permute-start | bytes 884744 | tf_op jit(solution)/shard_map/ppermute | solution.py:430
  622.3 17.5 %collective-permute-start.79 = (f32[32,768]{1,0:T(8,128)S(1)}, f32[32,768]{1,0:T(8,128)S(1)}, u32[]{:S(2)}, u32[]{:S(2)}) collective-permute-start(f32[32,768]{1,0:T(8,128)S(1)} %add.564), channel_id=1, source_target_pairs={{0,24},{4,28},{8,0},{12,4},{16,8},{20,12},{24,16},{28,20},{1,25},{... | collective-permute-start | bytes 294920 | tf_op jit(solution)/shard_map/ppermute | solution.py:430
  (155 other events, 756.8 us)
